TPU v7x, 32 devices: a whole 2x2x4 slice. The times are simulated.
32 devices in a mesh: seq: 8 (over y, x, core), head: 4 (over z).
Axes of the slice: x: 2, y: 2, z: 4, core: 2. Of those that a mesh axis runs over, the one named last changes fastest.
Arguments:
- tokens: bfloat16 [1, 4096, 1536], P(None, 'seq', 'head'), may hold values from -6 to 6
- decay_codes: int32 [1, 4096, 48], P(None, 'seq', 'head'), may hold values from 0 to 524288, as said below
- norm_gain: bfloat16 [1536], P('head'), may hold values from 0.25 to 1.75
- gate_weight: bfloat16 [1536, 3072], P(None, 'head'), may hold values from -0.15625 to 0.15625
- value_weight: bfloat16 [1536, 3072], P(None, 'head'), may hold values from -0.15625 to 0.15625
- state_weight: bfloat16 [1536, 256], replicated, may hold values from -0.15625 to 0.15625
- value_kernel: bfloat16 [4, 3072], P(None, 'head'), may hold values from -3 to 3
- value_bias: bfloat16 [3072], P('head'), may hold values from -3 to 3
- state_kernel: bfloat16 [4, 256], replicated, may hold values from -3 to 3
- state_bias: bfloat16 [256], replicated, may hold values from -3 to 3
- skip_scale: float32 [48], P('head'), may hold values from 0.5 to 1.5
- gated_gain: bfloat16 [3072], P('head'), may hold values from 0.25 to 1.75
- output_weight: bfloat16 [3072, 1536], P('head'), may hold values from -0.109375 to 0.109375
- cotangent: bfloat16 [1, 4096, 1536], P(None, 'seq', 'head'), may hold values from -6 to 6
Outputs:
- block_out: bfloat16 [1, 4096, 1536], P(None, 'seq', 'head')
- tokens_gradient: bfloat16 [1, 4096, 1536], P(None, 'seq', 'head')
- norm_gain_gradient: float32 [1536], P('head')
- gate_weight_gradient: float32 [1536, 3072], P(None, 'head')
- value_weight_gradient: float32 [1536, 3072], P(None, 'head')
- state_weight_gradient: float32 [1536, 256], replicated
- value_kernel_gradient: float32 [4, 3072], P(None, 'head')
- value_bias_gradient: float32 [3072], P('head')
- state_kernel_gradient: float32 [4, 256], replicated
- state_bias_gradient: float32 [256], replicated
- skip_scale_gradient: float32 [48], P('head')
- gated_gain_gradient: float32 [3072], P('head')
- output_weight_gradient: float32 [3072, 1536], P('head')
Inputs may be any that keep to these rules, and one draw needn't show every extreme that they name: `decay_codes`: decay factors are exp(-code / 1048576).
All inputs are finite; a program needn't handle non-finite values.
Results may differ from a plain program's by a relative error of at most 0.012.
The roundings to bfloat16 on the way count: a program that leaves them out, or rounds other values in their place, can miss the bound.
Values may be sent and summed in bfloat16 or wider, within the bound.
No kernel may reach another device: no remote copies, remote signals or barrier semaphores. Data moves between devices by JAX's collectives and lax.ppermute only.
A program may use at most 128 MiB of HBM per device.

v0:
```python
import functools

import jax
import jax.numpy as jnp
from jax import lax
from jax.experimental import pallas as pl
from jax.experimental.pallas import tpu as pltpu
from jax.sharding import Mesh
from jax.sharding import PartitionSpec as P

HEAD_DIM = 64
NSTATE = 128
KERNEL = 4
CHUNK = 128
BLOCK = 384
VMEM_LIMIT = 20 * 1024 * 1024
MARGIN = 32
HALO = 16


DECAY_STEP = 1.0 / 1048576.0
EPSILON = 1e-05
BF16 = jnp.bfloat16
F32 = jnp.float32


def tie_kernel(*refs):
    del refs


def tie(value, *others):
    return pl.pallas_call(
        tie_kernel,
        out_shape=jax.ShapeDtypeStruct(value.shape, value.dtype),
        in_specs=[pl.BlockSpec(memory_space=pl.ANY)] * (1 + len(others)),
        out_specs=pl.BlockSpec(memory_space=pl.ANY),
        input_output_aliases={0: 0},
        name="tie",
    )(value, *others)


def from_behind(value, by):
    axis = ("chip", "core")
    size = lax.axis_size("chip") * 2
    pairs = [(i, i + by) for i in range(size) if 0 <= i + by < size]
    return lax.ppermute(value, axis, pairs)


def beside(value):
    return lax.ppermute(value, "core", [(0, 1), (1, 0)])


def turn(value, axis, by):
    size = lax.axis_size(axis)
    return lax.ppermute(value, axis, [(i, (i + by) % size) for i in range(size)])


def turn_all(value, axis):
    return [value] + [turn(value, axis, by) for by in range(1, lax.axis_size(axis))]


def line_parts(value, axis):
    if lax.axis_size(axis) != 4:
        parts = turn_all(value, axis)
        return parts, value
    two = turn(value, axis, 2)
    one = lax.ppermute(value, axis, [(0, 1), (1, 2), (2, 3)])
    three = lax.ppermute(value, axis, [(1, 0), (2, 1), (3, 2)])
    passed = lax.ppermute(two, axis, [(2, 3), (1, 0)])
    return [value, one, two, three], passed


def deal(parts, axis):
    return lax.all_to_all(parts, axis, 0, 0)


def cross(value, bits):
    return lax.ppermute(value, "chip", [(i, i ^ bits) for i in range(lax.axis_size("chip"))])


def cross_all(value):
    return [value] + [cross(value, bits) for bits in range(1, lax.axis_size("chip"))]


def heads_sum(piece):
    total, low = piece, piece.astype(BF16)
    bits, size = 1, lax.axis_size("head")
    while bits < size:
        arrived = lax.ppermute(low, "head", [(i, i ^ bits) for i in range(size)])
        total, low = run(
            heads_kernel, "heads", piece.size,
            [(WHOLE, piece), (WHOLE, total), (WHOLE, arrived)],
            [(WHOLE, piece.shape, F32), (WHOLE, piece.shape, BF16)],
        )
        bits *= 2
    return low


def entering(core, chip, total, backward, meanwhile, later=lambda pair: ()):
    name = "after" if backward else "before"
    chips = lax.axis_size("chip")
    channels = total.shape[1]
    half = NSTATE // 2
    partner = beside(total)
    pair = run(
        functools.partial(pair_kernel, backward), name + "_pair", total.size,
        [core, (WHOLE, total), (WHOLE, partner)] + [(LOOSE, value) for value in meanwhile],
        [(WHOLE, (half + 8, channels), F32)],
    )[0]
    prefix = run(
        functools.partial(prefix_kernel, backward, chips), name + "_prefix", chips * pair.size,
        [chip] + [(WHOLE, value) for value in cross_all(pair)]
        + [(LOOSE, value) for value in later(pair)],
        [(WHOLE, (half, channels), F32)],
    )[0]
    return run(
        functools.partial(enter_kernel, backward), name + "_enter", total.size,
        [core, (WHOLE, partner), (WHOLE, prefix), (WHOLE, beside(prefix))],
        [(WHOLE, (NSTATE, channels), F32)],
    )[0]


def sum_pieces(chip, kept, given, name, cut, paired, before_half=()):
    chips, rows, channels = kept.shape
    arrived = beside(given)
    size = chips * rows * channels
    halves = run(
        functools.partial(half_kernel, paired, chips), name + "_half", size,
        [chip, (WHOLE, kept), (WHOLE, arrived)] + [(LOOSE, mark) for mark in before_half],
        [(WHOLE, (rows, channels), F32)] + [(WHOLE, (rows, channels), BF16)] * (chips - 1),
    )
    parts = [halves[0]] + [cross(halves[bits], bits) for bits in range(1, chips)]
    return run(
        functools.partial(piece_kernel, chips, paired, cut), name + "_piece", size,
        [(WHOLE, part) for part in parts],
        [(WHOLE, (cut, channels), BF16), (WHOLE, (rows - cut, channels), F32 if paired else BF16)],
    ), halves[0]


def collect(piece, order, mark=None):
    chips = lax.axis_size("chip")
    if chips != 4 or order is None:
        found = [(value[None], (bits,)) for bits, value in enumerate(cross_all(piece))]
    else:
        near, far = order
        both = jnp.stack([piece, cross(piece, near)])
        if mark is not None:
            both = tie(both, mark)
        found = [(both, (0, near)), (cross(both, far), (far, far ^ near))]
    return [(value, beside(value), bits) for value, bits in found]


def dot(left, right):
    return jnp.dot(left, right, preferred_element_type=F32)


def dot_nt(left, right):
    return lax.dot_general(left, right, (((1,), (1,)), ((), ())), preferred_element_type=F32)


def dot_tn(left, right):
    return lax.dot_general(left, right, (((0,), (0,)), ((), ())), preferred_element_type=F32)


def split(values):
    high = values.astype(BF16)
    return high, (values - high.astype(F32)).astype(BF16)


def lower_mask():
    row = lax.broadcasted_iota(jnp.int32, (CHUNK, CHUNK), 0)
    column = lax.broadcasted_iota(jnp.int32, (CHUNK, CHUNK), 1)
    return row >= column


def spread_heads(heads, channels):
    row = lax.broadcasted_iota(jnp.int32, (heads, channels), 0) * HEAD_DIM
    place = lax.broadcasted_iota(jnp.int32, (heads, channels), 1)
    return jnp.where((place >= row) & (place < row + HEAD_DIM), 1.0, 0.0).astype(BF16)


def expand(values, channels):
    high, low = split(values)
    spread = spread_heads(values.shape[1], channels)
    return dot(high, spread) + dot(low, spread)


def decay_kernel(codes_ref, weight_ref, e_ref, f_ref, k_ref):
    heads, channels = codes_ref.shape[1], k_ref.shape[1]
    lower = jnp.where(lower_mask(), 1.0, 0.0).astype(F32)
    count = codes_ref.shape[0] // CHUNK
    line = lax.broadcasted_iota(jnp.int32, (8, heads), 0)
    marks = jnp.zeros((8, heads), F32)
    total = jnp.zeros((1, heads), F32)
    for chunk in range(count):
        rows = pl.ds(chunk * CHUNK, CHUNK)
        logs = codes_ref[rows, :].astype(F32) * (-DECAY_STEP)
        cumulative = jnp.dot(
            lower, logs, precision=lax.Precision.HIGHEST, preferred_element_type=F32
        )
        last = cumulative[CHUNK - 1 :]
        middle = 0.5 * last
        e_ref[rows, :] = jnp.exp(cumulative - middle)
        f_ref[rows, :] = weight_ref[rows, :] * jnp.exp(middle - cumulative)
        marks = jnp.where(line == chunk, jnp.exp(middle), marks)
        total = total + last
    marks = jnp.where(line == 7, total, marks)
    high, low = split(marks)
    lowest = (marks - high.astype(F32) - low.astype(F32)).astype(BF16)
    spread = spread_heads(heads, channels)
    factors = dot(high, spread) + dot(low, spread) + dot(lowest, spread)
    k_ref[...] = factors


def pair_kernel(backward, core_ref, own_ref, other_ref, *refs):
    out_ref = refs[-1]
    half = NSTATE // 2
    logs, other_logs = own_ref[NSTATE:, :], other_ref[NSTATE:, :]
    for core in range(2):

        @pl.when(core_ref[0] == core)
        def _():
            rows = slice(core * half, (core + 1) * half)
            if core == (0 if backward else 1):
                out_ref[:half, :] = jnp.exp(logs[0:1]) * other_ref[rows, :] + own_ref[rows, :]
            else:
                out_ref[:half, :] = jnp.exp(other_logs[0:1]) * own_ref[rows, :] + other_ref[rows, :]

    out_ref[half:, :] = logs + other_logs


def prefix_kernel(backward, chips, chip_ref, *refs):
    parts, out_ref = refs[:chips], refs[-1]
    half = out_ref.shape[0]
    mine = chip_ref[0]
    total = jnp.zeros(out_ref.shape, F32)
    for bits in range(1, chips):
        source = lax.bitwise_xor(mine, bits)
        span = jnp.zeros((1, out_ref.shape[1]), F32)
        for other in range(1, chips):
            middle = lax.bitwise_xor(mine, other)
            if backward:
                between = (middle < source) & (middle > mine)
            else:
                between = (middle > source) & (middle < mine)
            span = span + jnp.where(between, parts[other][half : half + 1, :], 0.0)
        passes = source > mine if backward else source < mine
        total = total + jnp.where(passes, jnp.exp(span), 0.0) * parts[bits][:half, :]
    out_ref[...] = total


def enter_kernel(backward, core_ref, partner_ref, prefix_ref, other_ref, out_ref):
    half = prefix_ref.shape[0]
    decay = jnp.exp(partner_ref[NSTATE : NSTATE + 1, :])
    for core in range(2):

        @pl.when(core_ref[0] == core)
        def _():
            for place, ref in ((core, prefix_ref), (1 - core, other_ref)):
                rows = slice(place * half, (place + 1) * half)
                if core == (0 if backward else 1):
                    out_ref[rows, :] = decay * ref[...] + partner_ref[rows, :]
                else:
                    out_ref[rows, :] = ref[...]


def taps(window, kernel, bias, begin):
    summed = bias
    for offset in range(KERNEL):
        summed = summed + kernel[offset : offset + 1] * window[begin + offset : begin + offset + CHUNK]
    return summed


def silu_parts(values):
    sigmoid = jax.nn.sigmoid(values)
    return values * sigmoid, sigmoid * (1.0 + values * (1.0 - sigmoid))


def first_step(action):
    pl.when(pl.program_id(0) == 0)(action)


def clear(*refs):
    def action():
        for ref in refs:
            ref[...] = jnp.zeros_like(ref)

    first_step(action)


def place_parts(mine, parts, target, width, value):
    size = len(parts)
    if width % 128 == 0:
        for i in range(size):
            owner = lax.rem(mine + size - i, size)
            target[:, pl.ds(pl.multiple_of(owner * width, 128), width)] = value(i)
        return

    def write(me):
        for i in range(size):
            owner = (me + size - i) % size
            target[:, owner * width : (owner + 1) * width] = value(i)

    for me in range(size):
        pl.when(mine == me)(functools.partial(write, me))


def copies_kernel(one_ref, three_ref, own_ref, out_ref):
    for i in range(out_ref.shape[0]):
        out_ref[i] = own_ref[...]


def norm_kernel(size, head_ref, passed_ref, *refs):
    parts, gains = refs[:size], refs[size : 2 * size]
    passed_gain_ref, normed_ref, scale_ref, gain_ref = refs[2 * size :]
    width = parts[0].shape[1]
    mine = head_ref[0]

    def pick(i, refs, passed):
        if size == 4 and i == 1:
            return jnp.where(mine == 0, passed[...], refs[i][...])
        if size == 4 and i == 3:
            return jnp.where(mine == 3, passed[...], refs[i][...])
        return refs[i][...]

    part = lambda i: pick(i, parts, passed_ref).astype(F32)
    gain = lambda i: pick(i, gains, passed_gain_ref)[0:1].astype(F32)
    squares = sum(jnp.sum(part(i) ** 2, axis=1, keepdims=True) for i in range(size))
    scale = lax.rsqrt(squares / (size * width) + EPSILON)
    scale_ref[...] = jnp.broadcast_to(scale, scale_ref.shape)
    place_parts(
        mine, parts, normed_ref, width,
        lambda i: (part(i) * scale_ref[:, 0:1] * gain(i)).astype(BF16),
    )
    place_parts(mine, parts, gain_ref, width, lambda i: jnp.broadcast_to(gain(i), (8, width)))


def mixed_grad_kernel(parts_ref, weight_ref, out_ref, full_ref):
    size, _, width = parts_ref.shape
    for i in range(size):
        full_ref[:, i * width : (i + 1) * width] = parts_ref[i]
    out_ref[...] = dot_nt(full_ref[...], weight_ref[...])


def out_kernel(loose_ref, mixed_ref, weight_ref, out_ref):
    width = out_ref.shape[2]
    for owner in range(out_ref.shape[0]):
        value = dot(mixed_ref[...], weight_ref[:, owner * width : (owner + 1) * width])
        out_ref[owner] = value.astype(BF16)


def conv_kernel(
    value_ref, state_ref, value_kernel_ref, value_bias_ref, state_kernel_ref, state_bias_ref,
    f_ref, k_ref, conv_ref, weighted_ref, value_slope_ref, maps_ref, state_slope_ref, total_ref,
):
    chunk = pl.program_id(0)
    clear(total_ref)
    around = pl.ds(pl.multiple_of(chunk * CHUNK, CHUNK), CHUNK + HALO)
    pre = taps(
        state_ref[around, :].astype(F32), state_kernel_ref[...].astype(F32),
        state_bias_ref[...].astype(F32), HALO - KERNEL + 1,
    )
    conv, slope = silu_parts(pre)
    maps = conv.astype(BF16)
    maps_ref[...] = maps
    state_slope_ref[...] = slope
    pre = taps(
        value_ref[around, :].astype(F32), value_kernel_ref[...].astype(F32),
        value_bias_ref[...].astype(F32), HALO - KERNEL + 1,
    )
    conv, slope = silu_parts(pre)
    conv = conv.astype(BF16)
    conv_ref[...] = conv
    value_slope_ref[...] = slope
    weighted = (conv.astype(F32) * expand(f_ref[...], conv.shape[1])).astype(BF16)
    weighted_ref[...] = weighted
    factor = k_ref[pl.ds(chunk, 1), :]
    total_ref[:NSTATE, :] = factor * (
        factor * total_ref[:NSTATE, :] + dot_tn(maps[:, :NSTATE], weighted)
    )
    total_ref[NSTATE:, :] = jnp.broadcast_to(k_ref[7:8, :], (8, k_ref.shape[1]))


def mixer_kernel(
    state_in_ref, maps_ref, weighted_ref, conv_ref, e_ref, k_ref, skip_ref, gate_ref, grad_ref, gain_ref,
    mixer_ref, stats_ref, high_ref, low_ref, state_ref,
):
    chunk = pl.program_id(0)

    def start():
        state_ref[...] = state_in_ref[...]

    first_step(start)
    lane = lax.broadcasted_iota(jnp.int32, (CHUNK, CHUNK), 1)
    factor = k_ref[pl.ds(chunk, 1), :]
    input_map, output_map = maps_ref[:, :NSTATE], maps_ref[:, NSTATE:]
    weighted = weighted_ref[...]
    scaled = factor * state_ref[...]
    high, low = split(scaled)
    high_ref[0], low_ref[0] = high, low
    scores = jnp.where(lower_mask(), dot_nt(output_map, input_map), 0.0).astype(BF16)
    mixed = dot(
        jnp.concatenate([scores, output_map], axis=1), jnp.concatenate([weighted, high], axis=0)
    )
    mixed = mixed + dot(output_map, low)
    mixer = expand(e_ref[...], weighted.shape[1]) * mixed + skip_ref[...] * conv_ref[...].astype(F32)
    mixer_ref[...] = mixer
    gate = gate_ref[...]
    gated = mixer * (gate * jax.nn.sigmoid(gate))
    squares = jnp.sum(gated * gated, axis=1, keepdims=True)
    products = jnp.sum(gated * (grad_ref[...] * gain_ref[...].astype(F32)), axis=1, keepdims=True)
    sums = jnp.where(lane == 0, squares, jnp.where(lane == 1, products, 0.0))
    stats_ref[...] = sums.T[:8]
    state_ref[...] = factor * (scaled + dot_tn(input_map, weighted))


def column(row_block):
    rest = jnp.zeros((CHUNK - row_block.shape[0], CHUNK), F32)
    return jnp.concatenate([row_block, rest], axis=0).T


def row_of(sums):
    lane = lax.broadcasted_iota(jnp.int32, (CHUNK, CHUNK), 1)
    return jnp.where(lane == 0, sums, 0.0).T[:8]


def gate_kernel(
    inner, chunks, size, *refs
):
    stats_refs = refs[:size]
    (
        mixer_ref, gate_ref, grad_ref, gain_ref, conv_ref, e_ref, k_ref, maps_ref,
        mixed_ref, gate_grad_ref, mixer_grad_ref, small_ref, total_ref, cross_ref,
    ) = refs[size:]
    chunk = chunks - 1 - pl.program_id(0)
    clear(small_ref, total_ref)
    gain = gain_ref[...].astype(F32)
    stats = column(sum(ref[...] for ref in stats_refs))
    scale = lax.rsqrt(stats[:, 0:1] / inner + EPSILON)
    cross_term = stats[:, 1:2] * (scale * scale * scale) / inner
    gate = gate_ref[...]
    silu, slope = silu_parts(gate)
    mixer = mixer_ref[...]
    gated = mixer * silu
    normed = gated * scale
    mixed_ref[...] = (normed * gain).astype(BF16)
    grad = grad_ref[...]
    gated_grad = scale * (grad * gain) - gated * cross_term
    gate_grad = (gated_grad * mixer * slope).astype(BF16)
    gate_grad_ref[...] = gate_grad
    cross_ref[...] = row_of(jnp.sum(gate_grad.astype(F32) * gate, axis=1, keepdims=True))
    mixer_grad = gated_grad * silu
    mixer_grad_ref[...] = mixer_grad
    small_ref[0:1, :] += jnp.sum(grad * normed, axis=0, keepdims=True)
    small_ref[1:2, :] += jnp.sum(mixer_grad * conv_ref[...].astype(F32), axis=0, keepdims=True)
    high, low = split(expand(e_ref[...], grad.shape[1]) * mixer_grad)
    output_map = maps_ref[:, NSTATE:]
    factor = k_ref[pl.ds(chunk, 1), :]
    total_ref[:NSTATE, :] = factor * (
        factor * total_ref[:NSTATE, :] + (dot_tn(output_map, high) + dot_tn(output_map, low))
    )
    total_ref[NSTATE:, :] = jnp.broadcast_to(k_ref[7:8, :], (8, k_ref.shape[1]))


def back_kernel(
    chunks, early_ref, state_in_ref, mixer_grad_ref, e_ref, f_ref, k_ref, weighted_ref, high_ref, low_ref,
    maps_ref, value_slope_ref, state_slope_ref, skip_ref,
    value_ref, map_ref, state_ref,
):
    chunk = chunks - 1 - pl.program_id(0)

    def start():
        state_ref[...] = state_in_ref[...]

    first_step(start)
    lower = lower_mask()
    row = lax.broadcasted_iota(jnp.int32, (CHUNK, CHUNK), 0)
    upper = row <= lax.broadcasted_iota(jnp.int32, (CHUNK, CHUNK), 1)
    factor = k_ref[pl.ds(chunk, 1), :]
    input_map, output_map = maps_ref[:, :NSTATE], maps_ref[:, NSTATE:]
    weighted = weighted_ref[...]
    mixer_grad = mixer_grad_ref[...]
    high, low = split(expand(e_ref[...], weighted.shape[1]) * mixer_grad)
    scaled = factor * state_ref[...]
    state_high, state_low = split(scaled)
    both = jnp.concatenate([weighted, high_ref[0]], axis=0)
    sums = dot_nt(high, both) + dot_nt(low, both)
    score_grad = jnp.where(lower, sums[:, :CHUNK], 0.0).astype(BF16)
    output_grad = sums[:, CHUNK:] + dot_nt(high, low_ref[0]) + dot(score_grad, input_map)
    sums = dot_nt(weighted, jnp.concatenate([state_high, state_low], axis=0))
    input_grad = sums[:, :NSTATE] + sums[:, NSTATE:] + dot_tn(score_grad, output_map)
    scores = jnp.where(upper, dot_nt(input_map, output_map), 0.0).astype(BF16)
    grads = dot(
        jnp.concatenate([scores, input_map], axis=1), jnp.concatenate([high, state_high], axis=0)
    )
    decayed = expand(f_ref[...], weighted.shape[1]) * grads
    value_ref[...] = (decayed + skip_ref[...] * mixer_grad) * value_slope_ref[...]
    slope = state_slope_ref[...]
    map_ref[:, :NSTATE] = input_grad * slope[:, :NSTATE]
    map_ref[:, NSTATE:] = output_grad * slope[:, NSTATE:]
    state_ref[...] = factor * (scaled + (dot_tn(output_map, high) + dot_tn(output_map, low)))


def conv_back_kernel(
    chunks, value_ref, map_ref, after_ref, value_raw_ref, state_raw_ref, value_kernel_ref,
    state_kernel_ref, cross_in_ref,
    value_grad_ref, state_grad_ref, value_small_ref, state_small_ref, cross_ref, value_next_ref,
    state_next_ref,
):
    chunk = chunks - 1 - pl.program_id(0)
    channels = value_ref.shape[1]
    clear(value_small_ref, state_small_ref)

    def start():
        value_next_ref[...] = after_ref[:, :channels]
        state_next_ref[...] = after_ref[:, channels:]

    first_step(start)

    def back(slope_ref, next_ref, raw_ref, kernel_ref, grad_ref, small_ref):
        kernel = kernel_ref[...].astype(F32)
        slope = slope_ref[...]
        window = jnp.concatenate([slope, next_ref[...]], axis=0)
        around = pl.ds(pl.multiple_of(chunk * CHUNK, CHUNK), CHUNK + HALO)
        raw = raw_ref[around, :].astype(F32)
        grad = jnp.zeros_like(slope)
        for offset in range(KERNEL):
            back_by = KERNEL - 1 - offset
            grad = grad + kernel[offset : offset + 1] * window[back_by : back_by + CHUNK]
            begin = HALO - KERNEL + 1 + offset
            small_ref[offset : offset + 1, :] += jnp.sum(
                slope * raw[begin : begin + CHUNK], axis=0, keepdims=True
            )
        small_ref[KERNEL : KERNEL + 1, :] += jnp.sum(slope, axis=0, keepdims=True)
        grad = grad.astype(BF16)
        grad_ref[...] = grad
        next_ref[...] = slope[:8]
        return jnp.sum(grad.astype(F32) * raw[HALO:], axis=1, keepdims=True)

    crossed = back(map_ref, state_next_ref, state_raw_ref, state_kernel_ref, state_grad_ref, state_small_ref)
    crossed = crossed + back(
        value_ref, value_next_ref, value_raw_ref, value_kernel_ref, value_grad_ref, value_small_ref
    )
    cross_ref[...] = cross_in_ref[...] + row_of(crossed)


def normed_kernel(
    chunks, late_ref, gate_grad_ref, value_grad_ref, state_grad_ref, gate_weight_ref, value_weight_ref,
    state_weight_ref, cross_ref, out_ref
):
    value = (
        dot_nt(gate_grad_ref[...], gate_weight_ref[...])
        + dot_nt(value_grad_ref[...], value_weight_ref[...])
        + dot_nt(state_grad_ref[...], state_weight_ref[...])
    )
    count = value.shape[0]
    out_ref[0, :count, :] = value.astype(BF16)
    line = lax.broadcasted_iota(jnp.int32, (HALO, CHUNK), 0)
    packed = jnp.zeros((HALO, CHUNK), F32)
    for chunk in range(chunks):
        row = cross_ref[0:1, chunk * CHUNK : (chunk + 1) * CHUNK]
        high = row.astype(BF16).astype(F32)
        packed = jnp.where(line == chunk, high, packed)
        packed = jnp.where(line == chunks + chunk, row - high, packed)
    out_ref[0, count:, :] = jnp.zeros((HALO, value.shape[1]), BF16)
    out_ref[0, count:, :CHUNK] = packed.astype(BF16)


def last_kernel(full_width, parts_ref, tokens_ref, scale_ref, gain_ref, cotangent_ref, out_ref):
    count = tokens_ref.shape[0]
    chunks = count // CHUNK
    size = parts_ref.shape[0]
    crossed = sum(parts_ref[i, count:, :CHUNK].astype(F32) for i in range(size))
    crossed = crossed[:chunks] + crossed[chunks : 2 * chunks]
    for chunk in range(chunks):
        rows = slice(chunk * CHUNK, (chunk + 1) * CHUNK)
        normed_grad = sum(parts_ref[i, rows, :].astype(F32) for i in range(size))
        scale = scale_ref[HALO + chunk * CHUNK : HALO + (chunk + 1) * CHUNK, 0:1]
        total = column(jnp.broadcast_to(crossed[chunk : chunk + 1], (8, CHUNK)))[:, 0:1]
        out_ref[rows, :] = (
            scale * gain_ref[...].astype(F32) * normed_grad
            - tokens_ref[rows, :].astype(F32) * (scale * scale * total / full_width)
            + cotangent_ref[rows, :].astype(F32)
        ).astype(BF16)


def store_piece(core_ref, kept_ref, given_ref, place, begin, piece):
    chips = kept_ref.shape[0]
    core, chip = place // chips, lax.rem(place, chips)
    rows = slice(begin, begin + piece.shape[0])
    piece = piece.astype(BF16)

    @pl.when(core_ref[0] == core)
    def _():
        kept_ref[chip, rows, :] = piece

    @pl.when(core_ref[0] != core)
    def _():
        given_ref[chip, rows, :] = piece


def gain_row(weight, block):
    sums = jnp.sum(weight.astype(F32) * block, axis=1, keepdims=True)
    lane = lax.broadcasted_iota(jnp.int32, (CHUNK, CHUNK), 1)
    rows = [
        jnp.where(lane == 0, sums[i : i + CHUNK], 0.0).T[0:1] for i in range(0, BLOCK, CHUNK)
    ]
    return jnp.concatenate(rows, axis=1)


def early_kernel(
    loose_ref, core_ref, normed_ref, gate_ref, mixed_ref, grad_ref, weight_ref,
    kept_ref, given_ref, gain_ref, held_ref
):
    chips, rows, channels = kept_ref.shape
    at = pl.program_id(0)
    count, width = grad_ref.shape
    pieces = 2 * chips
    step = width // pieces
    out_rows = channels // pieces
    out_blocks = channels // BLOCK
    every = width // BLOCK // out_blocks

    @pl.when(lax.rem(at, every) == 0)
    def _():
        held_ref[...] = dot_tn(mixed_ref[...], grad_ref[...])

    block = dot_tn(normed_ref[HALO : HALO + count, :], gate_ref[...])
    gain_ref[...] = gain_row(weight_ref[...], block)
    for i in range(BLOCK // step):
        place = at * (BLOCK // step) + i
        begin = lax.rem(at, every) * (BLOCK // step * out_rows) + i * out_rows
        own = held_ref[pl.ds(pl.multiple_of(begin, 8), out_rows), :]
        parts = [block[i * step : (i + 1) * step]]
        parts += [own[:, j : j + channels] for j in range(0, width, channels)]
        store_piece(core_ref, kept_ref, given_ref, place, 0, jnp.concatenate(parts, axis=0))


def late_kernel(
    early_ref, core_ref, normed_ref, value_ref, state_ref, value_small_ref, gate_small_ref, gain_ref,
    state_small_ref, value_weight_ref, state_weight_ref, gain_full_ref,
    kept_ref, given_ref, own_ref, shared_ref, gains_ref,
):
    chips, rows, channels = kept_ref.shape
    at = pl.program_id(0)
    count, maps_width = state_ref.shape
    width = gains_ref.shape[1]
    pieces = 2 * chips
    step = width // pieces
    lanes = channels // 128
    part = 2 * step // lanes
    columns = normed_ref[HALO : HALO + count, :]
    value = dot_tn(columns, value_ref[...])
    state = dot_tn(columns, state_ref[...])
    gain = (
        gain_ref[...] + gain_row(value_weight_ref[...], value) + gain_row(state_weight_ref[...], state)
    ) / gain_full_ref[0:1, :]
    gains_ref[0:1, pl.ds(pl.multiple_of(at * BLOCK, 128), BLOCK)] = gain
    for i in range(BLOCK // step):
        piece = slice(i * step, (i + 1) * step)
        stacked = jnp.concatenate([state[piece, :128], state[piece, 128:]], axis=0)
        stacked = jnp.concatenate(
            [stacked[j * part : (j + 1) * part] for j in range(lanes)], axis=1
        )
        store_piece(
            core_ref, kept_ref, given_ref, at * (BLOCK // step) + i, 0,
            jnp.concatenate([value[piece], stacked], axis=0),
        )

    @pl.when(at == width // BLOCK - 1)
    def _():
        own_ref[...] = jnp.zeros_like(own_ref)
        own_ref[: KERNEL + 1, :] = value_small_ref[: KERNEL + 1, :]
        own_ref[KERNEL + 1 : KERNEL + 3, :] = gate_small_ref[:2, :]
        shared_ref[...] = jnp.zeros_like(shared_ref)
        begin = width // channels
        for i in range(begin):
            shared_ref[i : i + 1, :] = gains_ref[0:1, i * channels : (i + 1) * channels]
        for i in range(0, (KERNEL + 1) * maps_width, 128):
            tap, column_from = divmod(i, maps_width)
            row, column_to = divmod(i, channels)
            shared_ref[begin + row : begin + row + 1, column_to : column_to + 128] = state_small_ref[
                tap : tap + 1, column_from : column_from + 128
            ]
        line = lax.broadcasted_iota(jnp.int32, (HALO, channels), 0)
        for place in range(pieces):
            own, shared = own_ref[place : place + 1, :], shared_ref[place : place + 1, :]
            own_high, shared_high = (v.astype(BF16).astype(F32) for v in (own, shared))
            small = jnp.zeros((HALO, channels), F32)
            for to, value in enumerate((own_high, own - own_high, shared_high, shared - shared_high)):
                small = jnp.where(line == to, value, small)
            store_piece(core_ref, kept_ref, given_ref, place, step + part, small)


def merge_pairs(block):
    tail = block[-HALO:]
    line = lax.broadcasted_iota(jnp.int32, tail.shape, 0)
    own, shared = tail[0:1] + tail[1:2], tail[2:3] + tail[3:4]
    own_high, shared_high = own.astype(BF16).astype(F32), shared.astype(BF16).astype(F32)
    new = jnp.zeros_like(tail)
    for at, value in enumerate((own_high, own - own_high, shared_high, shared - shared_high)):
        new = jnp.where(line == at, value, new)
    return jnp.concatenate([block[:-HALO], new], axis=0)


def heads_kernel(piece_ref, total_ref, arrived_ref, out_ref, low_ref):
    total = merge_pairs(total_ref[...] + arrived_ref[...].astype(F32))
    line = lax.broadcasted_iota(jnp.int32, total.shape, 0)
    first = total.shape[0] - HALO
    own = (line >= first) & (line < first + 2)
    out_ref[...] = total
    low_ref[...] = jnp.where(own, piece_ref[...], total).astype(BF16)


def half_kernel(paired, chips, chip_ref, kept_ref, arrived_ref, *refs):
    outs = refs[-chips:]
    for bits in range(chips):
        place = lax.bitwise_xor(chip_ref[0], bits)
        value = kept_ref[place].astype(F32) + arrived_ref[place].astype(F32)
        if paired:
            value = merge_pairs(value)
        outs[bits][...] = value.astype(outs[bits].dtype)


def piece_kernel(parts, paired, cut, *refs):
    total = sum(ref[...].astype(F32) for ref in refs[:parts])
    first_ref, last_ref = refs[parts:]
    first_ref[...] = total[:cut].astype(BF16)
    last_ref[...] = merge_pairs(total[cut:]) if paired else total[cut:].astype(BF16)


def each_piece(core_ref, chip_ref, chips, groups, refs):
    refs = iter(refs)
    for part, bits_lists in enumerate(groups):
        number = 0
        for bits_list in bits_lists:
            for core, ref in ((core_ref[0], next(refs)), (1 - core_ref[0], next(refs))):
                for at, bits in enumerate(bits_list):
                    place = core * chips + lax.bitwise_xor(chip_ref[0], bits)
                    yield part, number, place, ref[at].astype(F32)
                    number += 1


def send_rows(buffer_ref, number, target_ref, place, sem_ref):
    rows = buffer_ref.shape[1]
    copy = pltpu.make_async_copy(
        buffer_ref.at[number],
        target_ref.at[pl.ds(pl.multiple_of(place * rows, 8), rows), :],
        sem_ref.at[number],
    )
    copy.start()
    return copy


def early_out_kernel(chips, groups, core_ref, chip_ref, *refs):
    gate_ref, output_ref, gate_buffer, output_buffer, gate_sems, output_sems = refs[-6:]
    out_rows, width = output_buffer.shape[1:]
    channels = gate_buffer.shape[2]
    copies = []
    for part, number, place, value in each_piece(core_ref, chip_ref, chips, groups, refs[:-6]):
        if part == 0:
            gate_buffer[number] = value
            copies.append(send_rows(gate_buffer, number, gate_ref, place, gate_sems))
        else:
            output_buffer[number] = jnp.concatenate(
                [value[i * out_rows : (i + 1) * out_rows] for i in range(width // channels)], axis=1
            )
            copies.append(send_rows(output_buffer, number, output_ref, place, output_sems))
    for copy in copies:
        copy.wait()


def late_out_kernel(chips, groups, core_ref, chip_ref, *refs):
    value_ref, buffer, sems = refs[-3:]
    copies = []
    for _, number, place, value in each_piece(core_ref, chip_ref, chips, groups, refs[:-3]):
        buffer[number] = value
        copies.append(send_rows(buffer, number, value_ref, place, sems))
    for copy in copies:
        copy.wait()


def shared_out_kernel(chips, groups, size, core_ref, chip_ref, head_ref, loose_ref, *refs):
    (
        state_ref, value_kernel_ref, value_bias_ref, state_kernel_ref, state_bias_ref, skip_ref,
        gated_ref, gain_ref, buffer, sems, own_ref, shared_ref,
    ) = refs[-12:]
    step, maps_width = buffer.shape[1:]
    channels = own_ref.shape[1]
    lanes = channels // 128
    rows = 2 * step // lanes
    copies = []
    for _, number, place, piece in each_piece(core_ref, chip_ref, chips, groups, refs[:-12]):
        stacked = jnp.concatenate(
            [piece[:rows, i * 128 : (i + 1) * 128] for i in range(lanes)], axis=0
        )
        buffer[number] = jnp.concatenate([stacked[:step], stacked[step:]], axis=1)
        copies.append(send_rows(buffer, number, state_ref, place, sems))
        own_ref[pl.ds(place, 1), :] = piece[rows : rows + 1] + piece[rows + 1 : rows + 2]
        shared_ref[pl.ds(place, 1), :] = piece[rows + 2 : rows + 3] + piece[rows + 3 : rows + 4]
    value_kernel_ref[...] = own_ref[:KERNEL, :]
    value_bias_ref[...] = own_ref[KERNEL, :]
    gated_ref[...] = own_ref[KERNEL + 1, :]
    heads = skip_ref.shape[0]
    at = lax.broadcasted_iota(jnp.int32, (heads, channels), 1)
    row = lax.broadcasted_iota(jnp.int32, (heads, channels), 0) * HEAD_DIM
    inside = (at >= row) & (at < row + HEAD_DIM)
    skip_ref[...] = jnp.sum(jnp.where(inside, own_ref[KERNEL + 2 : KERNEL + 3, :], 0.0), axis=1)
    own_width = gain_ref.shape[0]
    gain_rows = -(-own_width * size // channels)
    for head in range(size):
        row, begin = divmod(head * own_width, channels)

        @pl.when(head_ref[0] == head)
        def _(row=row, begin=begin):
            gain_ref[...] = shared_ref[row, begin : begin + own_width]

    for i in range(0, (KERNEL + 1) * maps_width, 128):
        tap, column_to = divmod(i, maps_width)
        row, column_from = divmod(i, channels)
        value = shared_ref[gain_rows + row : gain_rows + row + 1, column_from : column_from + 128]
        if tap < KERNEL:
            state_kernel_ref[tap : tap + 1, column_to : column_to + 128] = value
        else:
            state_bias_ref[column_to : column_to + 128] = value[0]
    for copy in copies:
        copy.wait()


SCALAR = "scalar"
WHOLE = "whole"
BLOCKED = "blocked"
LANES = "lanes"
LEADING = "leading"
LOOSE = "loose"


def run(kernel, name, flops, args, outs, steps=None, backward=False, scratch=()):
    at = (lambda i: steps - 1 - i) if backward else (lambda i: i)

    def spec(kind, shape):
        if isinstance(kind, int):
            return pl.BlockSpec((kind,) + shape[1:], lambda i: (at(i), 0))
        if kind == SCALAR:
            return pl.BlockSpec(memory_space=pltpu.SMEM)
        if kind == LOOSE:
            return pl.BlockSpec(memory_space=pl.ANY)
        if isinstance(kind, tuple):
            return pl.BlockSpec(*kind)
        if steps is None:
            return pl.BlockSpec(memory_space=pltpu.VMEM)
        if kind == BLOCKED:
            return pl.BlockSpec((CHUNK, shape[1]), lambda i: (at(i), 0))
        if kind == LANES:
            return pl.BlockSpec((shape[0], CHUNK), lambda i: (0, at(i)))
        if kind == LEADING:
            return pl.BlockSpec((1,) + shape[1:], lambda i: (at(i),) + (0,) * (len(shape) - 1))
        return pl.BlockSpec(shape, lambda i: (0,) * len(shape))

    moved = sum(a.size * a.dtype.itemsize for kind, a in args if kind != LOOSE)
    shapes = [jax.ShapeDtypeStruct(shape, dtype) for _, shape, dtype in outs]
    moved += sum(a.size * a.dtype.itemsize for a in shapes)
    return pl.pallas_call(
        kernel,
        out_shape=shapes,
        in_specs=[spec(kind, a.shape) for kind, a in args],
        out_specs=[spec(kind, shape) for kind, shape, _ in outs],
        scratch_shapes=list(scratch),
        compiler_params=pltpu.CompilerParams(vmem_limit_bytes=VMEM_LIMIT),
        cost_estimate=pl.CostEstimate(flops=flops, bytes_accessed=moved, transcendentals=0),
        name=name,
        **({} if steps is None else {"grid": (steps,)}),
    )(*(a for _, a in args))


def per_device(
    tokens, decay_codes, norm_gain, gate_weight, value_weight, state_weight, value_kernel, value_bias,
    state_kernel, state_bias, skip_scale, gated_gain, output_weight, cotangent,
):
    tokens, decay_codes, cotangent = tokens[0], decay_codes[0], cotangent[0]
    count, own_width = tokens.shape
    heads = skip_scale.shape[0]
    channels = heads * HEAD_DIM
    head_size, chips = lax.axis_size("head"), lax.axis_size("chip")
    seq_size = 2 * chips
    width = own_width * head_size
    maps_width = 2 * NSTATE
    chunks = count // CHUNK
    core = (SCALAR, lax.axis_index("core").astype(jnp.int32)[None])
    chip = (SCALAR, lax.axis_index("chip").astype(jnp.int32)[None])
    head = (SCALAR, lax.axis_index("head").astype(jnp.int32)[None])

    rows = count + MARGIN
    packed = jnp.concatenate(
        [
            from_behind(tokens[-HALO:], 1),
            tokens,
            jnp.broadcast_to(norm_gain[None], (MARGIN - HALO, own_width)),
        ],
        axis=0,
    )
    logs = decay_codes.astype(F32) * (-DECAY_STEP)
    input_weight = jnp.sqrt(-jnp.expm1(2.0 * logs))
    e_full, f_full, factors = run(
        decay_kernel, "decays", count * channels * 200,
        [(WHOLE, decay_codes), (WHOLE, input_weight)],
        [
            (WHOLE, (count, heads), F32),
            (WHOLE, (count, heads), F32),
            (WHOLE, (8, channels), F32),
        ],
    )
    parts, passed = line_parts(packed, "head")
    cotangent_parts = deal(
        run(
            copies_kernel, "copies", 1,
            [(LOOSE, parts[1]), (LOOSE, parts[-1]), (WHOLE, cotangent)],
            [(WHOLE, (head_size, count, own_width), BF16)],
        )[0],
        "head",
    )
    skip_full = jnp.repeat(skip_scale, HEAD_DIM)[None]

    half = rows // 2
    gain_rows = ((MARGIN - HALO, own_width), lambda i: ((HALO + count) // (MARGIN - HALO), 0))
    normed, scale_in, gain_full = run(
        functools.partial(norm_kernel, head_size), "norm", count * width * 10,
        [head, (half, passed)] + [(half, part) for part in parts]
        + [(gain_rows, part) for part in parts] + [(gain_rows, passed)],
        [(half, (rows, width), BF16), (half, (rows, 128), F32), (WHOLE, (8, width), F32)],
        steps=2,
    )
    value_raw = dot(normed, value_weight).astype(BF16)
    state_raw = dot(normed, state_weight).astype(BF16)
    conv, weighted, value_slope, maps, map_slope, local_end = run(
        conv_kernel, "conv", count * channels * 400,
        [
            (WHOLE, value_raw), (WHOLE, state_raw), (WHOLE, value_kernel), (WHOLE, value_bias[None]),
            (WHOLE, state_kernel), (WHOLE, state_bias[None]), (BLOCKED, f_full), (WHOLE, factors),
        ],
        [
            (BLOCKED, (count, channels), BF16),
            (BLOCKED, (count, channels), BF16),
            (BLOCKED, (count, channels), F32),
            (BLOCKED, (count, maps_width), BF16),
            (BLOCKED, (count, maps_width), F32),
            (WHOLE, (NSTATE + 8, channels), F32),
        ],
        steps=chunks,
    )
    gate_pre = dot(normed, gate_weight)[HALO : HALO + count]
    state_in = entering(core, chip, local_end, False, (gate_pre,))
    mixed_grad, full_cotangent = run(
        mixed_grad_kernel, "mixed_grad", 2 * count * width * channels,
        [(WHOLE, cotangent_parts), (WHOLE, output_weight)],
        [(WHOLE, (count, channels), F32), (WHOLE, (count, width), BF16)],
    )
    mixer, stats, high, low = run(
        mixer_kernel, "mixer", count * channels * 1000,
        [
            (WHOLE, state_in), (BLOCKED, maps), (BLOCKED, weighted), (BLOCKED, conv),
            (BLOCKED, e_full), (WHOLE, factors), (WHOLE, skip_full), (BLOCKED, gate_pre),
            (BLOCKED, mixed_grad), (WHOLE, gated_gain[None]),
        ],
        [
            (BLOCKED, (count, channels), F32),
            (LANES, (8, count), F32),
            (LEADING, (chunks, NSTATE, channels), BF16),
            (LEADING, (chunks, NSTATE, channels), BF16),
        ],
        steps=chunks,
        scratch=[pltpu.VMEM((NSTATE, channels), F32)],
    )
    mixed, gate_grad, mixer_grad, gate_small, start_grad, gate_cross = run(
        functools.partial(gate_kernel, float(channels * head_size), chunks, head_size),
        "gate", count * channels * 600,
        [(LANES, part) for part in turn_all(stats, "head")]
        + [
            (BLOCKED, mixer), (BLOCKED, gate_pre), (BLOCKED, mixed_grad), (WHOLE, gated_gain[None]),
            (BLOCKED, conv), (BLOCKED, e_full), (WHOLE, factors), (BLOCKED, maps),
        ],
        [
            (BLOCKED, (count, channels), BF16),
            (BLOCKED, (count, channels), BF16),
            (BLOCKED, (count, channels), F32),
            (WHOLE, (8, channels), F32),
            (WHOLE, (NSTATE + 8, channels), F32),
            (LANES, (8, count), F32),
        ],
        steps=chunks,
        backward=True,
    )
    step, out_rows = width // seq_size, channels // seq_size
    early_rows = step + out_rows * (width // channels)
    features = width // BLOCK
    feature_block = ((rows, BLOCK), lambda i: (0, i))
    every = features // (channels // BLOCK)
    out_parts = run(
        out_kernel, "out", 2 * count * channels * width,
        [(LOOSE, start_grad), (WHOLE, mixed), (WHOLE, output_weight)],
        [(WHOLE, (head_size, count, own_width), BF16)],
    )[0]
    early_made = []

    def make_early(pair):
        early_made.extend(
            run(
                early_kernel, "early", 4 * count * channels * width,
                [
                    (LOOSE, pair), core, (feature_block, normed), (WHOLE, gate_grad),
                    (((count, BLOCK), lambda i: (0, i // every)), mixed), (WHOLE, full_cotangent),
                    (BLOCK, gate_weight),
                ],
                [(WHOLE, (chips, early_rows, channels), BF16)] * 2
                + [(((1, BLOCK), lambda i: (0, i)), (1, width), F32)],
                steps=features,
                scratch=[pltpu.VMEM((BLOCK, width), F32)],
            )
        )
        return early_made[1:2]

    grad_after = entering(core, chip, start_grad, True, (out_parts,), make_early)
    early_kept, early_given, early_gain = early_made
    (early_gate, early_out), half_mark = sum_pieces(
        chip, early_kept, early_given, "early", step, False
    )
    branch = jnp.sum(deal(out_parts, "head").astype(F32), axis=0)
    block_out = (tokens.astype(F32) + branch).astype(BF16)

    value_grads, map_grads = run(
        functools.partial(back_kernel, chunks), "back", count * channels * 2000,
        [
            (LOOSE, half_mark), (WHOLE, grad_after), (BLOCKED, mixer_grad), (BLOCKED, e_full),
            (BLOCKED, f_full), (WHOLE, factors), (BLOCKED, weighted), (LEADING, high),
            (LEADING, low), (BLOCKED, maps), (BLOCKED, value_slope), (BLOCKED, map_slope),
            (WHOLE, skip_full),
        ],
        [(BLOCKED, (count, channels), F32), (BLOCKED, (count, maps_width), F32)],
        steps=chunks,
        backward=True,
        scratch=[pltpu.VMEM((NSTATE, channels), F32)],
    )
    after = from_behind(jnp.concatenate([value_grads[:8], map_grads[:8]], axis=1), -1)
    value_raw_grad, state_raw_grad, value_small, state_small, crossed = run(
        functools.partial(conv_back_kernel, chunks), "conv_back", count * channels * 100,
        [
            (BLOCKED, value_grads), (BLOCKED, map_grads), (WHOLE, after),
            (WHOLE, value_raw), (WHOLE, state_raw), (WHOLE, value_kernel), (WHOLE, state_kernel),
            (LANES, gate_cross),
        ],
        [
            (BLOCKED, (count, channels), BF16),
            (BLOCKED, (count, maps_width), BF16),
            (WHOLE, (8, channels), F32),
            (WHOLE, (8, maps_width), F32),
            (LANES, (8, count), F32),
        ],
        steps=chunks,
        backward=True,
        scratch=[pltpu.VMEM((8, channels), F32), pltpu.VMEM((8, maps_width), F32)],
    )
    lanes = channels // 128
    state_rows = 2 * step // lanes
    late_rows = step + state_rows + HALO
    late_kept, late_given = run(
        late_kernel, "late", 3 * count * channels * width,
        [
            (LOOSE, early_gate), core, (feature_block, normed), (WHOLE, value_raw_grad),
            (WHOLE, state_raw_grad),
            (WHOLE, value_small), (WHOLE, gate_small), (((1, BLOCK), lambda i: (0, i)), early_gain),
            (WHOLE, state_small), (BLOCK, value_weight), (BLOCK, state_weight),
            (((8, BLOCK), lambda i: (0, i)), gain_full),
        ],
        [(WHOLE, (chips, late_rows, channels), BF16)] * 2,
        steps=features,
        scratch=[
            pltpu.VMEM((HALO, channels), F32),
            pltpu.VMEM((HALO, channels), F32),
            pltpu.VMEM((8, width), F32),
        ],
    )
    normed_parts = run(
        functools.partial(normed_kernel, chunks), "normed", 4 * count * channels * width,
        [
            (LOOSE, late_given), (WHOLE, gate_grad), (WHOLE, value_raw_grad),
            (WHOLE, state_raw_grad), (own_width, gate_weight), (own_width, value_weight),
            (own_width, state_weight), (WHOLE, crossed),
        ],
        [(LEADING, (head_size, count + HALO, own_width), BF16)],
        steps=head_size,
    )[0]
    (late_piece, shared_piece), late_mark = sum_pieces(
        chip, late_kept, late_given, "late", step, True, (normed_parts,)
    )
    normed_parts = deal(normed_parts, "head")
    shared_piece = heads_sum(shared_piece)

    def unpack(kernel, name, pieces, outs, flops, scratch, extra=(), args=()):
        groups = [collect(*piece) for piece in pieces]
        bits = [[found[2] for found in group] for group in groups]
        arrays = [(WHOLE, value) for group in groups for found in group for value in found[:2]]
        return run(
            functools.partial(kernel, chips, bits, *extra), name, flops,
            [core, chip, *args] + arrays, outs, scratch=scratch,
        )

    sems = pltpu.SemaphoreType.DMA((seq_size,))
    gate_weight_gradient, output_weight_gradient = unpack(
        early_out_kernel, "early_out",
        [(early_gate, (2, 1), late_mark), (early_out, (1, 2), late_mark)],
        [(LOOSE, (width, channels), F32), (LOOSE, (channels, width), F32)], 4 * channels * width,
        [
            pltpu.VMEM((seq_size, step, channels), F32),
            pltpu.VMEM((seq_size, out_rows, width), F32),
            sems,
            sems,
        ],
    )
    value_weight_gradient = unpack(
        late_out_kernel, "late_out", [(late_piece, None)],
        [(LOOSE, (width, channels), F32)], 2 * channels * width,
        [pltpu.VMEM((seq_size, step, channels), F32), sems],
    )[0]
    (
        state_weight_gradient, value_kernel_gradient, value_bias_gradient, state_kernel_gradient,
        state_bias_gradient, skip_scale_gradient, gated_gain_gradient, norm_gain_gradient,
    ) = unpack(
        shared_out_kernel, "shared_out", [(shared_piece, (2, 1))],
        [
            (LOOSE, (width, maps_width), F32),
            (WHOLE, (KERNEL, channels), F32),
            (WHOLE, (channels,), F32),
            (WHOLE, (KERNEL, maps_width), F32),
            (WHOLE, (maps_width,), F32),
            (WHOLE, (heads,), F32),
            (WHOLE, (channels,), F32),
            (WHOLE, (own_width,), F32),
        ],
        2 * maps_width * width,
        [
            pltpu.VMEM((seq_size, step, maps_width), F32),
            sems,
            pltpu.VMEM((HALO, channels), F32),
            pltpu.VMEM((HALO, channels), F32),
        ],
        extra=(head_size,),
        args=[head, (LOOSE, gate_weight_gradient)],
    )
    tokens_gradient = run(
        functools.partial(last_kernel, float(width)), "last", count * own_width * 20,
        [
            (WHOLE, normed_parts), (WHOLE, tokens), (WHOLE, scale_in),
            (WHOLE, norm_gain[None]), (WHOLE, cotangent),
        ],
        [(WHOLE, (count, own_width), BF16)],
    )[0]
    return (
        block_out[None],
        tokens_gradient[None],
        norm_gain_gradient,
        gate_weight_gradient,
        value_weight_gradient,
        state_weight_gradient,
        value_kernel_gradient,
        value_bias_gradient,
        state_kernel_gradient,
        state_bias_gradient,
        skip_scale_gradient,
        gated_gain_gradient,
        output_weight_gradient,
    )


def solution(mesh):
    seq_size, head_size = mesh.shape["seq"], mesh.shape["head"]
    mesh = Mesh(mesh.devices.reshape(seq_size // 2, 2, head_size), ("chip", "core", "head"))
    seq = ("chip", "core")
    in_specs = (
        P(None, seq, "head"),
        P(None, seq, "head"),
        P("head"),
        P(None, "head"),
        P(None, "head"),
        P(),
        P(None, "head"),
        P("head"),
        P(),
        P(),
        P("head"),
        P("head"),
        P("head", None),
        P(None, seq, "head"),
    )
    out_specs = (
        P(None, seq, "head"),
        P(None, seq, "head"),
        P("head"),
        P(None, "head"),
        P(None, "head"),
        P(),
        P(None, "head"),
        P("head"),
        P(),
        P(),
        P("head"),
        P("head"),
        P("head", None),
    )
    return jax.shard_map(
        per_device, mesh=mesh, in_specs=in_specs, out_specs=out_specs, check_vma=False
    )
```

profile of v0, /device:TPU:1, one launch (start us, length us, event | category | flops | bytes accessed | tf_op | source)
XLA Modules:
  0.0 298.7 jit_solution(17782368183454213371)
XLA Ops:
  1.4 4.5 %collective-permute-start = (bf16[16,384]{1,0:T(8,128)(2,1)S(1)}, bf16[16,384]{1,0:T(8,128)(2,1)S(1)}, u32[]{:S(2)}, u32[]{:S(2)}) collective-permute-start(bf16[16,384]{1,0:T(8,128)(2,1)S(1)} %slice_bitcast_fusion), channel_id=1, source_target_pairs={{0,4},{4,8},{8,12},{12,16},{16,20},{20,24},{24,28},{1,5},{5,9},{9,... | collective-permute-start | bytes 36872 | tf_op jit(solution)/shard_map/ppermute | solution.py:46
  9.7 4.0 %collective-permute-start.3 = (bf16[544,384]{1,0:T(8,128)(2,1)S(1)}, bf16[544,384]{1,0:T(8,128)(2,1)S(1)}, u32[]{:S(2)}, u32[]{:S(2)}) collective-permute-start(bf16[544,384]{1,0:T(8,128)(2,1)S(1)} %pad_maximum_fusion.2.refs_0_.refs_4_), channel_id=1, source_target_pairs={{0,1},{1,2},{2,3},{4,5},{5,6},{6,7},{8,9},{9,10},{10,11},{12,13},{... | collective-permute-start | bytes 1253384 | tf_op jit(solution)/shard_map/ppermute | solution.py:67
  16.1 4.3 %collective-permute-done.4.refs_3_.refs_7_.three_ref = bf16[544,384]{1,0:T(8,128)(2,1)S(1)} collective-permute-done((bf16[544,384]{1,0:T(8,128)(2,1)S(1)}, bf16[544,384]{1,0:T(8,128)(2,1)S(1)}, u32[]{:S(2)}, u32[]{:S(2)}) %collective-permute-start.4) | collective-permute-done | bytes 417824 | tf_op jit(solution)/shard_map/ppermute | solution.py:68
  25.4 13.2 %all-to-all-start = ((bf16[4,512,384]{2,1,0:T(8,128)(2,1)}), bf16[4,512,384]{2,1,0:T(8,128)(2,1)}, u32[]{:S(2)}, u32[]{:S(2)}) async-start(bf16[4,512,384]{2,1,0:T(8,128)(2,1)} %copies.1), calls=%async_computation | async-start | bytes 3145728 | tf_op jit(solution)/shard_map/all_to_all | solution.py:74
  38.6 14.2 %collective-permute-done.1.refs_2_.refs_6_ = bf16[544,384]{1,0:T(8,128)(2,1)S(1)} collective-permute-done((bf16[544,384]{1,0:T(8,128)(2,1)S(1)}, bf16[544,384]{1,0:T(8,128)(2,1)S(1)}, u32[]{:S(2)}, u32[]{:S(2)}) %collective-permute-start.1) | collective-permute-done | bytes 417824 | tf_op jit(solution)/shard_map/ppermute | solution.py:55
  55.0 19.3 %collective-permute-done.2.passed_ref.refs_8_ = bf16[544,384]{1,0:T(8,128)(2,1)S(1)} collective-permute-done((bf16[544,384]{1,0:T(8,128)(2,1)S(1)}, bf16[544,384]{1,0:T(8,128)(2,1)S(1)}, u32[]{:S(2)}, u32[]{:S(2)}) %collective-permute-start.2) | collective-permute-done | bytes 417824 | tf_op jit(solution)/shard_map/ppermute | solution.py:69
  79.3 4.1 %conv.1 = (bf16[512,768]{1,0:T(8,128)(2,1)S(1)}, bf16[512,768]{1,0:T(8,128)(2,1)S(1)}, f32[512,768]{1,0:T(8,128)S(1)}, bf16[512,256]{1,0:T(8,128)(2,1)S(1)}, f32...) custom-call(bf16[544,768]{1,0:T(8,128)(2,1)S(1)} %convolution_convert_fusion.value_ref.value_raw_ref, ...), custom_call_target="tpu_custom_call" | custom-call | flops 157286400 | bytes 5523456 | tf_op jit(solution)/shard_map/conv/pallas_call | solution.py:863
  87.7 4.0 %collective-permute-start.8 = (f32[72,768]{1,0:T(8,128)}, f32[72,768]{1,0:T(8,128)}, u32[]{:S(2)}, u32[]{:S(2)}) collective-permute-start(f32[72,768]{1,0:T(8,128)} %before_pair.1.refs_0_), channel_id=1, source_target_pairs={{0,24},{8,16},{16,8},{24,0},{1,25},{9,17},{17,9},{25,1},{2,26},{10... | collective-permute-start | bytes 663560 | tf_op jit(solution)/shard_map/ppermute | solution.py:78
  93.3 4.4 %collective-permute-done.8.refs_3_ = f32[72,768]{1,0:T(8,128)} collective-permute-done((f32[72,768]{1,0:T(8,128)}, f32[72,768]{1,0:T(8,128)}, u32[]{:S(2)}, u32[]{:S(2)}) %collective-permute-start.8) | collective-permute-done | bytes 221216 | tf_op jit(solution)/shard_map/ppermute | solution.py:78
  97.7 5.5 %collective-permute-done.7.refs_2_ = f32[72,768]{1,0:T(8,128)} collective-permute-done((f32[72,768]{1,0:T(8,128)}, f32[72,768]{1,0:T(8,128)}, u32[]{:S(2)}, u32[]{:S(2)}) %collective-permute-start.7) | collective-permute-done | bytes 221216 | tf_op jit(solution)/shard_map/ppermute | solution.py:78
  112.7 2.9 mixed_grad.1
  119.9 5.3 %collective-permute-start.12 = (f32[8,512]{1,0:T(8,128)S(1)}, f32[8,512]{1,0:T(8,128)S(1)}, u32[]{:S(2)}, u32[]{:S(2)}) collective-permute-start(f32[8,512]{1,0:T(8,128)S(1)} %get-tuple-element.83.refs_0_), channel_id=1, source_target_pairs={{0,3},{1,0},{2,1},{3,2},{4,7},{5,4},{6,5},{7,6},{8,11},{9,8},{10,9... | collective-permute-start | bytes 49160 | tf_op jit(solution)/shard_map/ppermute | solution.py:55
  129.7 3.8 %gate.1 = (bf16[512,768]{1,0:T(8,128)(2,1)S(1)}, bf16[512,768]{1,0:T(8,128)(2,1)S(1)}, f32[512,768]{1,0:T(8,128)S(1)}, f32[8,768]{1,0:T(8,128)S(1)}, f32[136,768]{1,0:T(8,128)S(1)}, /*index=5*/f32[8,512]{1,0:T(8,128)S(1)}) custom-call(f32[8,512]{1,0:T(8,128)S(1)} %get-tuple-element.83.refs_0_, f32[8,512]{1,0:T(8,128)S(1)} %collective-permute-done.10.refs_1_, ...), custom_call_target="tpu_custom_call" | custom-call | flops 235929600 | bytes 9487872 | tf_op jit(solution)/shard_map/gate/pallas_call | solution.py:863
  136.5 2.9 out.1.refs_0_
  141.1 6.6 %early.1 = (bf16[4,384,768]{2,1,0:T(8,128)(2,1)S(1)}, bf16[4,384,768]{2,1,0:T(8,128)(2,1)}, f32[1,1536]{1,0:T(1,128)S(1)}) custom-call(f32[72,768]{1,0:T(8,128)S(1)} %after_pair.1.loose_ref.refs_0_, s32[1]{0:T(128)} %bitcast.core_ref, bf16[544,1536]{1,0:T(8,128)(2,1)S(1)} %copy-done.69, bf16[512,768]{1,0:T(8,128)(2,1)S(1)} %get-tuple-element.87.gate_ref.gate_grad_ref, ...), custom_call_target="tpu_custom_call" | custom-call | flops 2415919104 | bytes 11900932 | tf_op jit(solution)/shard_map/early/pallas_call | solution.py:863
  149.0 4.6 %all-to-all-start.1 = ((bf16[4,512,384]{2,1,0:T(8,128)(2,1)}), bf16[4,512,384]{2,1,0:T(8,128)(2,1)}, u32[]{:S(2)}, u32[]{:S(2)}) async-start(bf16[4,512,384]{2,1,0:T(8,128)(2,1)} %out.1.refs_0_), calls=%async_computation.1 | async-start | bytes 3145728 | tf_op jit(solution)/shard_map/all_to_all | solution.py:74
  163.1 3.7 %collective-permute-done.19.refs_2_ = f32[72,768]{1,0:T(8,128)S(1)} collective-permute-done((f32[72,768]{1,0:T(8,128)S(1)}, f32[72,768]{1,0:T(8,128)S(1)}, u32[]{:S(2)}, u32[]{:S(2)}) %collective-permute-start.19) | collective-permute-done | bytes 221216 | tf_op jit(solution)/shard_map/ppermute | solution.py:78
  169.5 5.6 %back.1 = (f32[512,768]{1,0:T(8,128)S(1)}, f32[512,256]{1,0:T(8,128)S(1)}) custom-call(f32[384,768]{1,0:T(8,128)S(1)} %get-tuple-element.91.refs_0_.early_ref, f32[128,768]{1,0:T(8,128)S(1)} %after_enter.1.state_in_ref, f32[512,768]{1,0:T(8,128)S(1)} %copy-done.25, f32[512,12]{1,0:T(8,128)S(1)} %get-tuple-element.81.e_ref.refs_9_, f32[512,12]{1,0:T(8,128)S(1)} %copy-done.33, ...), custom_call_target="tpu_custom_call" | custom-call | flops 786432000 | bytes 8858624 | tf_op jit(solution)/shard_map/back/pallas_call | solution.py:863
  177.5 14.7 %collective-permute-done.22.after_ref = f32[8,1024]{1,0:T(8,128)S(1)} collective-permute-done((f32[8,1024]{1,0:T(8,128)S(1)}, f32[8,1024]{1,0:T(8,128)S(1)}, u32[]{:S(2)}, u32[]{:S(2)}) %collective-permute-start.22) | collective-permute-done | bytes 32800 | tf_op jit(solution)/shard_map/ppermute | solution.py:46
  192.2 3.5 %conv_back.1 = (bf16[512,768]{1,0:T(8,128)(2,1)S(1)}, bf16[512,256]{1,0:T(8,128)(2,1)S(1)}, f32[8,768]{1,0:T(8,128)S(1)}, f32[8,256]{1,0:T(8,128)S(1)}, f32[8,512]{1,0:T(8,128)S(1)}) custom-call(f32[512,768]{1,0:T(8,128)S(1)} %get-tuple-element.101.value_ref, f32[512,256]{1,0:T(8,128)S(1)} %get-tuple-element.102.map_ref, ...), custom_call_target="tpu_custom_call" | custom-call | flops 39321600 | bytes 4366336 | tf_op jit(solution)/shard_map/conv_back/pallas_call | solution.py:863
  197.5 5.2 %late.1 = (bf16[4,272,768]{2,1,0:T(8,128)(2,1)S(1)}, bf16[4,272,768]{2,1,0:T(8,128)(2,1)}) custom-call(bf16[192,768]{1,0:T(8,128)(2,1)S(1)} %get-tuple-element.95.early_ref, s32[1]{0:T(128)} %bitcast.core_ref, bf16[544,1536]{1,0:T(8,128)(2,1)S(1)} %copy-done.70, bf16[512,768]{1,0:T(8,128)(2,1)S(1)} %get-tuple-element.104.value_ref.value_grad_ref, ...), custom_call_target="tpu_custom_call" | custom-call | flops 1811939328 | bytes 9320452 | tf_op jit(solution)/shard_map/late/pallas_call | solution.py:863
  202.7 5.3 %normed.1.refs_0_ = bf16[4,528,384]{2,1,0:T(8,128)(2,1)} custom-call(bf16[4,272,768]{2,1,0:T(8,128)(2,1)} %get-tuple-element.111.late_ref, bf16[512,768]{1,0:T(8,128)(2,1)S(1)} %copy-done.41, bf16[512,768]{1,0:T(8,128)(2,1)S(1)} %get-tuple-element.104.value_ref.value_grad_ref, bf16[512,256]{1,0:T(8,128)(2,1)S(1)} %get-tuple-element.105.state_ref.state_grad_ref, ...), custom_call_target="tpu_custom_call" | custom-call | flops 2415919104 | bytes 8978432 | tf_op jit(solution)/shard_map/normed/pallas_call | solution.py:863
  208.0 4.4 %all-to-all-start.2 = ((bf16[4,528,384]{2,1,0:T(8,128)(2,1)}), bf16[4,528,384]{2,1,0:T(8,128)(2,1)S(1)}, u32[]{:S(2)}, u32[]{:S(2)}) async-start(bf16[4,528,384]{2,1,0:T(8,128)(2,1)} %normed.1.refs_0_), calls=%async_computation.2 | async-start | bytes 3244032 | tf_op jit(solution)/shard_map/all_to_all | solution.py:74
  226.4 3.3 %collective-permute-done.32.refs_1_ = bf16[272,768]{1,0:T(8,128)(2,1)S(1)} collective-permute-done((bf16[272,768]{1,0:T(8,128)(2,1)}, bf16[272,768]{1,0:T(8,128)(2,1)S(1)}, u32[]{:S(2)}, u32[]{:S(2)}) %collective-permute-start.32) | collective-permute-done | bytes 417824 | tf_op jit(solution)/shard_map/ppermute | solution.py:78
  230.7 8.7 %collective-permute-done.34.refs_3_ = bf16[272,768]{1,0:T(8,128)(2,1)} collective-permute-done((bf16[272,768]{1,0:T(8,128)(2,1)}, bf16[272,768]{1,0:T(8,128)(2,1)}, u32[]{:S(2)}, u32[]{:S(2)}) %collective-permute-start.34) | collective-permute-done | bytes 417824 | tf_op jit(solution)/shard_map/ppermute | solution.py:78
  242.8 10.8 %collective-permute-done.35.arrived_ref = bf16[80,768]{1,0:T(8,128)(2,1)S(1)} collective-permute-done((bf16[80,768]{1,0:T(8,128)(2,1)S(1)}, bf16[80,768]{1,0:T(8,128)(2,1)S(1)}, u32[]{:S(2)}, u32[]{:S(2)}) %collective-permute-start.35) | collective-permute-done | bytes 122912 | tf_op jit(solution)/shard_map/ppermute | solution.py:89
  254.3 3.5 %collective-permute-start.41 = (bf16[1,192,768]{2,1,0:T(8,128)(2,1)S(1)}, bf16[1,192,768]{2,1,0:T(8,128)(2,1)S(1)}, u32[]{:S(2)}, u32[]{:S(2)}) collective-permute-start(bf16[1,192,768]{2,1,0:T(8,128)(2,1)S(1)} %bitcast.36), channel_id=1, source_target_pairs={{0,4},{4,0},{1,5},{5,1},{2,6},{6,2},{3,7},{7,3},{8,12},{12,8},{9,1... | collective-permute-start | bytes 884744 | tf_op jit(solution)/shard_map/ppermute | solution.py:50
  262.5 3.5 %collective-permute-done.44 = bf16[192,768]{1,0:T(8,128)(2,1)S(1)} collective-permute-done((bf16[192,768]{1,0:T(8,128)(2,1)S(1)}, bf16[192,768]{1,0:T(8,128)(2,1)S(1)}, u32[]{:S(2)}, u32[]{:S(2)}) %collective-permute-start.44) | collective-permute-done | bytes 294944 | tf_op jit(solution)/shard_map/ppermute | solution.py:78
  269.2 2.9 collective-permute-done.37
  276.7 3.6 %collective-permute-done.39.refs_2_ = bf16[2,80,768]{2,1,0:T(8,128)(2,1)} collective-permute-done((bf16[2,80,768]{2,1,0:T(8,128)(2,1)S(1)}, bf16[2,80,768]{2,1,0:T(8,128)(2,1)}, u32[]{:S(2)}, u32[]{:S(2)}) %collective-permute-start.39) | collective-permute-done | bytes 245792 | tf_op jit(solution)/shard_map/ppermute | solution.py:78
  287.3 5.7 %early_out.1 = (f32[1536,768]{1,0:T(8,128)}, f32[768,1536]{1,0:T(8,128)}) custom-call(s32[1]{0:T(128)} %bitcast.core_ref, s32[1]{0:T(128)} %bitcast.5.chip_ref, bf16[2,192,768]{2,1,0:T(8,128)(2,1)S(1)} %copy-done.2, bf16[2,192,768]{2,1,0:T(8,128)(2,1)} %collective-permute-done.25.refs_1_, bf16[2,192,768]{2,1,0:T(8,128)(2,1)} %collective-permute-done.26.refs_2_, ...), custom_call_target="tpu_custom_call" | custom-call | flops 4718592 | bytes 14155784 | tf_op jit(solution)/shard_map/early_out/pallas_call | solution.py:863
  295.5 3.0 %shared_out.1 = (f32[1536,256]{1,0:T(8,128)}, f32[4,768]{1,0:T(4,128)}, f32[768]{0:T(1024)}, f32[4,256]{1,0:T(4,128)}, f32[256]{0:T(256)}, /*index=5*/f32[12]{0:T(128)}, f32[768]{0:T(1024)}, f32[384]{0:T(512)}) custom-call(s32[1]{0:T(128)} %bitcast.core_ref, s32[1]{0:T(128)} %bitcast.5.chip_ref, s32[1]{0:T(128)} %bitcast.1.head_ref, ...), custom_call_target="tpu_custom_call" | custom-call | flops 786432 | bytes 2581052 | tf_op jit(solution)/shard_map/shared_out/pallas_call | solution.py:863
  (282 shorter events, 105.8 us)
Async XLA Ops:
  8.4 12.0 %collective-permute-start.4 = (bf16[544,384]{1,0:T(8,128)(2,1)S(1)}, bf16[544,384]{1,0:T(8,128)(2,1)S(1)}, u32[]{:S(2)}, u32[]{:S(2)}) collective-permute-start(bf16[544,384]{1,0:T(8,128)(2,1)S(1)} %pad_maximum_fusion.2.refs_0_.refs_4_), channel_id=1, source_target_pairs={{1,0},{2,1},{3,2},{5,4},{6,5},{7,6},{9,8},{10,9},{11,10},{13,12},{... | collective-permute-start | bytes 1253384 | tf_op jit(solution)/shard_map/ppermute | solution.py:68
  9.7 13.4 %collective-permute-start.3 = (bf16[544,384]{1,0:T(8,128)(2,1)S(1)}, bf16[544,384]{1,0:T(8,128)(2,1)S(1)}, u32[]{:S(2)}, u32[]{:S(2)}) collective-permute-start(bf16[544,384]{1,0:T(8,128)(2,1)S(1)} %pad_maximum_fusion.2.refs_0_.refs_4_), channel_id=1, source_target_pairs={{0,1},{1,2},{2,3},{4,5},{5,6},{6,7},{8,9},{9,10},{10,11},{12,13},{... | collective-permute-start | bytes 1253384 | tf_op jit(solution)/shard_map/ppermute | solution.py:67
  13.7 39.1 %collective-permute-start.1 = (bf16[544,384]{1,0:T(8,128)(2,1)S(1)}, bf16[544,384]{1,0:T(8,128)(2,1)S(1)}, u32[]{:S(2)}, u32[]{:S(2)}) collective-permute-start(bf16[544,384]{1,0:T(8,128)(2,1)S(1)} %pad_maximum_fusion.2.refs_0_.refs_4_), channel_id=1, source_target_pairs={{0,2},{1,3},{2,0},{3,1},{4,6},{5,7},{6,4},{7,5},{8,10},{9,11},{10,... | collective-permute-start | bytes 1253384 | tf_op jit(solution)/shard_map/ppermute | solution.py:55
  25.4 85.6 %all-to-all-start = ((bf16[4,512,384]{2,1,0:T(8,128)(2,1)}), bf16[4,512,384]{2,1,0:T(8,128)(2,1)}, u32[]{:S(2)}, u32[]{:S(2)}) async-start(bf16[4,512,384]{2,1,0:T(8,128)(2,1)} %copies.1), calls=%async_computation | async-start | bytes 3145728 | tf_op jit(solution)/shard_map/all_to_all | solution.py:74
  52.8 21.5 %collective-permute-start.2 = (bf16[544,384]{1,0:T(8,128)(2,1)S(1)}, bf16[544,384]{1,0:T(8,128)(2,1)S(1)}, u32[]{:S(2)}, u32[]{:S(2)}) collective-permute-start(bf16[544,384]{1,0:T(8,128)(2,1)S(1)} %collective-permute-done.1.refs_2_.refs_6_), channel_id=1, source_target_pairs={{2,3},{1,0},{6,7},{5,4},{10,11},{9,8},{14,15},{13,12},{18,19},{17,... | collective-permute-start | bytes 1253384 | tf_op jit(solution)/shard_map/ppermute | solution.py:69
  91.8 11.4 %collective-permute-start.7 = (f32[72,768]{1,0:T(8,128)}, f32[72,768]{1,0:T(8,128)}, u32[]{:S(2)}, u32[]{:S(2)}) collective-permute-start(f32[72,768]{1,0:T(8,128)} %before_pair.1.refs_0_), channel_id=1, source_target_pairs={{0,16},{8,24},{16,0},{24,8},{1,17},{9,25},{17,1},{25,9},{2,18},{10... | collective-permute-start | bytes 663560 | tf_op jit(solution)/shard_map/ppermute | solution.py:78
  93.2 10.5 %collective-permute-start.6 = (f32[72,768]{1,0:T(8,128)}, f32[72,768]{1,0:T(8,128)}, u32[]{:S(2)}, u32[]{:S(2)}) collective-permute-start(f32[72,768]{1,0:T(8,128)} %before_pair.1.refs_0_), channel_id=1, source_target_pairs={{0,8},{8,0},{16,24},{24,16},{1,9},{9,1},{17,25},{25,17},{2,10},{10... | collective-permute-start | bytes 663560 | tf_op jit(solution)/shard_map/ppermute | solution.py:78
  149.0 59.0 %all-to-all-start.1 = ((bf16[4,512,384]{2,1,0:T(8,128)(2,1)}), bf16[4,512,384]{2,1,0:T(8,128)(2,1)}, u32[]{:S(2)}, u32[]{:S(2)}) async-start(bf16[4,512,384]{2,1,0:T(8,128)(2,1)} %out.1.refs_0_), calls=%async_computation.1 | async-start | bytes 3145728 | tf_op jit(solution)/shard_map/all_to_all | solution.py:74
  154.6 12.2 %collective-permute-start.19 = (f32[72,768]{1,0:T(8,128)S(1)}, f32[72,768]{1,0:T(8,128)S(1)}, u32[]{:S(2)}, u32[]{:S(2)}) collective-permute-start(f32[72,768]{1,0:T(8,128)S(1)} %after_pair.1.loose_ref.refs_0_), channel_id=1, source_target_pairs={{0,16},{8,24},{16,0},{24,8},{1,17},{9,25},{17,1},{25,9},{2,18},{10... | collective-permute-start | bytes 663560 | tf_op jit(solution)/shard_map/ppermute | solution.py:78
  155.2 11.5 %collective-permute-start.18 = (f32[72,768]{1,0:T(8,128)S(1)}, f32[72,768]{1,0:T(8,128)S(1)}, u32[]{:S(2)}, u32[]{:S(2)}) collective-permute-start(f32[72,768]{1,0:T(8,128)S(1)} %after_pair.1.loose_ref.refs_0_), channel_id=1, source_target_pairs={{0,8},{8,0},{16,24},{24,16},{1,9},{9,1},{17,25},{25,17},{2,10},{10... | collective-permute-start | bytes 663560 | tf_op jit(solution)/shard_map/ppermute | solution.py:78
  160.3 35.4 %collective-permute-start.15 = (bf16[384,768]{1,0:T(8,128)(2,1)S(1)}, bf16[384,768]{1,0:T(8,128)(2,1)S(1)}, u32[]{:S(2)}, u32[]{:S(2)}) collective-permute-start(bf16[384,768]{1,0:T(8,128)(2,1)S(1)} %get-tuple-element.92), channel_id=1, source_target_pairs={{0,8},{8,0},{16,24},{24,16},{1,9},{9,1},{17,25},{25,17},{2,10},{10... | collective-permute-start | bytes 1769480 | tf_op jit(solution)/shard_map/ppermute | solution.py:78
  160.7 35.0 %collective-permute-start.16 = (bf16[384,768]{1,0:T(8,128)(2,1)S(1)}, bf16[384,768]{1,0:T(8,128)(2,1)S(1)}, u32[]{:S(2)}, u32[]{:S(2)}) collective-permute-start(bf16[384,768]{1,0:T(8,128)(2,1)S(1)} %get-tuple-element.93), channel_id=1, source_target_pairs={{0,16},{8,24},{16,0},{24,8},{1,17},{9,25},{17,1},{25,9},{2,18},{10... | collective-permute-start | bytes 1769480 | tf_op jit(solution)/shard_map/ppermute | solution.py:78
  161.7 34.1 %collective-permute-start.17 = (bf16[384,768]{1,0:T(8,128)(2,1)S(1)}, bf16[384,768]{1,0:T(8,128)(2,1)S(1)}, u32[]{:S(2)}, u32[]{:S(2)}) collective-permute-start(bf16[384,768]{1,0:T(8,128)(2,1)S(1)} %get-tuple-element.94), channel_id=1, source_target_pairs={{0,24},{8,16},{16,8},{24,0},{1,25},{9,17},{17,9},{25,1},{2,26},{10... | collective-permute-start | bytes 1769480 | tf_op jit(solution)/shard_map/ppermute | solution.py:78
  175.1 17.0 %collective-permute-start.22 = (f32[8,1024]{1,0:T(8,128)S(1)}, f32[8,1024]{1,0:T(8,128)S(1)}, u32[]{:S(2)}, u32[]{:S(2)}) collective-permute-start(f32[8,1024]{1,0:T(8,128)S(1)} %pad_maximum_fusion.4), channel_id=1, source_target_pairs={{4,0},{8,4},{12,8},{16,12},{20,16},{24,20},{28,24},{5,1},{9,5},{13... | collective-permute-start | bytes 98312 | tf_op jit(solution)/shard_map/ppermute | solution.py:46
  202.6 10.3 %collective-permute-start.24 = (bf16[4,272,768]{2,1,0:T(8,128)(2,1)}, bf16[4,272,768]{2,1,0:T(8,128)(2,1)}, u32[]{:S(2)}, u32[]{:S(2)}) collective-permute-start(bf16[4,272,768]{2,1,0:T(8,128)(2,1)} %get-tuple-element.111.late_ref), channel_id=1, source_target_pairs={{0,4},{4,0},{1,5},{5,1},{2,6},{6,2},{3,7},{7,3},{8,12},{12,8},{9,1... | collective-permute-start | bytes 5013512 | tf_op jit(solution)/shard_map/ppermute | solution.py:50
  208.0 74.5 %all-to-all-start.2 = ((bf16[4,528,384]{2,1,0:T(8,128)(2,1)}), bf16[4,528,384]{2,1,0:T(8,128)(2,1)S(1)}, u32[]{:S(2)}, u32[]{:S(2)}) async-start(bf16[4,528,384]{2,1,0:T(8,128)(2,1)} %normed.1.refs_0_), calls=%async_computation.2 | async-start | bytes 3244032 | tf_op jit(solution)/shard_map/all_to_all | solution.py:74
  216.5 13.2 %collective-permute-start.32 = (bf16[272,768]{1,0:T(8,128)(2,1)}, bf16[272,768]{1,0:T(8,128)(2,1)S(1)}, u32[]{:S(2)}, u32[]{:S(2)}) collective-permute-start(bf16[272,768]{1,0:T(8,128)(2,1)} %get-tuple-element.118), channel_id=1, source_target_pairs={{0,8},{8,0},{16,24},{24,16},{1,9},{9,1},{17,25},{25,17},{2,10},{10... | collective-permute-start | bytes 1253384 | tf_op jit(solution)/shard_map/ppermute | solution.py:78
  218.0 12.7 %collective-permute-start.33 = (bf16[272,768]{1,0:T(8,128)(2,1)}, bf16[272,768]{1,0:T(8,128)(2,1)}, u32[]{:S(2)}, u32[]{:S(2)}) collective-permute-start(bf16[272,768]{1,0:T(8,128)(2,1)} %get-tuple-element.119), channel_id=1, source_target_pairs={{0,16},{8,24},{16,0},{24,8},{1,17},{9,25},{17,1},{25,9},{2,18},{10... | collective-permute-start | bytes 1253384 | tf_op jit(solution)/shard_map/ppermute | solution.py:78
  218.9 20.4 %collective-permute-start.34 = (bf16[272,768]{1,0:T(8,128)(2,1)}, bf16[272,768]{1,0:T(8,128)(2,1)}, u32[]{:S(2)}, u32[]{:S(2)}) collective-permute-start(bf16[272,768]{1,0:T(8,128)(2,1)} %get-tuple-element.120), channel_id=1, source_target_pairs={{0,24},{8,16},{16,8},{24,0},{1,25},{9,17},{17,9},{25,1},{2,26},{10... | collective-permute-start | bytes 1253384 | tf_op jit(solution)/shard_map/ppermute | solution.py:78
  221.4 32.8 %collective-permute-start.26 = (bf16[2,192,768]{2,1,0:T(8,128)(2,1)}, bf16[2,192,768]{2,1,0:T(8,128)(2,1)}, u32[]{:S(2)}, u32[]{:S(2)}) collective-permute-start(bf16[2,192,768]{2,1,0:T(8,128)(2,1)} %tie.2.refs_0_), channel_id=1, source_target_pairs={{0,8},{8,0},{16,24},{24,16},{1,9},{9,1},{17,25},{25,17},{2,10},{10... | collective-permute-start | bytes 1769480 | tf_op jit(solution)/shard_map/ppermute | solution.py:78
  221.7 32.6 %collective-permute-start.25 = (bf16[2,192,768]{2,1,0:T(8,128)(2,1)}, bf16[2,192,768]{2,1,0:T(8,128)(2,1)}, u32[]{:S(2)}, u32[]{:S(2)}) collective-permute-start(bf16[2,192,768]{2,1,0:T(8,128)(2,1)} %tie.2.refs_0_), channel_id=1, source_target_pairs={{0,4},{4,0},{1,5},{5,1},{2,6},{6,2},{3,7},{7,3},{8,12},{12,8},{9,1... | collective-permute-start | bytes 1769480 | tf_op jit(solution)/shard_map/ppermute | solution.py:50
  229.7 37.5 %collective-permute-start.30 = (bf16[2,192,768]{2,1,0:T(8,128)(2,1)}, bf16[2,192,768]{2,1,0:T(8,128)(2,1)}, u32[]{:S(2)}, u32[]{:S(2)}) collective-permute-start(bf16[2,192,768]{2,1,0:T(8,128)(2,1)} %tie.3.refs_4_), channel_id=1, source_target_pairs={{0,16},{8,24},{16,0},{24,8},{1,17},{9,25},{17,1},{25,9},{2,18},{10... | collective-permute-start | bytes 1769480 | tf_op jit(solution)/shard_map/ppermute | solution.py:78
  240.7 12.9 %collective-permute-start.35 = (bf16[80,768]{1,0:T(8,128)(2,1)S(1)}, bf16[80,768]{1,0:T(8,128)(2,1)S(1)}, u32[]{:S(2)}, u32[]{:S(2)}) collective-permute-start(bf16[80,768]{1,0:T(8,128)(2,1)S(1)} %convert_element_type.29), channel_id=1, source_target_pairs={{0,1},{1,0},{2,3},{3,2},{4,5},{5,4},{6,7},{7,6},{8,9},{9,8},{10,11... | collective-permute-start | bytes 368648 | tf_op jit(solution)/shard_map/ppermute | solution.py:89
  242.0 17.8 %collective-permute-start.46 = (bf16[192,768]{1,0:T(8,128)(2,1)S(1)}, bf16[192,768]{1,0:T(8,128)(2,1)S(1)}, u32[]{:S(2)}, u32[]{:S(2)}) collective-permute-start(bf16[192,768]{1,0:T(8,128)(2,1)S(1)} %get-tuple-element.126), channel_id=1, source_target_pairs={{0,24},{8,16},{16,8},{24,0},{1,25},{9,17},{17,9},{25,1},{2,26},{10... | collective-permute-start | bytes 884744 | tf_op jit(solution)/shard_map/ppermute | solution.py:78
  253.7 12.4 %collective-permute-start.44 = (bf16[192,768]{1,0:T(8,128)(2,1)S(1)}, bf16[192,768]{1,0:T(8,128)(2,1)S(1)}, u32[]{:S(2)}, u32[]{:S(2)}) collective-permute-start(bf16[192,768]{1,0:T(8,128)(2,1)S(1)} %get-tuple-element.126), channel_id=1, source_target_pairs={{0,16},{8,24},{16,0},{24,8},{1,17},{9,25},{17,1},{25,9},{2,18},{10... | collective-permute-start | bytes 884744 | tf_op jit(solution)/shard_map/ppermute | solution.py:78
  254.3 13.4 %collective-permute-start.41 = (bf16[1,192,768]{2,1,0:T(8,128)(2,1)S(1)}, bf16[1,192,768]{2,1,0:T(8,128)(2,1)S(1)}, u32[]{:S(2)}, u32[]{:S(2)}) collective-permute-start(bf16[1,192,768]{2,1,0:T(8,128)(2,1)S(1)} %bitcast.36), channel_id=1, source_target_pairs={{0,4},{4,0},{1,5},{5,1},{2,6},{6,2},{3,7},{7,3},{8,12},{12,8},{9,1... | collective-permute-start | bytes 884744 | tf_op jit(solution)/shard_map/ppermute | solution.py:50
  259.8 13.2 %collective-permute-start.47 = (bf16[1,192,768]{2,1,0:T(8,128)(2,1)S(1)}, bf16[1,192,768]{2,1,0:T(8,128)(2,1)S(1)}, u32[]{:S(2)}, u32[]{:S(2)}) collective-permute-start(bf16[1,192,768]{2,1,0:T(8,128)(2,1)S(1)} %bitcast.38), channel_id=1, source_target_pairs={{0,4},{4,0},{1,5},{5,1},{2,6},{6,2},{3,7},{7,3},{8,12},{12,8},{9,1... | collective-permute-start | bytes 884744 | tf_op jit(solution)/shard_map/ppermute | solution.py:50
  267.8 19.5 %collective-permute-start.29 = (bf16[2,192,768]{2,1,0:T(8,128)(2,1)S(1)}, bf16[2,192,768]{2,1,0:T(8,128)(2,1)}, u32[]{:S(2)}, u32[]{:S(2)}) collective-permute-start(bf16[2,192,768]{2,1,0:T(8,128)(2,1)S(1)} %copy-done.3), channel_id=1, source_target_pairs={{0,4},{4,0},{1,5},{5,1},{2,6},{6,2},{3,7},{7,3},{8,12},{12,8},{9,1... | collective-permute-start | bytes 1769480 | tf_op jit(solution)/shard_map/ppermute | solution.py:50
  268.1 19.2 %collective-permute-start.27 = (bf16[2,192,768]{2,1,0:T(8,128)(2,1)}, bf16[2,192,768]{2,1,0:T(8,128)(2,1)}, u32[]{:S(2)}, u32[]{:S(2)}) collective-permute-start(bf16[2,192,768]{2,1,0:T(8,128)(2,1)} %collective-permute-done.26.refs_2_), channel_id=1, source_target_pairs={{0,4},{4,0},{1,5},{5,1},{2,6},{6,2},{3,7},{7,3},{8,12},{12,8},{9,1... | collective-permute-start | bytes 1769480 | tf_op jit(solution)/shard_map/ppermute | solution.py:50
  272.1 15.2 %collective-permute-start.31 = (bf16[2,192,768]{2,1,0:T(8,128)(2,1)}, bf16[2,192,768]{2,1,0:T(8,128)(2,1)}, u32[]{:S(2)}, u32[]{:S(2)}) collective-permute-start(bf16[2,192,768]{2,1,0:T(8,128)(2,1)} %collective-permute-done.30.refs_6_), channel_id=1, source_target_pairs={{0,4},{4,0},{1,5},{5,1},{2,6},{6,2},{3,7},{7,3},{8,12},{12,8},{9,1... | collective-permute-start | bytes 1769480 | tf_op jit(solution)/shard_map/ppermute | solution.py:50
  276.0 17.1 %collective-permute-start.38 = (bf16[2,80,768]{2,1,0:T(8,128)(2,1)S(1)}, bf16[2,80,768]{2,1,0:T(8,128)(2,1)}, u32[]{:S(2)}, u32[]{:S(2)}) collective-permute-start(bf16[2,80,768]{2,1,0:T(8,128)(2,1)S(1)} %pad_maximum_fusion.3.refs_0_), channel_id=1, source_target_pairs={{0,4},{4,0},{1,5},{5,1},{2,6},{6,2},{3,7},{7,3},{8,12},{12,8},{9,1... | collective-permute-start | bytes 737288 | tf_op jit(solution)/shard_map/ppermute | solution.py:50
  280.3 12.8 %collective-permute-start.40 = (bf16[2,80,768]{2,1,0:T(8,128)(2,1)}, bf16[2,80,768]{2,1,0:T(8,128)(2,1)}, u32[]{:S(2)}, u32[]{:S(2)}) collective-permute-start(bf16[2,80,768]{2,1,0:T(8,128)(2,1)} %collective-permute-done.39.refs_2_), channel_id=1, source_target_pairs={{0,4},{4,0},{1,5},{5,1},{2,6},{6,2},{3,7},{7,3},{8,12},{12,8},{9,1... | collective-permute-start | bytes 737288 | tf_op jit(solution)/shard_map/ppermute | solution.py:50
  (98 other events, 718.5 us)
where the time goes:
time: 300 us; the launch traced here: 299 us
  waiting for transfers between devices  113 us (38%)
  starting transfers between devices  80.9 us (27%)
  Pallas kernels  68.8 us (23%)
  local copies, waits for them, and re-layouts  24.2 us (8%)
  other arithmetic  6.56 us (2%)
  matrix products  3.43 us (1%)
    pallas_call x29, Pallas kernels, run(): pl.pallas_call(kernel, out_shape=shapes, in_specs=[spec(kind, a.shape) fo...  68.8 us
    ppermute x21, waiting for transfers between devices, cross(): lax.ppermute(value, 'chip', [(i, i ^ bits) for i in range(lax.axis_size('...  37.5 us
    unnamed x159, local copies, waits for them, and re-layouts  22.6 us
    all_to_all x3, starting transfers between devices, deal(): return lax.all_to_all(parts, axis, 0, 0)  22.2 us
    ppermute x1, waiting for transfers between devices, line_parts(): passed = lax.ppermute(two, axis, [(2, 3), (1, 0)])  19.3 us
    ppermute x4, waiting for transfers between devices, turn(): lax.ppermute(value, axis, [(i, (i + by) % size) for i in range(size)])  18.3 us
    ppermute x16, starting transfers between devices, beside(): return lax.ppermute(value, 'core', [(0, 1), (1, 0)])  18.3 us
    ppermute x21, starting transfers between devices, cross(): lax.ppermute(value, 'chip', [(i, i ^ bits) for i in range(lax.axis_size('...  17.7 us
  transfers between devices with their start and end apart: 51, of which 24 were waited for; matrix products, arithmetic and copies ran while one was open for 3% of the time, Pallas kernels for 17%

commit v1 on v0

--- a/solution.py
+++ b/solution.py
@@ -117,24 +117,68 @@
         functools.partial(enter_kernel, backward), name + "_enter", total.size,
         [core, (WHOLE, partner), (WHOLE, prefix), (WHOLE, beside(prefix))],
         [(WHOLE, (NSTATE, channels), F32)],
-    )[0]
-
-
-def sum_pieces(chip, kept, given, name, cut, paired, before_half=()):
+    )[0], prefix
+
+
+def sum_pieces(chip, kept, given, name, square, cut, paired, before_half=()):
     chips, rows, channels = kept.shape
     arrived = beside(given)
     size = chips * rows * channels
-    halves = run(
-        functools.partial(half_kernel, paired, chips), name + "_half", size,
+    if paired:
+        outs = [(WHOLE, (cut, channels), BF16), (WHOLE, (rows - cut, channels), F32)]
+    else:
+        outs = [(WHOLE, (rows, channels), BF16)]
+    if chips != 4 or not square:
+        halves = run(
+            functools.partial(half_kernel, paired, chips), name + "_half", size,
+            [chip, (WHOLE, kept), (WHOLE, arrived)] + [(LOOSE, mark) for mark in before_half],
+            [(WHOLE, (rows, channels), F32)] + [(WHOLE, (rows, channels), BF16)] * (chips - 1),
+        )
+        parts = [halves[0]] + [cross(halves[bits], bits) for bits in range(1, chips)]
+        found = run(
+            functools.partial(piece_kernel, chips, paired, cut), name + "_piece", size,
+            [(WHOLE, part) for part in parts], outs,
+        )
+        return found, halves[0]
+    rest = rows - cut
+    state = run(
+        square_half_kernel, name + "_half", size,
         [chip, (WHOLE, kept), (WHOLE, arrived)] + [(LOOSE, mark) for mark in before_half],
-        [(WHOLE, (rows, channels), F32)] + [(WHOLE, (rows, channels), BF16)] * (chips - 1),
-    )
-    parts = [halves[0]] + [cross(halves[bits], bits) for bits in range(1, chips)]
+        [
+            (WHOLE, (2, cut, channels), F32), (WHOLE, (2, cut, channels), BF16),
+            (WHOLE, (2, rest, channels), F32), (WHOLE, (2, rest, channels), BF16),
+        ],
+    )
+    return state, state[0]
+
+
+def square_next(name, state, size, mark):
+    first, first_give, last, last_give = state
+    _, cut, channels = first.shape
+    rest = last.shape[1]
     return run(
-        functools.partial(piece_kernel, chips, paired, cut), name + "_piece", size,
-        [(WHOLE, part) for part in parts],
-        [(WHOLE, (cut, channels), BF16), (WHOLE, (rows - cut, channels), F32 if paired else BF16)],
-    ), halves[0]
+        square_next_kernel, name + "_next", size,
+        [
+            (WHOLE, first), (WHOLE, cross(first_give, 1)),
+            (WHOLE, last), (WHOLE, cross(last_give, 2)), (LOOSE, mark),
+        ],
+        [
+            (WHOLE, (cut, channels), F32), (WHOLE, (cut, channels), BF16),
+            (WHOLE, (rest, channels), F32), (WHOLE, (rest, channels), BF16),
+        ],
+    )
+
+
+def square_end(name, state, outs, size, mark):
+    first, first_give, last, last_give = state
+    return run(
+        square_last_kernel, name + "_piece", size,
+        [
+            (WHOLE, first), (WHOLE, cross(first_give, 2)),
+            (WHOLE, last), (WHOLE, cross(last_give, 1)), (LOOSE, mark),
+        ],
+        outs,
+    )
 
 
 def collect(piece, order, mark=None):
@@ -305,7 +349,7 @@
         pl.when(mine == me)(functools.partial(write, me))
 
 
-def copies_kernel(one_ref, three_ref, own_ref, out_ref):
+def copies_kernel(loose_ref, own_ref, out_ref):
     for i in range(out_ref.shape[0]):
         out_ref[i] = own_ref[...]
 
@@ -724,9 +768,41 @@
 
 def piece_kernel(parts, paired, cut, *refs):
     total = sum(ref[...].astype(F32) for ref in refs[:parts])
-    first_ref, last_ref = refs[parts:]
+    if not paired:
+        refs[-1][...] = total.astype(BF16)
+        return
+    first_ref, last_ref = refs[-2:]
     first_ref[...] = total[:cut].astype(BF16)
-    last_ref[...] = merge_pairs(total[cut:]) if paired else total[cut:].astype(BF16)
+    last_ref[...] = merge_pairs(total[cut:])
+
+
+def square_half_kernel(
+    chip_ref, kept_ref, arrived_ref, loose_ref, first_ref, first_give_ref, last_ref, last_give_ref
+):
+    cut = first_ref.shape[1]
+    for bits in range(4):
+        place = lax.bitwise_xor(chip_ref[0], bits)
+        value = kept_ref[place].astype(F32) + arrived_ref[place].astype(F32)
+        low, high = bits & 1, bits >> 1
+        ref = first_give_ref if low else first_ref
+        ref[high] = value[:cut].astype(ref.dtype)
+        ref = last_give_ref if high else last_ref
+        ref[low] = value[cut:].astype(ref.dtype)
+
+
+def square_next_kernel(
+    first_ref, first_got_ref, last_ref, last_got_ref, loose_ref,
+    first_out_ref, first_give_ref, last_out_ref, last_give_ref,
+):
+    first_out_ref[...] = first_ref[0] + first_got_ref[0].astype(F32)
+    first_give_ref[...] = (first_ref[1] + first_got_ref[1].astype(F32)).astype(BF16)
+    last_out_ref[...] = last_ref[0] + last_got_ref[0].astype(F32)
+    last_give_ref[...] = (last_ref[1] + last_got_ref[1].astype(F32)).astype(BF16)
+
+
+def square_last_kernel(first_ref, first_got_ref, last_ref, last_got_ref, loose_ref, *outs):
+    outs[0][...] = (first_ref[...] + first_got_ref[...].astype(F32)).astype(BF16)
+    outs[1][...] = (last_ref[...] + last_got_ref[...].astype(F32)).astype(BF16)
 
 
 def each_piece(core_ref, chip_ref, chips, groups, refs):
@@ -911,14 +987,6 @@
         ],
     )
     parts, passed = line_parts(packed, "head")
-    cotangent_parts = deal(
-        run(
-            copies_kernel, "copies", 1,
-            [(LOOSE, parts[1]), (LOOSE, parts[-1]), (WHOLE, cotangent)],
-            [(WHOLE, (head_size, count, own_width), BF16)],
-        )[0],
-        "head",
-    )
     skip_full = jnp.repeat(skip_scale, HEAD_DIM)[None]
 
     half = rows // 2
@@ -930,6 +998,13 @@
         [(half, (rows, width), BF16), (half, (rows, 128), F32), (WHOLE, (8, width), F32)],
         steps=2,
     )
+    cotangent_parts = deal(
+        run(
+            copies_kernel, "copies", 1, [(LOOSE, normed), (WHOLE, cotangent)],
+            [(WHOLE, (head_size, count, own_width), BF16)],
+        )[0],
+        "head",
+    )
     value_raw = dot(normed, value_weight).astype(BF16)
     state_raw = dot(normed, state_weight).astype(BF16)
     conv, weighted, value_slope, maps, map_slope, local_end = run(
@@ -949,7 +1024,7 @@
         steps=chunks,
     )
     gate_pre = dot(normed, gate_weight)[HALO : HALO + count]
-    state_in = entering(core, chip, local_end, False, (gate_pre,))
+    state_in, _ = entering(core, chip, local_end, False, (gate_pre,))
     mixed_grad, full_cotangent = run(
         mixed_grad_kernel, "mixed_grad", 2 * count * width * channels,
         [(WHOLE, cotangent_parts), (WHOLE, output_weight)],
@@ -1019,10 +1094,10 @@
         )
         return early_made[1:2]
 
-    grad_after = entering(core, chip, start_grad, True, (out_parts,), make_early)
+    grad_after, after_prefix = entering(core, chip, start_grad, True, (out_parts,), make_early)
     early_kept, early_given, early_gain = early_made
-    (early_gate, early_out), half_mark = sum_pieces(
-        chip, early_kept, early_given, "early", step, False
+    early_state, half_mark = sum_pieces(
+        chip, early_kept, early_given, "early", True, step, False, (after_prefix,)
     )
     branch = jnp.sum(deal(out_parts, "head").astype(F32), axis=0)
     block_out = (tokens.astype(F32) + branch).astype(BF16)
@@ -1059,6 +1134,28 @@
         backward=True,
         scratch=[pltpu.VMEM((8, channels), F32), pltpu.VMEM((8, maps_width), F32)],
     )
+    next_mark = early_state[0]
+    if chips == 4:
+        early_state = square_next("early", early_state, early_rows * channels, crossed)
+        next_mark = early_state[0]
+    normed_parts = run(
+        functools.partial(normed_kernel, chunks), "normed", 4 * count * channels * width,
+        [
+            (LOOSE, next_mark), (WHOLE, gate_grad), (WHOLE, value_raw_grad),
+            (WHOLE, state_raw_grad), (own_width, gate_weight), (own_width, value_weight),
+            (own_width, state_weight), (WHOLE, crossed),
+        ],
+        [(LEADING, (head_size, count + HALO, own_width), BF16)],
+        steps=head_size,
+    )[0]
+    if chips == 4:
+        early_gate, early_out = square_end(
+            "early", early_state,
+            [(WHOLE, (step, channels), BF16), (WHOLE, (early_rows - step, channels), BF16)],
+            early_rows * channels, normed_parts,
+        )
+    else:
+        early_gate, early_out = early_state[0][:step], early_state[0][step:]
     lanes = channels // 128
     state_rows = 2 * step // lanes
     late_rows = step + state_rows + HALO
@@ -1079,18 +1176,8 @@
             pltpu.VMEM((8, width), F32),
         ],
     )
-    normed_parts = run(
-        functools.partial(normed_kernel, chunks), "normed", 4 * count * channels * width,
-        [
-            (LOOSE, late_given), (WHOLE, gate_grad), (WHOLE, value_raw_grad),
-            (WHOLE, state_raw_grad), (own_width, gate_weight), (own_width, value_weight),
-            (own_width, state_weight), (WHOLE, crossed),
-        ],
-        [(LEADING, (head_size, count + HALO, own_width), BF16)],
-        steps=head_size,
-    )[0]
     (late_piece, shared_piece), late_mark = sum_pieces(
-        chip, late_kept, late_given, "late", step, True, (normed_parts,)
+        chip, late_kept, late_given, "late", False, step, True
     )
     normed_parts = deal(normed_parts, "head")
     shared_piece = heads_sum(shared_piece)

time: 300 us -> 274 us (0.913)
  starting transfers between devices: 80.9 us -> 64.9 us
  waiting for transfers between devices: 113 us -> 101 us
    ppermute x2, waiting for transfers between devices: 15.5 us -> 4.13 us  [from_behind(): return lax.ppermute(value, axis, pairs)]
    ppermute x1, waiting for transfers between devices: 19.3 us -> 8.48 us  [line_parts(): passed = lax.ppermute(two, axis, [(2, 3), (1, 0)])]
    ppermute x21 -> x22, waiting for transfers between devices: 37.5 us -> 46.8 us  [cross(): lax.ppermute(value, 'chip', [(i, i ^ bits) for i in range(lax.axis_size('...]
    all_to_all x3, starting transfers between devices: 22.2 us -> 13.4 us  [deal(): return lax.all_to_all(parts, axis, 0, 0)]
    ppermute x2, waiting for transfers between devices: 12.8 us -> 17.8 us  [heads_sum(): arrived = lax.ppermute(low, 'head', [(i, i ^ bits) for i in range(size)])]
    ppermute x16, starting transfers between devices: 18.3 us -> 15.2 us  [beside(): return lax.ppermute(value, 'core', [(0, 1), (1, 0)])]
    ppermute x21 -> x22, starting transfers between devices: 17.7 us -> 16.8 us  [cross(): lax.ppermute(value, 'chip', [(i, i ^ bits) for i in range(lax.axis_size('...]
    pallas_call x29 -> x30, Pallas kernels: 68.8 us -> 69.3 us  [run(): pl.pallas_call(kernel, out_shape=shapes, in_specs=[spec(kind, a.shape) fo...]
  transfers between devices with their start and end apart: 51 -> 52, of which waited for: 24 -> 25; matrix products, arithmetic and copies ran while one was open for 3% -> 4% of each run, Pallas kernels for 17% -> 18%
where the time goes in v1:
time: 274 us; the launch traced here: 273 us
  waiting for transfers between devices  101 us (37%)
  Pallas kernels  69.3 us (25%)
  starting transfers between devices  64.9 us (24%)
  local copies, waits for them, and re-layouts  23.7 us (9%)
  other arithmetic  6.56 us (2%)
  matrix products  5.02 us (2%)
    pallas_call x30, Pallas kernels, run(): pl.pallas_call(kernel, out_shape=shapes, in_specs=[spec(kind, a.shape) fo...  69.3 us
    ppermute x22, waiting for transfers between devices, cross(): lax.ppermute(value, 'chip', [(i, i ^ bits) for i in range(lax.axis_size('...  46.8 us
    unnamed x195, local copies, waits for them, and re-layouts  22.1 us
    ppermute x2, waiting for transfers between devices, heads_sum(): arrived = lax.ppermute(low, 'head', [(i, i ^ bits) for i in range(size)])  17.8 us
    ppermute x22, starting transfers between devices, cross(): lax.ppermute(value, 'chip', [(i, i ^ bits) for i in range(lax.axis_size('...  16.8 us
    ppermute x4, waiting for transfers between devices, turn(): lax.ppermute(value, axis, [(i, (i + by) % size) for i in range(size)])  15.9 us
    ppermute x16, starting transfers between devices, beside(): return lax.ppermute(value, 'core', [(0, 1), (1, 0)])  15.2 us
    all_to_all x3, starting transfers between devices, deal(): return lax.all_to_all(parts, axis, 0, 0)  13.4 us
  transfers between devices with their start and end apart: 52, of which 25 were waited for; matrix products, arithmetic and copies ran while one was open for 4% of the time, Pallas kernels for 18%

profile of v1, /device:TPU:1, one launch (start us, length us, event | category | flops | bytes accessed | tf_op | source)
XLA Modules:
  0.0 272.7 jit_solution(6251608121921285904)
XLA Ops:
  1.4 4.5 %collective-permute-start = (bf16[16,384]{1,0:T(8,128)(2,1)S(1)}, bf16[16,384]{1,0:T(8,128)(2,1)S(1)}, u32[]{:S(2)}, u32[]{:S(2)}) collective-permute-start(bf16[16,384]{1,0:T(8,128)(2,1)S(1)} %slice_bitcast_fusion), channel_id=1, source_target_pairs={{0,4},{4,8},{8,12},{12,16},{16,20},{20,24},{24,28},{1,5},{5,9},{9,... | collective-permute-start | bytes 36872 | tf_op jit(solution)/shard_map/ppermute | solution.py:46
  10.8 3.2 %collective-permute-start.3 = (bf16[544,384]{1,0:T(8,128)(2,1)S(1)}, bf16[544,384]{1,0:T(8,128)(2,1)S(1)}, u32[]{:S(2)}, u32[]{:S(2)}) collective-permute-start(bf16[544,384]{1,0:T(8,128)(2,1)S(1)} %pad_maximum_fusion.2.refs_0_.refs_4_), channel_id=1, source_target_pairs={{0,1},{1,2},{2,3},{4,5},{5,6},{6,7},{8,9},{9,10},{10,11},{12,13},{... | collective-permute-start | bytes 1253384 | tf_op jit(solution)/shard_map/ppermute | solution.py:67
  15.3 14.4 %collective-permute-done.1.refs_2_.refs_6_ = bf16[544,384]{1,0:T(8,128)(2,1)S(1)} collective-permute-done((bf16[544,384]{1,0:T(8,128)(2,1)S(1)}, bf16[544,384]{1,0:T(8,128)(2,1)S(1)}, u32[]{:S(2)}, u32[]{:S(2)}) %collective-permute-start.1) | collective-permute-done | bytes 417824 | tf_op jit(solution)/shard_map/ppermute | solution.py:55
  31.0 4.0 %collective-permute-done.4.refs_3_.refs_7_ = bf16[544,384]{1,0:T(8,128)(2,1)S(1)} collective-permute-done((bf16[544,384]{1,0:T(8,128)(2,1)S(1)}, bf16[544,384]{1,0:T(8,128)(2,1)S(1)}, u32[]{:S(2)}, u32[]{:S(2)}) %collective-permute-start.4) | collective-permute-done | bytes 417824 | tf_op jit(solution)/shard_map/ppermute | solution.py:68
  35.1 8.5 %collective-permute-done.2.passed_ref.refs_8_ = bf16[544,384]{1,0:T(8,128)(2,1)S(1)} collective-permute-done((bf16[544,384]{1,0:T(8,128)(2,1)S(1)}, bf16[544,384]{1,0:T(8,128)(2,1)S(1)}, u32[]{:S(2)}, u32[]{:S(2)}) %collective-permute-start.2) | collective-permute-done | bytes 417824 | tf_op jit(solution)/shard_map/ppermute | solution.py:69
  48.4 4.5 %all-to-all-start = ((bf16[4,512,384]{2,1,0:T(8,128)(2,1)}), bf16[4,512,384]{2,1,0:T(8,128)(2,1)}, u32[]{:S(2)}, u32[]{:S(2)}) async-start(bf16[4,512,384]{2,1,0:T(8,128)(2,1)} %copies.1), calls=%async_computation | async-start | bytes 3145728 | tf_op jit(solution)/shard_map/all_to_all | solution.py:74
  58.1 4.1 %conv.1 = (bf16[512,768]{1,0:T(8,128)(2,1)S(1)}, bf16[512,768]{1,0:T(8,128)(2,1)S(1)}, f32[512,768]{1,0:T(8,128)S(1)}, bf16[512,256]{1,0:T(8,128)(2,1)S(1)}, f32...) custom-call(bf16[544,768]{1,0:T(8,128)(2,1)S(1)} %convolution_convert_fusion.value_ref.value_raw_ref, ...), custom_call_target="tpu_custom_call" | custom-call | flops 157286400 | bytes 5523456 | tf_op jit(solution)/shard_map/conv/pallas_call | solution.py:939
  69.9 4.7 %collective-permute-done.6.refs_1_ = f32[72,768]{1,0:T(8,128)} collective-permute-done((f32[72,768]{1,0:T(8,128)}, f32[72,768]{1,0:T(8,128)}, u32[]{:S(2)}, u32[]{:S(2)}) %collective-permute-start.6) | collective-permute-done | bytes 221216 | tf_op jit(solution)/shard_map/ppermute | solution.py:78
  75.4 4.9 %collective-permute-done.8.refs_3_ = f32[72,768]{1,0:T(8,128)} collective-permute-done((f32[72,768]{1,0:T(8,128)}, f32[72,768]{1,0:T(8,128)}, u32[]{:S(2)}, u32[]{:S(2)}) %collective-permute-start.8) | collective-permute-done | bytes 221216 | tf_op jit(solution)/shard_map/ppermute | solution.py:78
  91.3 2.9 %mixed_grad.1 = (f32[512,768]{1,0:T(8,128)S(1)}, bf16[512,1536]{1,0:T(8,128)(2,1)S(1)}) custom-call(bf16[4,512,384]{2,1,0:T(8,128)(2,1)} %all-to-all-done.parts_ref, bf16[768,1536]{1,0:T(8,128)(2,1)S(1)} %copy-done.11), custom_call_target="tpu_custom_call" | custom-call | flops 1207959552 | bytes 7077888 | tf_op jit(solution)/shard_map/mixed_grad/pallas_call | solution.py:939
  103.3 3.8 %gate.1 = (bf16[512,768]{1,0:T(8,128)(2,1)S(1)}, bf16[512,768]{1,0:T(8,128)(2,1)S(1)}, f32[512,768]{1,0:T(8,128)S(1)}, f32[8,768]{1,0:T(8,128)S(1)}, f32[136,768]{1,0:T(8,128)S(1)}, /*index=5*/f32[8,512]{1,0:T(8,128)S(1)}) custom-call(f32[8,512]{1,0:T(8,128)S(1)} %get-tuple-element.87.refs_0_, f32[8,512]{1,0:T(8,128)S(1)} %collective-permute-done.10.refs_1_, ...), custom_call_target="tpu_custom_call" | custom-call | flops 235929600 | bytes 9487872 | tf_op jit(solution)/shard_map/gate/pallas_call | solution.py:939
  107.1 2.7 collective-permute-start.13
  109.9 2.9 %out.1.refs_0_ = bf16[4,512,384]{2,1,0:T(8,128)(2,1)} custom-call(f32[136,768]{1,0:T(8,128)S(1)} %get-tuple-element.89.loose_ref.own_ref, bf16[512,768]{1,0:T(8,128)(2,1)S(1)} %get-tuple-element.90.mixed_ref, bf16[768,1536]{1,0:T(8,128)(2,1)S(1)} %copy-done.12), custom_call_target="tpu_custom_call" | custom-call | flops 1207959552 | bytes 4718592 | tf_op jit(solution)/shard_map/out/pallas_call | solution.py:939
  114.7 6.6 %early.1 = (bf16[4,384,768]{2,1,0:T(8,128)(2,1)S(1)}, bf16[4,384,768]{2,1,0:T(8,128)(2,1)}, f32[1,1536]{1,0:T(1,128)S(1)}) custom-call(f32[72,768]{1,0:T(8,128)S(1)} %after_pair.1.loose_ref.refs_0_, s32[1]{0:T(128)} %bitcast.core_ref, bf16[544,1536]{1,0:T(8,128)(2,1)S(1)} %copy-done.22, bf16[512,768]{1,0:T(8,128)(2,1)S(1)} %get-tuple-element.91.gate_ref.gate_grad_ref, ...), custom_call_target="tpu_custom_call" | custom-call | flops 2415919104 | bytes 11900932 | tf_op jit(solution)/shard_map/early/pallas_call | solution.py:939
  123.3 4.4 %all-to-all-start.1 = ((bf16[4,512,384]{2,1,0:T(8,128)(2,1)}), bf16[4,512,384]{2,1,0:T(8,128)(2,1)}, u32[]{:S(2)}, u32[]{:S(2)}) async-start(bf16[4,512,384]{2,1,0:T(8,128)(2,1)} %out.1.refs_0_), calls=%async_computation.1 | async-start | bytes 3145728 | tf_op jit(solution)/shard_map/all_to_all | solution.py:74
  130.4 4.1 %collective-permute-done.15.refs_1_ = f32[72,768]{1,0:T(8,128)S(1)} collective-permute-done((f32[72,768]{1,0:T(8,128)}, f32[72,768]{1,0:T(8,128)S(1)}, u32[]{:S(2)}, u32[]{:S(2)}) %collective-permute-start.15) | collective-permute-done | bytes 221216 | tf_op jit(solution)/shard_map/ppermute | solution.py:78
  134.5 4.8 %collective-permute-done.17.refs_3_ = f32[72,768]{1,0:T(8,128)S(1)} collective-permute-done((f32[72,768]{1,0:T(8,128)}, f32[72,768]{1,0:T(8,128)S(1)}, u32[]{:S(2)}, u32[]{:S(2)}) %collective-permute-start.17) | collective-permute-done | bytes 221216 | tf_op jit(solution)/shard_map/ppermute | solution.py:78
  147.6 5.6 %back.1 = (f32[512,768]{1,0:T(8,128)S(1)}, f32[512,256]{1,0:T(8,128)S(1)}) custom-call(f32[2,192,768]{2,1,0:T(8,128)S(1)} %get-tuple-element.95.early_ref.first_ref, f32[128,768]{1,0:T(8,128)S(1)} %after_enter.1.state_in_ref, f32[512,768]{1,0:T(8,128)S(1)} %copy-done.32, f32[512,12]{1,0:T(8,128)S(1)} %get-tuple-element.85.e_ref.refs_9_, ...), custom_call_target="tpu_custom_call" | custom-call | flops 786432000 | bytes 8858624 | tf_op jit(solution)/shard_map/back/pallas_call | solution.py:939
  155.6 3.3 %collective-permute-done.21.after_ref = f32[8,1024]{1,0:T(8,128)S(1)} collective-permute-done((f32[8,1024]{1,0:T(8,128)S(1)}, f32[8,1024]{1,0:T(8,128)S(1)}, u32[]{:S(2)}, u32[]{:S(2)}) %collective-permute-start.21) | collective-permute-done | bytes 32800 | tf_op jit(solution)/shard_map/ppermute | solution.py:46
  158.9 3.7 %conv_back.1 = (bf16[512,768]{1,0:T(8,128)(2,1)S(1)}, bf16[512,256]{1,0:T(8,128)(2,1)S(1)}, f32[8,768]{1,0:T(8,128)S(1)}, f32[8,256]{1,0:T(8,128)S(1)}, f32[8,512]{1,0:T(8,128)S(1)}) custom-call(f32[512,768]{1,0:T(8,128)S(1)} %get-tuple-element.104.value_ref, f32[512,256]{1,0:T(8,128)S(1)} %get-tuple-element.105.map_ref, ...), custom_call_target="tpu_custom_call" | custom-call | flops 39321600 | bytes 4366336 | tf_op jit(solution)/shard_map/conv_back/pallas_call | solution.py:939
  164.8 5.4 %normed.1.loose_ref = bf16[4,528,384]{2,1,0:T(8,128)(2,1)} custom-call(f32[192,768]{1,0:T(8,128)S(1)} %get-tuple-element.108.late_ref.first_ref, bf16[512,768]{1,0:T(8,128)(2,1)S(1)} %copy-done.46, bf16[512,768]{1,0:T(8,128)(2,1)S(1)} %get-tuple-element.109.value_grad_ref.value_ref, bf16[512,256]{1,0:T(8,128)(2,1)S(1)} %get-tuple-element.110.state_grad_ref.state_ref, ...), custom_call_target="tpu_custom_call" | custom-call | flops 2415919104 | bytes 8978432 | tf_op jit(solution)/shard_map/normed/pallas_call | solution.py:939
  173.8 5.2 %late.1 = (bf16[4,272,768]{2,1,0:T(8,128)(2,1)S(1)}, bf16[4,272,768]{2,1,0:T(8,128)(2,1)}) custom-call(bf16[192,768]{1,0:T(8,128)(2,1)S(1)} %get-tuple-element.115.early_ref, s32[1]{0:T(128)} %bitcast.core_ref, bf16[544,1536]{1,0:T(8,128)(2,1)S(1)} %copy-done.22, bf16[512,768]{1,0:T(8,128)(2,1)S(1)} %get-tuple-element.109.value_grad_ref.value_ref, ...), custom_call_target="tpu_custom_call" | custom-call | flops 1811939328 | bytes 9320452 | tf_op jit(solution)/shard_map/late/pallas_call | solution.py:939
  180.5 4.5 %all-to-all-start.2 = ((bf16[4,528,384]{2,1,0:T(8,128)(2,1)}), bf16[4,528,384]{2,1,0:T(8,128)(2,1)S(1)}, u32[]{:S(2)}, u32[]{:S(2)}) async-start(bf16[4,528,384]{2,1,0:T(8,128)(2,1)} %normed.1.loose_ref), calls=%async_computation.2 | async-start | bytes 3244032 | tf_op jit(solution)/shard_map/all_to_all | solution.py:74
  185.6 2.6 late_half.1
  198.7 3.8 %collective-permute-done.33.refs_1_ = bf16[272,768]{1,0:T(8,128)(2,1)S(1)} collective-permute-done((bf16[272,768]{1,0:T(8,128)(2,1)}, bf16[272,768]{1,0:T(8,128)(2,1)S(1)}, u32[]{:S(2)}, u32[]{:S(2)}) %collective-permute-start.33) | collective-permute-done | bytes 417824 | tf_op jit(solution)/shard_map/ppermute | solution.py:78
  203.5 8.8 %collective-permute-done.35.refs_3_ = bf16[272,768]{1,0:T(8,128)(2,1)} collective-permute-done((bf16[272,768]{1,0:T(8,128)(2,1)}, bf16[272,768]{1,0:T(8,128)(2,1)}, u32[]{:S(2)}, u32[]{:S(2)}) %collective-permute-start.35) | collective-permute-done | bytes 417824 | tf_op jit(solution)/shard_map/ppermute | solution.py:78
  215.5 10.7 %collective-permute-done.36.arrived_ref = bf16[80,768]{1,0:T(8,128)(2,1)S(1)} collective-permute-done((bf16[80,768]{1,0:T(8,128)(2,1)S(1)}, bf16[80,768]{1,0:T(8,128)(2,1)S(1)}, u32[]{:S(2)}, u32[]{:S(2)}) %collective-permute-start.36) | collective-permute-done | bytes 122912 | tf_op jit(solution)/shard_map/ppermute | solution.py:89
  226.9 7.2 %collective-permute-done.37.arrived_ref = bf16[80,768]{1,0:T(8,128)(2,1)S(1)} collective-permute-done((bf16[80,768]{1,0:T(8,128)(2,1)S(1)}, bf16[80,768]{1,0:T(8,128)(2,1)S(1)}, u32[]{:S(2)}, u32[]{:S(2)}) %collective-permute-start.37) | collective-permute-done | bytes 122912 | tf_op jit(solution)/shard_map/ppermute | solution.py:89
  238.1 5.0 %collective-permute-done.47 = bf16[192,768]{1,0:T(8,128)(2,1)S(1)} collective-permute-done((bf16[192,768]{1,0:T(8,128)(2,1)S(1)}, bf16[192,768]{1,0:T(8,128)(2,1)S(1)}, u32[]{:S(2)}, u32[]{:S(2)}) %collective-permute-start.47) | collective-permute-done | bytes 294944 | tf_op jit(solution)/shard_map/ppermute | solution.py:78
  250.9 3.4 %collective-permute-done.40.refs_2_ = bf16[2,80,768]{2,1,0:T(8,128)(2,1)} collective-permute-done((bf16[2,80,768]{2,1,0:T(8,128)(2,1)S(1)}, bf16[2,80,768]{2,1,0:T(8,128)(2,1)}, u32[]{:S(2)}, u32[]{:S(2)}) %collective-permute-start.40) | collective-permute-done | bytes 245792 | tf_op jit(solution)/shard_map/ppermute | solution.py:78
  261.4 5.7 %early_out.1 = (f32[1536,768]{1,0:T(8,128)}, f32[768,1536]{1,0:T(8,128)}) custom-call(s32[1]{0:T(128)} %bitcast.core_ref, s32[1]{0:T(128)} %bitcast.5.chip_ref, bf16[2,192,768]{2,1,0:T(8,128)(2,1)S(1)} %copy-done.2, bf16[2,192,768]{2,1,0:T(8,128)(2,1)} %collective-permute-done.26.refs_1_, bf16[2,192,768]{2,1,0:T(8,128)(2,1)} %collective-permute-done.27.refs_2_, ...), custom_call_target="tpu_custom_call" | custom-call | flops 4718592 | bytes 14155784 | tf_op jit(solution)/shard_map/early_out/pallas_call | solution.py:939
  269.5 3.0 %shared_out.1 = (f32[1536,256]{1,0:T(8,128)}, f32[4,768]{1,0:T(4,128)}, f32[768]{0:T(1024)}, f32[4,256]{1,0:T(4,128)}, f32[256]{0:T(256)}, /*index=5*/f32[12]{0:T(128)}, f32[768]{0:T(1024)}, f32[384]{0:T(512)}) custom-call(s32[1]{0:T(128)} %bitcast.core_ref, s32[1]{0:T(128)} %bitcast.5.chip_ref, s32[1]{0:T(128)} %bitcast.1.head_ref, ...), custom_call_target="tpu_custom_call" | custom-call | flops 786432 | bytes 2581052 | tf_op jit(solution)/shard_map/shared_out/pallas_call | solution.py:939
  (321 shorter events, 107.8 us)
Async XLA Ops:
  8.4 21.3 %collective-permute-start.1 = (bf16[544,384]{1,0:T(8,128)(2,1)S(1)}, bf16[544,384]{1,0:T(8,128)(2,1)S(1)}, u32[]{:S(2)}, u32[]{:S(2)}) collective-permute-start(bf16[544,384]{1,0:T(8,128)(2,1)S(1)} %pad_maximum_fusion.2.refs_0_.refs_4_), channel_id=1, source_target_pairs={{0,2},{1,3},{2,0},{3,1},{4,6},{5,7},{6,4},{7,5},{8,10},{9,11},{10,... | collective-permute-start | bytes 1253384 | tf_op jit(solution)/shard_map/ppermute | solution.py:55
  10.8 20.3 %collective-permute-start.3 = (bf16[544,384]{1,0:T(8,128)(2,1)S(1)}, bf16[544,384]{1,0:T(8,128)(2,1)S(1)}, u32[]{:S(2)}, u32[]{:S(2)}) collective-permute-start(bf16[544,384]{1,0:T(8,128)(2,1)S(1)} %pad_maximum_fusion.2.refs_0_.refs_4_), channel_id=1, source_target_pairs={{0,1},{1,2},{2,3},{4,5},{5,6},{6,7},{8,9},{9,10},{10,11},{12,13},{... | collective-permute-start | bytes 1253384 | tf_op jit(solution)/shard_map/ppermute | solution.py:67
  14.0 21.1 %collective-permute-start.4 = (bf16[544,384]{1,0:T(8,128)(2,1)S(1)}, bf16[544,384]{1,0:T(8,128)(2,1)S(1)}, u32[]{:S(2)}, u32[]{:S(2)}) collective-permute-start(bf16[544,384]{1,0:T(8,128)(2,1)S(1)} %pad_maximum_fusion.2.refs_0_.refs_4_), channel_id=1, source_target_pairs={{1,0},{2,1},{3,2},{5,4},{6,5},{7,6},{9,8},{10,9},{11,10},{13,12},{... | collective-permute-start | bytes 1253384 | tf_op jit(solution)/shard_map/ppermute | solution.py:68
  29.7 13.8 %collective-permute-start.2 = (bf16[544,384]{1,0:T(8,128)(2,1)S(1)}, bf16[544,384]{1,0:T(8,128)(2,1)S(1)}, u32[]{:S(2)}, u32[]{:S(2)}) collective-permute-start(bf16[544,384]{1,0:T(8,128)(2,1)S(1)} %collective-permute-done.1.refs_2_.refs_6_), channel_id=1, source_target_pairs={{2,3},{1,0},{6,7},{5,4},{10,11},{9,8},{14,15},{13,12},{18,19},{17,... | collective-permute-start | bytes 1253384 | tf_op jit(solution)/shard_map/ppermute | solution.py:69
  48.4 41.3 %all-to-all-start = ((bf16[4,512,384]{2,1,0:T(8,128)(2,1)}), bf16[4,512,384]{2,1,0:T(8,128)(2,1)}, u32[]{:S(2)}, u32[]{:S(2)}) async-start(bf16[4,512,384]{2,1,0:T(8,128)(2,1)} %copies.1), calls=%async_computation | async-start | bytes 3145728 | tf_op jit(solution)/shard_map/all_to_all | solution.py:74
  68.7 11.5 %collective-permute-start.8 = (f32[72,768]{1,0:T(8,128)}, f32[72,768]{1,0:T(8,128)}, u32[]{:S(2)}, u32[]{:S(2)}) collective-permute-start(f32[72,768]{1,0:T(8,128)} %before_pair.1.refs_0_), channel_id=1, source_target_pairs={{0,24},{8,16},{16,8},{24,0},{1,25},{9,17},{17,9},{25,1},{2,26},{10... | collective-permute-start | bytes 663560 | tf_op jit(solution)/shard_map/ppermute | solution.py:78
  123.3 17.0 %collective-permute-start.14 = (bf16[4,384,768]{2,1,0:T(8,128)(2,1)}, bf16[4,384,768]{2,1,0:T(8,128)(2,1)}, u32[]{:S(2)}, u32[]{:S(2)}) collective-permute-start(bf16[4,384,768]{2,1,0:T(8,128)(2,1)} %get-tuple-element.94.refs_4_), channel_id=1, source_target_pairs={{0,4},{4,0},{1,5},{5,1},{2,6},{6,2},{3,7},{7,3},{8,12},{12,8},{9,1... | collective-permute-start | bytes 7077896 | tf_op jit(solution)/shard_map/ppermute | solution.py:50
  123.3 57.2 %all-to-all-start.1 = ((bf16[4,512,384]{2,1,0:T(8,128)(2,1)}), bf16[4,512,384]{2,1,0:T(8,128)(2,1)}, u32[]{:S(2)}, u32[]{:S(2)}) async-start(bf16[4,512,384]{2,1,0:T(8,128)(2,1)} %out.1.refs_0_), calls=%async_computation.1 | async-start | bytes 3145728 | tf_op jit(solution)/shard_map/all_to_all | solution.py:74
  128.6 10.7 %collective-permute-start.17 = (f32[72,768]{1,0:T(8,128)}, f32[72,768]{1,0:T(8,128)S(1)}, u32[]{:S(2)}, u32[]{:S(2)}) collective-permute-start(f32[72,768]{1,0:T(8,128)} %copy-done.41), channel_id=1, source_target_pairs={{0,24},{8,16},{16,8},{24,0},{1,25},{9,17},{17,9},{25,1},{2,26},{10... | collective-permute-start | bytes 663560 | tf_op jit(solution)/shard_map/ppermute | solution.py:78
  142.7 19.9 %collective-permute-start.18 = (bf16[2,192,768]{2,1,0:T(8,128)(2,1)S(1)}, bf16[2,192,768]{2,1,0:T(8,128)(2,1)S(1)}, u32[]{:S(2)}, u32[]{:S(2)}) collective-permute-start(bf16[2,192,768]{2,1,0:T(8,128)(2,1)S(1)} %get-tuple-element.96), channel_id=1, source_target_pairs={{0,8},{8,0},{16,24},{24,16},{1,9},{9,1},{17,25},{25,17},{2,10},{10... | collective-permute-start | bytes 1769480 | tf_op jit(solution)/shard_map/ppermute | solution.py:78
  143.4 19.3 %collective-permute-start.19 = (bf16[2,192,768]{2,1,0:T(8,128)(2,1)S(1)}, bf16[2,192,768]{2,1,0:T(8,128)(2,1)S(1)}, u32[]{:S(2)}, u32[]{:S(2)}) collective-permute-start(bf16[2,192,768]{2,1,0:T(8,128)(2,1)S(1)} %get-tuple-element.98), channel_id=1, source_target_pairs={{0,16},{8,24},{16,0},{24,8},{1,17},{9,25},{17,1},{25,9},{2,18},{10... | collective-permute-start | bytes 1769480 | tf_op jit(solution)/shard_map/ppermute | solution.py:78
  180.5 76.0 %all-to-all-start.2 = ((bf16[4,528,384]{2,1,0:T(8,128)(2,1)}), bf16[4,528,384]{2,1,0:T(8,128)(2,1)S(1)}, u32[]{:S(2)}, u32[]{:S(2)}) async-start(bf16[4,528,384]{2,1,0:T(8,128)(2,1)} %normed.1.loose_ref), calls=%async_computation.2 | async-start | bytes 3244032 | tf_op jit(solution)/shard_map/all_to_all | solution.py:74
  185.1 11.4 %collective-permute-start.29 = (bf16[192,768]{1,0:T(8,128)(2,1)}, bf16[192,768]{1,0:T(8,128)(2,1)}, u32[]{:S(2)}, u32[]{:S(2)}) collective-permute-start(bf16[192,768]{1,0:T(8,128)(2,1)} %copy-done.55), channel_id=1, source_target_pairs={{0,8},{8,0},{16,24},{24,16},{1,9},{9,1},{17,25},{25,17},{2,10},{10... | collective-permute-start | bytes 884744 | tf_op jit(solution)/shard_map/ppermute | solution.py:78
  189.1 13.4 %collective-permute-start.33 = (bf16[272,768]{1,0:T(8,128)(2,1)}, bf16[272,768]{1,0:T(8,128)(2,1)S(1)}, u32[]{:S(2)}, u32[]{:S(2)}) collective-permute-start(bf16[272,768]{1,0:T(8,128)(2,1)} %get-tuple-element.126), channel_id=1, source_target_pairs={{0,8},{8,0},{16,24},{24,16},{1,9},{9,1},{17,25},{25,17},{2,10},{10... | collective-permute-start | bytes 1253384 | tf_op jit(solution)/shard_map/ppermute | solution.py:78
  190.1 13.5 %collective-permute-start.34 = (bf16[272,768]{1,0:T(8,128)(2,1)}, bf16[272,768]{1,0:T(8,128)(2,1)}, u32[]{:S(2)}, u32[]{:S(2)}) collective-permute-start(bf16[272,768]{1,0:T(8,128)(2,1)} %get-tuple-element.127), channel_id=1, source_target_pairs={{0,16},{8,24},{16,0},{24,8},{1,17},{9,25},{17,1},{25,9},{2,18},{10... | collective-permute-start | bytes 1253384 | tf_op jit(solution)/shard_map/ppermute | solution.py:78
  191.5 20.8 %collective-permute-start.35 = (bf16[272,768]{1,0:T(8,128)(2,1)}, bf16[272,768]{1,0:T(8,128)(2,1)}, u32[]{:S(2)}, u32[]{:S(2)}) collective-permute-start(bf16[272,768]{1,0:T(8,128)(2,1)} %get-tuple-element.128), channel_id=1, source_target_pairs={{0,24},{8,16},{16,8},{24,0},{1,25},{9,17},{17,9},{25,1},{2,26},{10... | collective-permute-start | bytes 1253384 | tf_op jit(solution)/shard_map/ppermute | solution.py:78
  194.4 31.8 %collective-permute-start.26 = (bf16[2,192,768]{2,1,0:T(8,128)(2,1)}, bf16[2,192,768]{2,1,0:T(8,128)(2,1)}, u32[]{:S(2)}, u32[]{:S(2)}) collective-permute-start(bf16[2,192,768]{2,1,0:T(8,128)(2,1)} %tie.2.refs_0_), channel_id=1, source_target_pairs={{0,4},{4,0},{1,5},{5,1},{2,6},{6,2},{3,7},{7,3},{8,12},{12,8},{9,1... | collective-permute-start | bytes 1769480 | tf_op jit(solution)/shard_map/ppermute | solution.py:50
  196.4 29.9 %collective-permute-start.27 = (bf16[2,192,768]{2,1,0:T(8,128)(2,1)}, bf16[2,192,768]{2,1,0:T(8,128)(2,1)}, u32[]{:S(2)}, u32[]{:S(2)}) collective-permute-start(bf16[2,192,768]{2,1,0:T(8,128)(2,1)} %tie.2.refs_0_), channel_id=1, source_target_pairs={{0,8},{8,0},{16,24},{24,16},{1,9},{9,1},{17,25},{25,17},{2,10},{10... | collective-permute-start | bytes 1769480 | tf_op jit(solution)/shard_map/ppermute | solution.py:78
  202.5 34.8 %collective-permute-start.31 = (bf16[2,192,768]{2,1,0:T(8,128)(2,1)}, bf16[2,192,768]{2,1,0:T(8,128)(2,1)}, u32[]{:S(2)}, u32[]{:S(2)}) collective-permute-start(bf16[2,192,768]{2,1,0:T(8,128)(2,1)} %tie.3.refs_4_), channel_id=1, source_target_pairs={{0,16},{8,24},{16,0},{24,8},{1,17},{9,25},{17,1},{25,9},{2,18},{10... | collective-permute-start | bytes 1769480 | tf_op jit(solution)/shard_map/ppermute | solution.py:78
  213.7 12.5 %collective-permute-start.36 = (bf16[80,768]{1,0:T(8,128)(2,1)S(1)}, bf16[80,768]{1,0:T(8,128)(2,1)S(1)}, u32[]{:S(2)}, u32[]{:S(2)}) collective-permute-start(bf16[80,768]{1,0:T(8,128)(2,1)S(1)} %convert_element_type.29), channel_id=1, source_target_pairs={{0,1},{1,0},{2,3},{3,2},{4,5},{5,4},{6,7},{7,6},{8,9},{9,8},{10,11... | collective-permute-start | bytes 368648 | tf_op jit(solution)/shard_map/ppermute | solution.py:89
  214.9 20.8 %collective-permute-start.43 = (bf16[192,768]{1,0:T(8,128)(2,1)S(1)}, bf16[192,768]{1,0:T(8,128)(2,1)S(1)}, u32[]{:S(2)}, u32[]{:S(2)}) collective-permute-start(bf16[192,768]{1,0:T(8,128)(2,1)S(1)} %get-tuple-element.134), channel_id=1, source_target_pairs={{0,8},{8,0},{16,24},{24,16},{1,9},{9,1},{17,25},{25,17},{2,10},{10... | collective-permute-start | bytes 884744 | tf_op jit(solution)/shard_map/ppermute | solution.py:78
  226.2 10.3 %collective-permute-start.45 = (bf16[192,768]{1,0:T(8,128)(2,1)S(1)}, bf16[192,768]{1,0:T(8,128)(2,1)S(1)}, u32[]{:S(2)}, u32[]{:S(2)}) collective-permute-start(bf16[192,768]{1,0:T(8,128)(2,1)S(1)} %get-tuple-element.134), channel_id=1, source_target_pairs={{0,16},{8,24},{16,0},{24,8},{1,17},{9,25},{17,1},{25,9},{2,18},{10... | collective-permute-start | bytes 884744 | tf_op jit(solution)/shard_map/ppermute | solution.py:78
  226.3 11.0 %collective-permute-start.42 = (bf16[1,192,768]{2,1,0:T(8,128)(2,1)S(1)}, bf16[1,192,768]{2,1,0:T(8,128)(2,1)S(1)}, u32[]{:S(2)}, u32[]{:S(2)}) collective-permute-start(bf16[1,192,768]{2,1,0:T(8,128)(2,1)S(1)} %bitcast.36), channel_id=1, source_target_pairs={{0,4},{4,0},{1,5},{5,1},{2,6},{6,2},{3,7},{7,3},{8,12},{12,8},{9,1... | collective-permute-start | bytes 884744 | tf_op jit(solution)/shard_map/ppermute | solution.py:50
  234.0 9.0 %collective-permute-start.47 = (bf16[192,768]{1,0:T(8,128)(2,1)S(1)}, bf16[192,768]{1,0:T(8,128)(2,1)S(1)}, u32[]{:S(2)}, u32[]{:S(2)}) collective-permute-start(bf16[192,768]{1,0:T(8,128)(2,1)S(1)} %get-tuple-element.134), channel_id=1, source_target_pairs={{0,24},{8,16},{16,8},{24,0},{1,25},{9,17},{17,9},{25,1},{2,26},{10... | collective-permute-start | bytes 884744 | tf_op jit(solution)/shard_map/ppermute | solution.py:78
  235.7 11.3 %collective-permute-start.44 = (bf16[1,192,768]{2,1,0:T(8,128)(2,1)S(1)}, bf16[1,192,768]{2,1,0:T(8,128)(2,1)S(1)}, u32[]{:S(2)}, u32[]{:S(2)}) collective-permute-start(bf16[1,192,768]{2,1,0:T(8,128)(2,1)S(1)} %bitcast.38), channel_id=1, source_target_pairs={{0,4},{4,0},{1,5},{5,1},{2,6},{6,2},{3,7},{7,3},{8,12},{12,8},{9,1... | collective-permute-start | bytes 884744 | tf_op jit(solution)/shard_map/ppermute | solution.py:50
  236.5 10.6 %collective-permute-start.46 = (bf16[1,192,768]{2,1,0:T(8,128)(2,1)S(1)}, bf16[1,192,768]{2,1,0:T(8,128)(2,1)S(1)}, u32[]{:S(2)}, u32[]{:S(2)}) collective-permute-start(bf16[1,192,768]{2,1,0:T(8,128)(2,1)S(1)} %bitcast.40), channel_id=1, source_target_pairs={{0,4},{4,0},{1,5},{5,1},{2,6},{6,2},{3,7},{7,3},{8,12},{12,8},{9,1... | collective-permute-start | bytes 884744 | tf_op jit(solution)/shard_map/ppermute | solution.py:50
  237.3 9.2 %collective-permute-start.38 = (bf16[80,768]{1,0:T(8,128)(2,1)S(1)}, bf16[80,768]{1,0:T(8,128)(2,1)S(1)}, u32[]{:S(2)}, u32[]{:S(2)}) collective-permute-start(bf16[80,768]{1,0:T(8,128)(2,1)S(1)} %get-tuple-element.132), channel_id=1, source_target_pairs={{0,16},{8,24},{16,0},{24,8},{1,17},{9,25},{17,1},{25,9},{2,18},{10... | collective-permute-start | bytes 368648 | tf_op jit(solution)/shard_map/ppermute | solution.py:78
  237.4 24.0 %collective-permute-start.30 = (bf16[2,192,768]{2,1,0:T(8,128)(2,1)S(1)}, bf16[2,192,768]{2,1,0:T(8,128)(2,1)}, u32[]{:S(2)}, u32[]{:S(2)}) collective-permute-start(bf16[2,192,768]{2,1,0:T(8,128)(2,1)S(1)} %copy-done.3), channel_id=1, source_target_pairs={{0,4},{4,0},{1,5},{5,1},{2,6},{6,2},{3,7},{7,3},{8,12},{12,8},{9,1... | collective-permute-start | bytes 1769480 | tf_op jit(solution)/shard_map/ppermute | solution.py:50
  243.1 18.3 %collective-permute-start.28 = (bf16[2,192,768]{2,1,0:T(8,128)(2,1)}, bf16[2,192,768]{2,1,0:T(8,128)(2,1)}, u32[]{:S(2)}, u32[]{:S(2)}) collective-permute-start(bf16[2,192,768]{2,1,0:T(8,128)(2,1)} %collective-permute-done.27.refs_2_), channel_id=1, source_target_pairs={{0,4},{4,0},{1,5},{5,1},{2,6},{6,2},{3,7},{7,3},{8,12},{12,8},{9,1... | collective-permute-start | bytes 1769480 | tf_op jit(solution)/shard_map/ppermute | solution.py:50
  246.5 14.9 %collective-permute-start.32 = (bf16[2,192,768]{2,1,0:T(8,128)(2,1)}, bf16[2,192,768]{2,1,0:T(8,128)(2,1)}, u32[]{:S(2)}, u32[]{:S(2)}) collective-permute-start(bf16[2,192,768]{2,1,0:T(8,128)(2,1)} %collective-permute-done.31.refs_6_), channel_id=1, source_target_pairs={{0,4},{4,0},{1,5},{5,1},{2,6},{6,2},{3,7},{7,3},{8,12},{12,8},{9,1... | collective-permute-start | bytes 1769480 | tf_op jit(solution)/shard_map/ppermute | solution.py:50
  250.2 16.9 %collective-permute-start.39 = (bf16[2,80,768]{2,1,0:T(8,128)(2,1)S(1)}, bf16[2,80,768]{2,1,0:T(8,128)(2,1)}, u32[]{:S(2)}, u32[]{:S(2)}) collective-permute-start(bf16[2,80,768]{2,1,0:T(8,128)(2,1)S(1)} %pad_maximum_fusion.3.refs_0_), channel_id=1, source_target_pairs={{0,4},{4,0},{1,5},{5,1},{2,6},{6,2},{3,7},{7,3},{8,12},{12,8},{9,1... | collective-permute-start | bytes 737288 | tf_op jit(solution)/shard_map/ppermute | solution.py:50
  254.4 12.8 %collective-permute-start.41 = (bf16[2,80,768]{2,1,0:T(8,128)(2,1)}, bf16[2,80,768]{2,1,0:T(8,128)(2,1)}, u32[]{:S(2)}, u32[]{:S(2)}) collective-permute-start(bf16[2,80,768]{2,1,0:T(8,128)(2,1)} %collective-permute-done.40.refs_2_), channel_id=1, source_target_pairs={{0,4},{4,0},{1,5},{5,1},{2,6},{6,2},{3,7},{7,3},{8,12},{12,8},{9,1... | collective-permute-start | bytes 737288 | tf_op jit(solution)/shard_map/ppermute | solution.py:50
  (117 other events, 768.5 us)

commit v2 on v1

--- a/solution.py
+++ b/solution.py
@@ -107,9 +107,10 @@
         [core, (WHOLE, total), (WHOLE, partner)] + [(LOOSE, value) for value in meanwhile],
         [(WHOLE, (half + 8, channels), F32)],
     )[0]
+    found = cross_all(pair)
     prefix = run(
         functools.partial(prefix_kernel, backward, chips), name + "_prefix", chips * pair.size,
-        [chip] + [(WHOLE, value) for value in cross_all(pair)]
+        [chip] + [(WHOLE, value) for value in found]
         + [(LOOSE, value) for value in later(pair)],
         [(WHOLE, (half, channels), F32)],
     )[0]
@@ -117,7 +118,7 @@
         functools.partial(enter_kernel, backward), name + "_enter", total.size,
         [core, (WHOLE, partner), (WHOLE, prefix), (WHOLE, beside(prefix))],
         [(WHOLE, (NSTATE, channels), F32)],
-    )[0], prefix
+    )[0], prefix, found[1]
 
 
 def sum_pieces(chip, kept, given, name, square, cut, paired, before_half=()):
@@ -349,14 +350,11 @@
         pl.when(mine == me)(functools.partial(write, me))
 
 
-def copies_kernel(loose_ref, own_ref, out_ref):
-    for i in range(out_ref.shape[0]):
-        out_ref[i] = own_ref[...]
-
-
 def norm_kernel(size, head_ref, passed_ref, *refs):
     parts, gains = refs[:size], refs[size : 2 * size]
-    passed_gain_ref, normed_ref, scale_ref, gain_ref = refs[2 * size :]
+    passed_gain_ref, own_ref, normed_ref, scale_ref, gain_ref, copy_ref = refs[2 * size :]
+    for i in range(size):
+        copy_ref[i] = own_ref[...]
     width = parts[0].shape[1]
     mine = head_ref[0]
 
@@ -589,7 +587,7 @@
 
 
 def normed_kernel(
-    chunks, late_ref, gate_grad_ref, value_grad_ref, state_grad_ref, gate_weight_ref, value_weight_ref,
+    chunks, early_ref, out_ref_in, gate_grad_ref, value_grad_ref, state_grad_ref, gate_weight_ref, value_weight_ref,
     state_weight_ref, cross_ref, out_ref
 ):
     value = (
@@ -856,7 +854,7 @@
         copy.wait()
 
 
-def shared_out_kernel(chips, groups, size, core_ref, chip_ref, head_ref, loose_ref, *refs):
+def shared_out_kernel(chips, groups, size, core_ref, chip_ref, head_ref, *refs):
     (
         state_ref, value_kernel_ref, value_bias_ref, state_kernel_ref, state_bias_ref, skip_ref,
         gated_ref, gain_ref, buffer, sems, own_ref, shared_ref,
@@ -908,6 +906,7 @@
 BLOCKED = "blocked"
 LANES = "lanes"
 LEADING = "leading"
+FAR = "far"
 LOOSE = "loose"
 
 
@@ -921,6 +920,8 @@
             return pl.BlockSpec(memory_space=pltpu.SMEM)
         if kind == LOOSE:
             return pl.BlockSpec(memory_space=pl.ANY)
+        if kind == FAR:
+            return pl.BlockSpec(memory_space=pltpu.HBM)
         if isinstance(kind, tuple):
             return pl.BlockSpec(*kind)
         if steps is None:
@@ -991,20 +992,22 @@
 
     half = rows // 2
     gain_rows = ((MARGIN - HALO, own_width), lambda i: ((HALO + count) // (MARGIN - HALO), 0))
-    normed, scale_in, gain_full = run(
+    normed, scale_in, gain_full, copies = run(
         functools.partial(norm_kernel, head_size), "norm", count * width * 10,
         [head, (half, passed)] + [(half, part) for part in parts]
-        + [(gain_rows, part) for part in parts] + [(gain_rows, passed)],
-        [(half, (rows, width), BF16), (half, (rows, 128), F32), (WHOLE, (8, width), F32)],
+        + [(gain_rows, part) for part in parts] + [(gain_rows, passed), (count // 2, cotangent)],
+        [
+            (half, (rows, width), BF16),
+            (half, (rows, 128), F32),
+            (WHOLE, (8, width), F32),
+            (
+                ((head_size, count // 2, own_width), lambda i: (0, i, 0)),
+                (head_size, count, own_width), BF16,
+            ),
+        ],
         steps=2,
     )
-    cotangent_parts = deal(
-        run(
-            copies_kernel, "copies", 1, [(LOOSE, normed), (WHOLE, cotangent)],
-            [(WHOLE, (head_size, count, own_width), BF16)],
-        )[0],
-        "head",
-    )
+    cotangent_parts = deal(copies, "head")
     value_raw = dot(normed, value_weight).astype(BF16)
     state_raw = dot(normed, state_weight).astype(BF16)
     conv, weighted, value_slope, maps, map_slope, local_end = run(
@@ -1024,7 +1027,7 @@
         steps=chunks,
     )
     gate_pre = dot(normed, gate_weight)[HALO : HALO + count]
-    state_in, _ = entering(core, chip, local_end, False, (gate_pre,))
+    state_in, _, _ = entering(core, chip, local_end, False, (gate_pre,))
     mixed_grad, full_cotangent = run(
         mixed_grad_kernel, "mixed_grad", 2 * count * width * channels,
         [(WHOLE, cotangent_parts), (WHOLE, output_weight)],
@@ -1094,12 +1097,15 @@
         )
         return early_made[1:2]
 
-    grad_after, after_prefix = entering(core, chip, start_grad, True, (out_parts,), make_early)
+    grad_after, after_prefix, after_first = entering(
+        core, chip, start_grad, True, (out_parts,), make_early
+    )
     early_kept, early_given, early_gain = early_made
     early_state, half_mark = sum_pieces(
         chip, early_kept, early_given, "early", True, step, False, (after_prefix,)
     )
-    branch = jnp.sum(deal(out_parts, "head").astype(F32), axis=0)
+    out_arrived = deal(tie(out_parts, after_first), "head")
+    branch = jnp.sum(out_arrived.astype(F32), axis=0)
     block_out = (tokens.astype(F32) + branch).astype(BF16)
 
     value_grads, map_grads = run(
@@ -1141,7 +1147,7 @@
     normed_parts = run(
         functools.partial(normed_kernel, chunks), "normed", 4 * count * channels * width,
         [
-            (LOOSE, next_mark), (WHOLE, gate_grad), (WHOLE, value_raw_grad),
+            (LOOSE, next_mark), (LOOSE, out_arrived), (WHOLE, gate_grad), (WHOLE, value_raw_grad),
             (WHOLE, state_raw_grad), (own_width, gate_weight), (own_width, value_weight),
             (own_width, state_weight), (WHOLE, crossed),
         ],
@@ -1195,7 +1201,7 @@
     gate_weight_gradient, output_weight_gradient = unpack(
         early_out_kernel, "early_out",
         [(early_gate, (2, 1), late_mark), (early_out, (1, 2), late_mark)],
-        [(LOOSE, (width, channels), F32), (LOOSE, (channels, width), F32)], 4 * channels * width,
+        [(FAR, (width, channels), F32), (FAR, (channels, width), F32)], 4 * channels * width,
         [
             pltpu.VMEM((seq_size, step, channels), F32),
             pltpu.VMEM((seq_size, out_rows, width), F32),
@@ -1205,7 +1211,7 @@
     )
     value_weight_gradient = unpack(
         late_out_kernel, "late_out", [(late_piece, None)],
-        [(LOOSE, (width, channels), F32)], 2 * channels * width,
+        [(FAR, (width, channels), F32)], 2 * channels * width,
         [pltpu.VMEM((seq_size, step, channels), F32), sems],
     )[0]
     (
@@ -1214,7 +1220,7 @@
     ) = unpack(
         shared_out_kernel, "shared_out", [(shared_piece, (2, 1))],
         [
-            (LOOSE, (width, maps_width), F32),
+            (FAR, (width, maps_width), F32),
             (WHOLE, (KERNEL, channels), F32),
             (WHOLE, (channels,), F32),
             (WHOLE, (KERNEL, maps_width), F32),
@@ -1231,7 +1237,7 @@
             pltpu.VMEM((HALO, channels), F32),
         ],
         extra=(head_size,),
-        args=[head, (LOOSE, gate_weight_gradient)],
+        args=[head],
     )
     tokens_gradient = run(
         functools.partial(last_kernel, float(width)), "last", count * own_width * 20,

time: 274 us -> 287 us (1.047)
  local copies, waits for them, and re-layouts: 23.7 us -> 32.9 us
  starting transfers between devices: 64.9 us -> 72.6 us
  waiting for transfers between devices: 101 us -> 96.1 us
    unnamed x195, local copies, waits for them, and re-layouts: 22.1 us -> 31.3 us
    ppermute x2, waiting for transfers between devices: 17.8 us -> 12.1 us  [heads_sum(): arrived = lax.ppermute(low, 'head', [(i, i ^ bits) for i in range(size)])]
    ppermute x1, waiting for transfers between devices: 4.01 us -> 0.01 us  [line_parts(): three = lax.ppermute(value, axis, [(1, 0), (2, 1), (3, 2)])]
    ppermute x22, starting transfers between devices: 16.8 us -> 20.8 us  [cross(): lax.ppermute(value, 'chip', [(i, i ^ bits) for i in range(lax.axis_size('...]
    ppermute x16, starting transfers between devices: 15.2 us -> 18.8 us  [beside(): return lax.ppermute(value, 'core', [(0, 1), (1, 0)])]
    pallas_call x30 -> x29, Pallas kernels: 69.3 us -> 71.1 us  [run(): pl.pallas_call(kernel, out_shape=shapes, in_specs=[spec(kind, a.shape) fo...]
  transfers between devices with their start and end apart: 52 -> 52, of which waited for: 25 -> 25; matrix products, arithmetic and copies ran while one was open for 4% -> 4% of each run, Pallas kernels for 18% -> 15%
where the time goes in v2:
time: 287 us; the launch traced here: 286 us
  waiting for transfers between devices  96.1 us (33%)
  starting transfers between devices  72.6 us (25%)
  Pallas kernels  71.1 us (25%)
  local copies, waits for them, and re-layouts  32.9 us (11%)
  other arithmetic  6.06 us (2%)
  matrix products  5.03 us (2%)
    pallas_call x29, Pallas kernels, run(): pl.pallas_call(kernel, out_shape=shapes, in_specs=[spec(kind, a.shape) fo...  71.1 us
    ppermute x22, waiting for transfers between devices, cross(): lax.ppermute(value, 'chip', [(i, i ^ bits) for i in range(lax.axis_size('...  47.4 us
    unnamed x195, local copies, waits for them, and re-layouts  31.3 us
    ppermute x22, starting transfers between devices, cross(): lax.ppermute(value, 'chip', [(i, i ^ bits) for i in range(lax.axis_size('...  20.8 us
    ppermute x16, starting transfers between devices, beside(): return lax.ppermute(value, 'core', [(0, 1), (1, 0)])  18.8 us
    ppermute x4, waiting for transfers between devices, turn(): lax.ppermute(value, axis, [(i, (i + by) % size) for i in range(size)])  17.5 us
    all_to_all x3, starting transfers between devices, deal(): return lax.all_to_all(parts, axis, 0, 0)  12.7 us
    ppermute x2, waiting for transfers between devices, heads_sum(): arrived = lax.ppermute(low, 'head', [(i, i ^ bits) for i in range(size)])  12.1 us
  transfers between devices with their start and end apart: 52, of which 25 were waited for; matrix products, arithmetic and copies ran while one was open for 4% of the time, Pallas kernels for 15%

profile of v2, /device:TPU:1, one launch (start us, length us, event | category | flops | bytes accessed | tf_op | source)
XLA Modules:
  0.0 285.7 jit_solution(5612827741374338077)
XLA Ops:
  1.4 4.5 %collective-permute-start = (bf16[16,384]{1,0:T(8,128)(2,1)S(1)}, bf16[16,384]{1,0:T(8,128)(2,1)S(1)}, u32[]{:S(2)}, u32[]{:S(2)}) collective-permute-start(bf16[16,384]{1,0:T(8,128)(2,1)S(1)} %slice_bitcast_fusion), channel_id=1, source_target_pairs={{0,4},{4,8},{8,12},{12,16},{16,20},{20,24},{24,28},{1,5},{5,9},{9,... | collective-permute-start | bytes 36872 | tf_op jit(solution)/shard_map/ppermute | solution.py:46
  12.1 4.0 %collective-permute-start.3 = (bf16[544,384]{1,0:T(8,128)(2,1)S(1)}, bf16[544,384]{1,0:T(8,128)(2,1)S(1)}, u32[]{:S(2)}, u32[]{:S(2)}) collective-permute-start(bf16[544,384]{1,0:T(8,128)(2,1)S(1)} %pad_maximum_fusion.2.refs_0_.refs_4_), channel_id=1, source_target_pairs={{0,1},{1,2},{2,3},{4,5},{5,6},{6,7},{8,9},{9,10},{10,11},{12,13},{... | collective-permute-start | bytes 1253384 | tf_op jit(solution)/shard_map/ppermute | solution.py:67
  16.1 13.7 %collective-permute-done.1.refs_2_.refs_6_ = bf16[544,384]{1,0:T(8,128)(2,1)S(1)} collective-permute-done((bf16[544,384]{1,0:T(8,128)(2,1)S(1)}, bf16[544,384]{1,0:T(8,128)(2,1)S(1)}, u32[]{:S(2)}, u32[]{:S(2)}) %collective-permute-start.1) | collective-permute-done | bytes 417824 | tf_op jit(solution)/shard_map/ppermute | solution.py:55
  31.0 10.9 %collective-permute-done.2.passed_ref.refs_8_ = bf16[544,384]{1,0:T(8,128)(2,1)S(1)} collective-permute-done((bf16[544,384]{1,0:T(8,128)(2,1)S(1)}, bf16[544,384]{1,0:T(8,128)(2,1)S(1)}, u32[]{:S(2)}, u32[]{:S(2)}) %collective-permute-start.2) | collective-permute-done | bytes 417824 | tf_op jit(solution)/shard_map/ppermute | solution.py:69
  47.9 4.5 %all-to-all-start = ((bf16[4,512,384]{2,1,0:T(8,128)(2,1)}), bf16[4,512,384]{2,1,0:T(8,128)(2,1)}, u32[]{:S(2)}, u32[]{:S(2)}) async-start(bf16[4,512,384]{2,1,0:T(8,128)(2,1)} %copy-done.31), calls=%async_computation | async-start | bytes 3145728 | tf_op jit(solution)/shard_map/all_to_all | solution.py:74
  57.6 4.1 %conv.1 = (bf16[512,768]{1,0:T(8,128)(2,1)S(1)}, bf16[512,768]{1,0:T(8,128)(2,1)S(1)}, f32[512,768]{1,0:T(8,128)S(1)}, bf16[512,256]{1,0:T(8,128)(2,1)S(1)}, f32...) custom-call(bf16[544,768]{1,0:T(8,128)(2,1)S(1)} %convolution_convert_fusion.value_ref.value_raw_ref, ...), custom_call_target="tpu_custom_call" | custom-call | flops 157286400 | bytes 5523456 | tf_op jit(solution)/shard_map/conv/pallas_call | solution.py:940
  70.6 4.8 %collective-permute-done.8.refs_3_ = f32[72,768]{1,0:T(8,128)} collective-permute-done((f32[72,768]{1,0:T(8,128)}, f32[72,768]{1,0:T(8,128)}, u32[]{:S(2)}, u32[]{:S(2)}) %collective-permute-start.8) | collective-permute-done | bytes 221216 | tf_op jit(solution)/shard_map/ppermute | solution.py:78
  75.4 5.3 %collective-permute-done.7.refs_2_ = f32[72,768]{1,0:T(8,128)} collective-permute-done((f32[72,768]{1,0:T(8,128)}, f32[72,768]{1,0:T(8,128)}, u32[]{:S(2)}, u32[]{:S(2)}) %collective-permute-start.7) | collective-permute-done | bytes 221216 | tf_op jit(solution)/shard_map/ppermute | solution.py:78
  90.7 2.9 %mixed_grad.1 = (f32[512,768]{1,0:T(8,128)S(1)}, bf16[512,1536]{1,0:T(8,128)(2,1)S(1)}) custom-call(bf16[4,512,384]{2,1,0:T(8,128)(2,1)} %all-to-all-done.parts_ref, bf16[768,1536]{1,0:T(8,128)(2,1)S(1)} %copy-done.11), custom_call_target="tpu_custom_call" | custom-call | flops 1207959552 | bytes 7077888 | tf_op jit(solution)/shard_map/mixed_grad/pallas_call | solution.py:940
  97.9 2.9 %collective-permute-start.12 = (f32[8,512]{1,0:T(8,128)S(1)}, f32[8,512]{1,0:T(8,128)S(1)}, u32[]{:S(2)}, u32[]{:S(2)}) collective-permute-start(f32[8,512]{1,0:T(8,128)S(1)} %get-tuple-element.89.refs_0_), channel_id=1, source_target_pairs={{0,3},{1,0},{2,1},{3,2},{4,7},{5,4},{6,5},{7,6},{8,11},{9,8},{10,9... | collective-permute-start | bytes 49160 | tf_op jit(solution)/shard_map/ppermute | solution.py:55
  101.7 2.6 collective-permute-done.11.refs_2_
  105.2 3.7 %gate.1 = (bf16[512,768]{1,0:T(8,128)(2,1)S(1)}, bf16[512,768]{1,0:T(8,128)(2,1)S(1)}, f32[512,768]{1,0:T(8,128)S(1)}, f32[8,768]{1,0:T(8,128)S(1)}, f32[136,768]{1,0:T(8,128)S(1)}, /*index=5*/f32[8,512]{1,0:T(8,128)S(1)}) custom-call(f32[8,512]{1,0:T(8,128)S(1)} %get-tuple-element.89.refs_0_, f32[8,512]{1,0:T(8,128)S(1)} %collective-permute-done.10.refs_1_, ...), custom_call_target="tpu_custom_call" | custom-call | flops 235929600 | bytes 9487872 | tf_op jit(solution)/shard_map/gate/pallas_call | solution.py:940
  116.1 6.6 %early.1 = (bf16[4,384,768]{2,1,0:T(8,128)(2,1)S(1)}, bf16[4,384,768]{2,1,0:T(8,128)(2,1)}, f32[1,1536]{1,0:T(1,128)S(1)}) custom-call(f32[72,768]{1,0:T(8,128)S(1)} %after_pair.1.loose_ref.refs_0_, s32[1]{0:T(128)} %bitcast.core_ref, bf16[544,1536]{1,0:T(8,128)(2,1)S(1)} %copy-done.79, bf16[512,768]{1,0:T(8,128)(2,1)S(1)} %get-tuple-element.93.gate_ref.gate_grad_ref, ...), custom_call_target="tpu_custom_call" | custom-call | flops 2415919104 | bytes 11900932 | tf_op jit(solution)/shard_map/early/pallas_call | solution.py:940
  125.9 5.3 %collective-permute-done.14.refs_1_ = f32[72,768]{1,0:T(8,128)S(1)} collective-permute-done((f32[72,768]{1,0:T(8,128)S(1)}, f32[72,768]{1,0:T(8,128)S(1)}, u32[]{:S(2)}, u32[]{:S(2)}) %collective-permute-start.14) | collective-permute-done | bytes 221216 | tf_op jit(solution)/shard_map/ppermute | solution.py:78
  131.9 3.6 %all-to-all-start.1 = ((bf16[4,512,384]{2,1,0:T(8,128)(2,1)}), bf16[4,512,384]{2,1,0:T(8,128)(2,1)S(1)}, u32[]{:S(2)}, u32[]{:S(2)}) async-start(bf16[4,512,384]{2,1,0:T(8,128)(2,1)} %tie.3), calls=%async_computation.1 | async-start | bytes 3145728 | tf_op jit(solution)/shard_map/all_to_all | solution.py:74
  138.0 4.3 %collective-permute-done.17.refs_3_ = f32[72,768]{1,0:T(8,128)S(1)} collective-permute-done((f32[72,768]{1,0:T(8,128)}, f32[72,768]{1,0:T(8,128)S(1)}, u32[]{:S(2)}, u32[]{:S(2)}) %collective-permute-start.17) | collective-permute-done | bytes 221216 | tf_op jit(solution)/shard_map/ppermute | solution.py:78
  142.3 6.5 %collective-permute-done.16.refs_2_ = f32[72,768]{1,0:T(8,128)S(1)} collective-permute-done((f32[72,768]{1,0:T(8,128)}, f32[72,768]{1,0:T(8,128)S(1)}, u32[]{:S(2)}, u32[]{:S(2)}) %collective-permute-start.16) | collective-permute-done | bytes 221216 | tf_op jit(solution)/shard_map/ppermute | solution.py:78
  156.8 5.6 %back.1 = (f32[512,768]{1,0:T(8,128)S(1)}, f32[512,256]{1,0:T(8,128)S(1)}) custom-call(f32[2,192,768]{2,1,0:T(8,128)S(1)} %get-tuple-element.97.early_ref.first_ref, f32[128,768]{1,0:T(8,128)S(1)} %after_enter.1.state_in_ref, f32[512,768]{1,0:T(8,128)S(1)} %copy-done.28, f32[512,12]{1,0:T(8,128)S(1)} %get-tuple-element.86.e_ref.refs_9_, ...), custom_call_target="tpu_custom_call" | custom-call | flops 786432000 | bytes 8858624 | tf_op jit(solution)/shard_map/back/pallas_call | solution.py:940
  164.8 4.1 %collective-permute-done.21.after_ref = f32[8,1024]{1,0:T(8,128)S(1)} collective-permute-done((f32[8,1024]{1,0:T(8,128)S(1)}, f32[8,1024]{1,0:T(8,128)S(1)}, u32[]{:S(2)}, u32[]{:S(2)}) %collective-permute-start.21) | collective-permute-done | bytes 32800 | tf_op jit(solution)/shard_map/ppermute | solution.py:46
  168.9 3.5 %conv_back.1 = (bf16[512,768]{1,0:T(8,128)(2,1)S(1)}, bf16[512,256]{1,0:T(8,128)(2,1)S(1)}, f32[8,768]{1,0:T(8,128)S(1)}, f32[8,256]{1,0:T(8,128)S(1)}, f32[8,512]{1,0:T(8,128)S(1)}) custom-call(f32[512,768]{1,0:T(8,128)S(1)} %get-tuple-element.106.value_ref, f32[512,256]{1,0:T(8,128)S(1)} %get-tuple-element.107.map_ref, ...), custom_call_target="tpu_custom_call" | custom-call | flops 39321600 | bytes 4366336 | tf_op jit(solution)/shard_map/conv_back/pallas_call | solution.py:940
  182.9 5.3 %normed.1.loose_ref = bf16[4,528,384]{2,1,0:T(8,128)(2,1)} custom-call(f32[192,768]{1,0:T(8,128)S(1)} %get-tuple-element.110.early_ref.first_ref, bf16[4,512,384]{2,1,0:T(8,128)(2,1)S(1)} %all-to-all-done.1.out_ref_in, bf16[512,768]{1,0:T(8,128)(2,1)S(1)} %copy-done.50, bf16[512,768]{1,0:T(8,128)(2,1)S(1)} %copy-done.52, bf16[512,256]{1,0:T(8,128)(2,1)S(1)} %copy-done.73, ...), custom_call_target="tpu_custom_call" | custom-call | flops 2415919104 | bytes 8978432 | tf_op jit(solution)/shard_map/normed/pallas_call | solution.py:940
  190.5 5.2 %late.1 = (bf16[4,272,768]{2,1,0:T(8,128)(2,1)S(1)}, bf16[4,272,768]{2,1,0:T(8,128)(2,1)}) custom-call(bf16[192,768]{1,0:T(8,128)(2,1)} %get-tuple-element.117.early_ref, s32[1]{0:T(128)} %bitcast.core_ref, bf16[544,1536]{1,0:T(8,128)(2,1)S(1)} %copy-done.80, bf16[512,768]{1,0:T(8,128)(2,1)S(1)} %copy-done.53, bf16[512,256]{1,0:T(8,128)(2,1)S(1)} %copy-done.74, ...), custom_call_target="tpu_custom_call" | custom-call | flops 1811939328 | bytes 9320452 | tf_op jit(solution)/shard_map/late/pallas_call | solution.py:940
  195.7 4.6 %all-to-all-start.2 = ((bf16[4,528,384]{2,1,0:T(8,128)(2,1)}), bf16[4,528,384]{2,1,0:T(8,128)(2,1)}, u32[]{:S(2)}, u32[]{:S(2)}) async-start(bf16[4,528,384]{2,1,0:T(8,128)(2,1)} %normed.1.loose_ref), calls=%async_computation.2 | async-start | bytes 3244032 | tf_op jit(solution)/shard_map/all_to_all | solution.py:74
  201.8 2.6 late_half.1
  218.9 8.7 %collective-permute-done.27.refs_3_ = bf16[272,768]{1,0:T(8,128)(2,1)} collective-permute-done((bf16[272,768]{1,0:T(8,128)(2,1)}, bf16[272,768]{1,0:T(8,128)(2,1)}, u32[]{:S(2)}, u32[]{:S(2)}) %collective-permute-start.27) | collective-permute-done | bytes 417824 | tf_op jit(solution)/shard_map/ppermute | solution.py:78
  231.3 10.1 %collective-permute-done.28.arrived_ref = bf16[80,768]{1,0:T(8,128)(2,1)S(1)} collective-permute-done((bf16[80,768]{1,0:T(8,128)(2,1)S(1)}, bf16[80,768]{1,0:T(8,128)(2,1)S(1)}, u32[]{:S(2)}, u32[]{:S(2)}) %collective-permute-start.28) | collective-permute-done | bytes 122912 | tf_op jit(solution)/shard_map/ppermute | solution.py:89
  242.8 3.5 %collective-permute-start.42 = (bf16[1,192,768]{2,1,0:T(8,128)(2,1)S(1)}, bf16[1,192,768]{2,1,0:T(8,128)(2,1)S(1)}, u32[]{:S(2)}, u32[]{:S(2)}) collective-permute-start(bf16[1,192,768]{2,1,0:T(8,128)(2,1)S(1)} %bitcast.34), channel_id=1, source_target_pairs={{0,4},{4,0},{1,5},{5,1},{2,6},{6,2},{3,7},{7,3},{8,12},{12,8},{9,1... | collective-permute-start | bytes 884744 | tf_op jit(solution)/shard_map/ppermute | solution.py:50
  248.4 2.9 %collective-permute-start.48 = (bf16[1,192,768]{2,1,0:T(8,128)(2,1)S(1)}, bf16[1,192,768]{2,1,0:T(8,128)(2,1)S(1)}, u32[]{:S(2)}, u32[]{:S(2)}) collective-permute-start(bf16[1,192,768]{2,1,0:T(8,128)(2,1)S(1)} %bitcast.36), channel_id=1, source_target_pairs={{0,4},{4,0},{1,5},{5,1},{2,6},{6,2},{3,7},{7,3},{8,12},{12,8},{9,1... | collective-permute-start | bytes 884744 | tf_op jit(solution)/shard_map/ppermute | solution.py:50
  264.1 4.2 %collective-permute-done.32.refs_2_ = bf16[2,80,768]{2,1,0:T(8,128)(2,1)} collective-permute-done((bf16[2,80,768]{2,1,0:T(8,128)(2,1)S(1)}, bf16[2,80,768]{2,1,0:T(8,128)(2,1)}, u32[]{:S(2)}, u32[]{:S(2)}) %collective-permute-start.32) | collective-permute-done | bytes 245792 | tf_op jit(solution)/shard_map/ppermute | solution.py:78
  271.6 2.7 last.1
  276.7 5.7 %early_out.1 = (f32[1536,768]{1,0:T(8,128)}, f32[768,1536]{1,0:T(8,128)}) custom-call(s32[1]{0:T(128)} %bitcast.core_ref, s32[1]{0:T(128)} %bitcast.6.chip_ref, bf16[2,192,768]{2,1,0:T(8,128)(2,1)S(1)} %copy-done.3, bf16[2,192,768]{2,1,0:T(8,128)(2,1)} %collective-permute-done.35.refs_1_, bf16[2,192,768]{2,1,0:T(8,128)(2,1)} %collective-permute-done.36.refs_2_, ...), custom_call_target="tpu_custom_call" | custom-call | flops 4718592 | bytes 14155784 | tf_op jit(solution)/shard_map/early_out/pallas_call | solution.py:940
  282.5 3.0 %shared_out.1 = (f32[1536,256]{1,0:T(8,128)}, f32[4,768]{1,0:T(4,128)}, f32[768]{0:T(1024)}, f32[4,256]{1,0:T(4,128)}, f32[256]{0:T(256)}, /*index=5*/f32[12]{0:T(128)}, f32[768]{0:T(1024)}, f32[384]{0:T(512)}) custom-call(s32[1]{0:T(128)} %bitcast.core_ref, s32[1]{0:T(128)} %bitcast.6.chip_ref, s32[1]{0:T(128)} %bitcast.1.head_ref, ...), custom_call_target="tpu_custom_call" | custom-call | flops 786432 | bytes 2581052 | tf_op jit(solution)/shard_map/shared_out/pallas_call | solution.py:940
  (321 shorter events, 121.9 us)
Async XLA Ops:
  8.4 21.3 %collective-permute-start.1 = (bf16[544,384]{1,0:T(8,128)(2,1)S(1)}, bf16[544,384]{1,0:T(8,128)(2,1)S(1)}, u32[]{:S(2)}, u32[]{:S(2)}) collective-permute-start(bf16[544,384]{1,0:T(8,128)(2,1)S(1)} %pad_maximum_fusion.2.refs_0_.refs_4_), channel_id=1, source_target_pairs={{0,2},{1,3},{2,0},{3,1},{4,6},{5,7},{6,4},{7,5},{8,10},{9,11},{10,... | collective-permute-start | bytes 1253384 | tf_op jit(solution)/shard_map/ppermute | solution.py:55
  10.8 20.3 %collective-permute-start.4 = (bf16[544,384]{1,0:T(8,128)(2,1)S(1)}, bf16[544,384]{1,0:T(8,128)(2,1)S(1)}, u32[]{:S(2)}, u32[]{:S(2)}) collective-permute-start(bf16[544,384]{1,0:T(8,128)(2,1)S(1)} %pad_maximum_fusion.2.refs_0_.refs_4_), channel_id=1, source_target_pairs={{1,0},{2,1},{3,2},{5,4},{6,5},{7,6},{9,8},{10,9},{11,10},{13,12},{... | collective-permute-start | bytes 1253384 | tf_op jit(solution)/shard_map/ppermute | solution.py:68
  12.1 19.0 %collective-permute-start.3 = (bf16[544,384]{1,0:T(8,128)(2,1)S(1)}, bf16[544,384]{1,0:T(8,128)(2,1)S(1)}, u32[]{:S(2)}, u32[]{:S(2)}) collective-permute-start(bf16[544,384]{1,0:T(8,128)(2,1)S(1)} %pad_maximum_fusion.2.refs_0_.refs_4_), channel_id=1, source_target_pairs={{0,1},{1,2},{2,3},{4,5},{5,6},{6,7},{8,9},{9,10},{10,11},{12,13},{... | collective-permute-start | bytes 1253384 | tf_op jit(solution)/shard_map/ppermute | solution.py:67
  29.7 12.2 %collective-permute-start.2 = (bf16[544,384]{1,0:T(8,128)(2,1)S(1)}, bf16[544,384]{1,0:T(8,128)(2,1)S(1)}, u32[]{:S(2)}, u32[]{:S(2)}) collective-permute-start(bf16[544,384]{1,0:T(8,128)(2,1)S(1)} %collective-permute-done.1.refs_2_.refs_6_), channel_id=1, source_target_pairs={{2,3},{1,0},{6,7},{5,4},{10,11},{9,8},{14,15},{13,12},{18,19},{17,... | collective-permute-start | bytes 1253384 | tf_op jit(solution)/shard_map/ppermute | solution.py:69
  47.9 41.1 %all-to-all-start = ((bf16[4,512,384]{2,1,0:T(8,128)(2,1)}), bf16[4,512,384]{2,1,0:T(8,128)(2,1)}, u32[]{:S(2)}, u32[]{:S(2)}) async-start(bf16[4,512,384]{2,1,0:T(8,128)(2,1)} %copy-done.31), calls=%async_computation | async-start | bytes 3145728 | tf_op jit(solution)/shard_map/all_to_all | solution.py:74
  69.1 11.6 %collective-permute-start.7 = (f32[72,768]{1,0:T(8,128)}, f32[72,768]{1,0:T(8,128)}, u32[]{:S(2)}, u32[]{:S(2)}) collective-permute-start(f32[72,768]{1,0:T(8,128)} %before_pair.1.refs_0_), channel_id=1, source_target_pairs={{0,16},{8,24},{16,0},{24,8},{1,17},{9,25},{17,1},{25,9},{2,18},{10... | collective-permute-start | bytes 663560 | tf_op jit(solution)/shard_map/ppermute | solution.py:78
  70.6 10.4 %collective-permute-start.6 = (f32[72,768]{1,0:T(8,128)}, f32[72,768]{1,0:T(8,128)}, u32[]{:S(2)}, u32[]{:S(2)}) collective-permute-start(f32[72,768]{1,0:T(8,128)} %before_pair.1.refs_0_), channel_id=1, source_target_pairs={{0,8},{8,0},{16,24},{24,16},{1,9},{9,1},{17,25},{25,17},{2,10},{10... | collective-permute-start | bytes 663560 | tf_op jit(solution)/shard_map/ppermute | solution.py:78
  124.7 26.0 %collective-permute-start.15 = (bf16[4,384,768]{2,1,0:T(8,128)(2,1)}, bf16[4,384,768]{2,1,0:T(8,128)(2,1)}, u32[]{:S(2)}, u32[]{:S(2)}) collective-permute-start(bf16[4,384,768]{2,1,0:T(8,128)(2,1)} %get-tuple-element.96.refs_4_), channel_id=1, source_target_pairs={{0,4},{4,0},{1,5},{5,1},{2,6},{6,2},{3,7},{7,3},{8,12},{12,8},{9,1... | collective-permute-start | bytes 7077896 | tf_op jit(solution)/shard_map/ppermute | solution.py:50
  131.9 44.4 %all-to-all-start.1 = ((bf16[4,512,384]{2,1,0:T(8,128)(2,1)}), bf16[4,512,384]{2,1,0:T(8,128)(2,1)S(1)}, u32[]{:S(2)}, u32[]{:S(2)}) async-start(bf16[4,512,384]{2,1,0:T(8,128)(2,1)} %tie.3), calls=%async_computation.1 | async-start | bytes 3145728 | tf_op jit(solution)/shard_map/all_to_all | solution.py:74
  136.7 12.0 %collective-permute-start.16 = (f32[72,768]{1,0:T(8,128)}, f32[72,768]{1,0:T(8,128)S(1)}, u32[]{:S(2)}, u32[]{:S(2)}) collective-permute-start(f32[72,768]{1,0:T(8,128)} %copy-done.38), channel_id=1, source_target_pairs={{0,16},{8,24},{16,0},{24,8},{1,17},{9,25},{17,1},{25,9},{2,18},{10... | collective-permute-start | bytes 663560 | tf_op jit(solution)/shard_map/ppermute | solution.py:78
  153.1 20.8 %collective-permute-start.18 = (bf16[2,192,768]{2,1,0:T(8,128)(2,1)S(1)}, bf16[2,192,768]{2,1,0:T(8,128)(2,1)S(1)}, u32[]{:S(2)}, u32[]{:S(2)}) collective-permute-start(bf16[2,192,768]{2,1,0:T(8,128)(2,1)S(1)} %get-tuple-element.98), channel_id=1, source_target_pairs={{0,8},{8,0},{16,24},{24,16},{1,9},{9,1},{17,25},{25,17},{2,10},{10... | collective-permute-start | bytes 1769480 | tf_op jit(solution)/shard_map/ppermute | solution.py:78
  154.4 19.5 %collective-permute-start.19 = (bf16[2,192,768]{2,1,0:T(8,128)(2,1)S(1)}, bf16[2,192,768]{2,1,0:T(8,128)(2,1)S(1)}, u32[]{:S(2)}, u32[]{:S(2)}) collective-permute-start(bf16[2,192,768]{2,1,0:T(8,128)(2,1)S(1)} %get-tuple-element.100), channel_id=1, source_target_pairs={{0,16},{8,24},{16,0},{24,8},{1,17},{9,25},{17,1},{25,9},{2,18},{10... | collective-permute-start | bytes 1769480 | tf_op jit(solution)/shard_map/ppermute | solution.py:78
  174.9 13.3 %collective-permute-start.22 = (bf16[192,768]{1,0:T(8,128)(2,1)}, bf16[192,768]{1,0:T(8,128)(2,1)}, u32[]{:S(2)}, u32[]{:S(2)}) collective-permute-start(bf16[192,768]{1,0:T(8,128)(2,1)} %get-tuple-element.114), channel_id=1, source_target_pairs={{0,16},{8,24},{16,0},{24,8},{1,17},{9,25},{17,1},{25,9},{2,18},{10... | collective-permute-start | bytes 884744 | tf_op jit(solution)/shard_map/ppermute | solution.py:78
  176.2 12.0 %collective-permute-start.23 = (bf16[192,768]{1,0:T(8,128)(2,1)}, bf16[192,768]{1,0:T(8,128)(2,1)}, u32[]{:S(2)}, u32[]{:S(2)}) collective-permute-start(bf16[192,768]{1,0:T(8,128)(2,1)} %get-tuple-element.116), channel_id=1, source_target_pairs={{0,8},{8,0},{16,24},{24,16},{1,9},{9,1},{17,25},{25,17},{2,10},{10... | collective-permute-start | bytes 884744 | tf_op jit(solution)/shard_map/ppermute | solution.py:78
  195.7 74.7 %all-to-all-start.2 = ((bf16[4,528,384]{2,1,0:T(8,128)(2,1)}), bf16[4,528,384]{2,1,0:T(8,128)(2,1)}, u32[]{:S(2)}, u32[]{:S(2)}) async-start(bf16[4,528,384]{2,1,0:T(8,128)(2,1)} %normed.1.loose_ref), calls=%async_computation.2 | async-start | bytes 3244032 | tf_op jit(solution)/shard_map/all_to_all | solution.py:74
  201.7 10.1 %collective-permute-start.38 = (bf16[192,768]{1,0:T(8,128)(2,1)}, bf16[192,768]{1,0:T(8,128)(2,1)}, u32[]{:S(2)}, u32[]{:S(2)}) collective-permute-start(bf16[192,768]{1,0:T(8,128)(2,1)} %get-tuple-element.134), channel_id=1, source_target_pairs={{0,8},{8,0},{16,24},{24,16},{1,9},{9,1},{17,25},{25,17},{2,10},{10... | collective-permute-start | bytes 884744 | tf_op jit(solution)/shard_map/ppermute | solution.py:78
  205.4 13.3 %collective-permute-start.25 = (bf16[272,768]{1,0:T(8,128)(2,1)}, bf16[272,768]{1,0:T(8,128)(2,1)S(1)}, u32[]{:S(2)}, u32[]{:S(2)}) collective-permute-start(bf16[272,768]{1,0:T(8,128)(2,1)} %get-tuple-element.126), channel_id=1, source_target_pairs={{0,8},{8,0},{16,24},{24,16},{1,9},{9,1},{17,25},{25,17},{2,10},{10... | collective-permute-start | bytes 1253384 | tf_op jit(solution)/shard_map/ppermute | solution.py:78
  206.7 12.2 %collective-permute-start.26 = (bf16[272,768]{1,0:T(8,128)(2,1)}, bf16[272,768]{1,0:T(8,128)(2,1)}, u32[]{:S(2)}, u32[]{:S(2)}) collective-permute-start(bf16[272,768]{1,0:T(8,128)(2,1)} %get-tuple-element.127), channel_id=1, source_target_pairs={{0,16},{8,24},{16,0},{24,8},{1,17},{9,25},{17,1},{25,9},{2,18},{10... | collective-permute-start | bytes 1253384 | tf_op jit(solution)/shard_map/ppermute | solution.py:78
  206.9 20.7 %collective-permute-start.27 = (bf16[272,768]{1,0:T(8,128)(2,1)}, bf16[272,768]{1,0:T(8,128)(2,1)}, u32[]{:S(2)}, u32[]{:S(2)}) collective-permute-start(bf16[272,768]{1,0:T(8,128)(2,1)} %get-tuple-element.128), channel_id=1, source_target_pairs={{0,24},{8,16},{16,8},{24,0},{1,25},{9,17},{17,9},{25,1},{2,26},{10... | collective-permute-start | bytes 1253384 | tf_op jit(solution)/shard_map/ppermute | solution.py:78
  210.6 32.1 %collective-permute-start.36 = (bf16[2,192,768]{2,1,0:T(8,128)(2,1)}, bf16[2,192,768]{2,1,0:T(8,128)(2,1)}, u32[]{:S(2)}, u32[]{:S(2)}) collective-permute-start(bf16[2,192,768]{2,1,0:T(8,128)(2,1)} %tie.4.refs_0_), channel_id=1, source_target_pairs={{0,8},{8,0},{16,24},{24,16},{1,9},{9,1},{17,25},{25,17},{2,10},{10... | collective-permute-start | bytes 1769480 | tf_op jit(solution)/shard_map/ppermute | solution.py:78
  211.8 31.0 %collective-permute-start.35 = (bf16[2,192,768]{2,1,0:T(8,128)(2,1)}, bf16[2,192,768]{2,1,0:T(8,128)(2,1)}, u32[]{:S(2)}, u32[]{:S(2)}) collective-permute-start(bf16[2,192,768]{2,1,0:T(8,128)(2,1)} %tie.4.refs_0_), channel_id=1, source_target_pairs={{0,4},{4,0},{1,5},{5,1},{2,6},{6,2},{3,7},{7,3},{8,12},{12,8},{9,1... | collective-permute-start | bytes 1769480 | tf_op jit(solution)/shard_map/ppermute | solution.py:50
  218.7 36.5 %collective-permute-start.40 = (bf16[2,192,768]{2,1,0:T(8,128)(2,1)}, bf16[2,192,768]{2,1,0:T(8,128)(2,1)}, u32[]{:S(2)}, u32[]{:S(2)}) collective-permute-start(bf16[2,192,768]{2,1,0:T(8,128)(2,1)} %tie.5.refs_4_), channel_id=1, source_target_pairs={{0,16},{8,24},{16,0},{24,8},{1,17},{9,25},{17,1},{25,9},{2,18},{10... | collective-permute-start | bytes 1769480 | tf_op jit(solution)/shard_map/ppermute | solution.py:78
  229.0 12.4 %collective-permute-start.28 = (bf16[80,768]{1,0:T(8,128)(2,1)S(1)}, bf16[80,768]{1,0:T(8,128)(2,1)S(1)}, u32[]{:S(2)}, u32[]{:S(2)}) collective-permute-start(bf16[80,768]{1,0:T(8,128)(2,1)S(1)} %convert_element_type.29), channel_id=1, source_target_pairs={{0,1},{1,0},{2,3},{3,2},{4,5},{5,4},{6,7},{7,6},{8,9},{9,8},{10,11... | collective-permute-start | bytes 368648 | tf_op jit(solution)/shard_map/ppermute | solution.py:89
  230.1 18.4 %collective-permute-start.47 = (bf16[192,768]{1,0:T(8,128)(2,1)S(1)}, bf16[192,768]{1,0:T(8,128)(2,1)S(1)}, u32[]{:S(2)}, u32[]{:S(2)}) collective-permute-start(bf16[192,768]{1,0:T(8,128)(2,1)S(1)} %get-tuple-element.136), channel_id=1, source_target_pairs={{0,24},{8,16},{16,8},{24,0},{1,25},{9,17},{17,9},{25,1},{2,26},{10... | collective-permute-start | bytes 884744 | tf_op jit(solution)/shard_map/ppermute | solution.py:78
  241.4 12.5 %collective-permute-start.45 = (bf16[192,768]{1,0:T(8,128)(2,1)S(1)}, bf16[192,768]{1,0:T(8,128)(2,1)S(1)}, u32[]{:S(2)}, u32[]{:S(2)}) collective-permute-start(bf16[192,768]{1,0:T(8,128)(2,1)S(1)} %get-tuple-element.136), channel_id=1, source_target_pairs={{0,16},{8,24},{16,0},{24,8},{1,17},{9,25},{17,1},{25,9},{2,18},{10... | collective-permute-start | bytes 884744 | tf_op jit(solution)/shard_map/ppermute | solution.py:78
  242.8 13.7 %collective-permute-start.42 = (bf16[1,192,768]{2,1,0:T(8,128)(2,1)S(1)}, bf16[1,192,768]{2,1,0:T(8,128)(2,1)S(1)}, u32[]{:S(2)}, u32[]{:S(2)}) collective-permute-start(bf16[1,192,768]{2,1,0:T(8,128)(2,1)S(1)} %bitcast.34), channel_id=1, source_target_pairs={{0,4},{4,0},{1,5},{5,1},{2,6},{6,2},{3,7},{7,3},{8,12},{12,8},{9,1... | collective-permute-start | bytes 884744 | tf_op jit(solution)/shard_map/ppermute | solution.py:50
  248.4 12.5 %collective-permute-start.48 = (bf16[1,192,768]{2,1,0:T(8,128)(2,1)S(1)}, bf16[1,192,768]{2,1,0:T(8,128)(2,1)S(1)}, u32[]{:S(2)}, u32[]{:S(2)}) collective-permute-start(bf16[1,192,768]{2,1,0:T(8,128)(2,1)S(1)} %bitcast.36), channel_id=1, source_target_pairs={{0,4},{4,0},{1,5},{5,1},{2,6},{6,2},{3,7},{7,3},{8,12},{12,8},{9,1... | collective-permute-start | bytes 884744 | tf_op jit(solution)/shard_map/ppermute | solution.py:50
  256.5 20.2 %collective-permute-start.39 = (bf16[2,192,768]{2,1,0:T(8,128)(2,1)S(1)}, bf16[2,192,768]{2,1,0:T(8,128)(2,1)}, u32[]{:S(2)}, u32[]{:S(2)}) collective-permute-start(bf16[2,192,768]{2,1,0:T(8,128)(2,1)S(1)} %copy-done.4), channel_id=1, source_target_pairs={{0,4},{4,0},{1,5},{5,1},{2,6},{6,2},{3,7},{7,3},{8,12},{12,8},{9,1... | collective-permute-start | bytes 1769480 | tf_op jit(solution)/shard_map/ppermute | solution.py:50
  256.9 19.8 %collective-permute-start.37 = (bf16[2,192,768]{2,1,0:T(8,128)(2,1)}, bf16[2,192,768]{2,1,0:T(8,128)(2,1)}, u32[]{:S(2)}, u32[]{:S(2)}) collective-permute-start(bf16[2,192,768]{2,1,0:T(8,128)(2,1)} %collective-permute-done.36.refs_2_), channel_id=1, source_target_pairs={{0,4},{4,0},{1,5},{5,1},{2,6},{6,2},{3,7},{7,3},{8,12},{12,8},{9,1... | collective-permute-start | bytes 1769480 | tf_op jit(solution)/shard_map/ppermute | solution.py:50
  260.1 16.6 %collective-permute-start.41 = (bf16[2,192,768]{2,1,0:T(8,128)(2,1)}, bf16[2,192,768]{2,1,0:T(8,128)(2,1)}, u32[]{:S(2)}, u32[]{:S(2)}) collective-permute-start(bf16[2,192,768]{2,1,0:T(8,128)(2,1)} %collective-permute-done.40.refs_6_), channel_id=1, source_target_pairs={{0,4},{4,0},{1,5},{5,1},{2,6},{6,2},{3,7},{7,3},{8,12},{12,8},{9,1... | collective-permute-start | bytes 1769480 | tf_op jit(solution)/shard_map/ppermute | solution.py:50
  263.7 18.8 %collective-permute-start.31 = (bf16[2,80,768]{2,1,0:T(8,128)(2,1)S(1)}, bf16[2,80,768]{2,1,0:T(8,128)(2,1)}, u32[]{:S(2)}, u32[]{:S(2)}) collective-permute-start(bf16[2,80,768]{2,1,0:T(8,128)(2,1)S(1)} %pad_maximum_fusion.3.refs_0_), channel_id=1, source_target_pairs={{0,4},{4,0},{1,5},{5,1},{2,6},{6,2},{3,7},{7,3},{8,12},{12,8},{9,1... | collective-permute-start | bytes 737288 | tf_op jit(solution)/shard_map/ppermute | solution.py:50
  268.3 14.2 %collective-permute-start.33 = (bf16[2,80,768]{2,1,0:T(8,128)(2,1)}, bf16[2,80,768]{2,1,0:T(8,128)(2,1)}, u32[]{:S(2)}, u32[]{:S(2)}) collective-permute-start(bf16[2,80,768]{2,1,0:T(8,128)(2,1)} %collective-permute-done.32.refs_2_), channel_id=1, source_target_pairs={{0,4},{4,0},{1,5},{5,1},{2,6},{6,2},{3,7},{7,3},{8,12},{12,8},{9,1... | collective-permute-start | bytes 737288 | tf_op jit(solution)/shard_map/ppermute | solution.py:50
  (117 other events, 633.6 us)

commit v3 on v1

--- a/solution.py
+++ b/solution.py
@@ -83,7 +83,7 @@
 
 
 def heads_sum(piece):
-    total, low = piece, piece.astype(BF16)
+    total, low, first = piece, piece.astype(BF16), None
     bits, size = 1, lax.axis_size("head")
     while bits < size:
         arrived = lax.ppermute(low, "head", [(i, i ^ bits) for i in range(size)])
@@ -92,8 +92,9 @@
             [(WHOLE, piece), (WHOLE, total), (WHOLE, arrived)],
             [(WHOLE, piece.shape, F32), (WHOLE, piece.shape, BF16)],
         )
+        first = low if first is None else first
         bits *= 2
-    return low
+    return low, first
 
 
 def entering(core, chip, total, backward, meanwhile, later=lambda pair: ()):
@@ -120,7 +121,7 @@
     )[0], prefix
 
 
-def sum_pieces(chip, kept, given, name, square, cut, paired, before_half=()):
+def sum_pieces(chip, kept, given, name, square, cut, paired, before_half=(), meanwhile=lambda mark: ()):
     chips, rows, channels = kept.shape
     arrived = beside(given)
     size = chips * rows * channels
@@ -137,7 +138,8 @@
         parts = [halves[0]] + [cross(halves[bits], bits) for bits in range(1, chips)]
         found = run(
             functools.partial(piece_kernel, chips, paired, cut), name + "_piece", size,
-            [(WHOLE, part) for part in parts], outs,
+            [(WHOLE, part) for part in parts] + [(LOOSE, mark) for mark in meanwhile(halves[0])],
+            outs,
         )
         return found, halves[0]
     rest = rows - cut
@@ -507,7 +509,7 @@
 
 
 def back_kernel(
-    chunks, early_ref, state_in_ref, mixer_grad_ref, e_ref, f_ref, k_ref, weighted_ref, high_ref, low_ref,
+    chunks, state_in_ref, mixer_grad_ref, e_ref, f_ref, k_ref, weighted_ref, high_ref, low_ref,
     maps_ref, value_slope_ref, state_slope_ref, skip_ref,
     value_ref, map_ref, state_ref,
 ):
@@ -546,7 +548,7 @@
 
 
 def conv_back_kernel(
-    chunks, value_ref, map_ref, after_ref, value_raw_ref, state_raw_ref, value_kernel_ref,
+    chunks, early_ref, value_ref, map_ref, after_ref, value_raw_ref, state_raw_ref, value_kernel_ref,
     state_kernel_ref, cross_in_ref,
     value_grad_ref, state_grad_ref, value_small_ref, state_small_ref, cross_ref, value_next_ref,
     state_next_ref,
@@ -856,7 +858,7 @@
         copy.wait()
 
 
-def shared_out_kernel(chips, groups, size, core_ref, chip_ref, head_ref, loose_ref, *refs):
+def shared_out_kernel(chips, groups, size, core_ref, chip_ref, head_ref, *refs):
     (
         state_ref, value_kernel_ref, value_bias_ref, state_kernel_ref, state_bias_ref, skip_ref,
         gated_ref, gain_ref, buffer, sems, own_ref, shared_ref,
@@ -908,6 +910,7 @@
 BLOCKED = "blocked"
 LANES = "lanes"
 LEADING = "leading"
+FAR = "far"
 LOOSE = "loose"
 
 
@@ -921,6 +924,8 @@
             return pl.BlockSpec(memory_space=pltpu.SMEM)
         if kind == LOOSE:
             return pl.BlockSpec(memory_space=pl.ANY)
+        if kind == FAR:
+            return pl.BlockSpec(memory_space=pltpu.HBM)
         if isinstance(kind, tuple):
             return pl.BlockSpec(*kind)
         if steps is None:
@@ -1075,37 +1080,14 @@
         [(LOOSE, start_grad), (WHOLE, mixed), (WHOLE, output_weight)],
         [(WHOLE, (head_size, count, own_width), BF16)],
     )[0]
-    early_made = []
-
-    def make_early(pair):
-        early_made.extend(
-            run(
-                early_kernel, "early", 4 * count * channels * width,
-                [
-                    (LOOSE, pair), core, (feature_block, normed), (WHOLE, gate_grad),
-                    (((count, BLOCK), lambda i: (0, i // every)), mixed), (WHOLE, full_cotangent),
-                    (BLOCK, gate_weight),
-                ],
-                [(WHOLE, (chips, early_rows, channels), BF16)] * 2
-                + [(((1, BLOCK), lambda i: (0, i)), (1, width), F32)],
-                steps=features,
-                scratch=[pltpu.VMEM((BLOCK, width), F32)],
-            )
-        )
-        return early_made[1:2]
-
-    grad_after, after_prefix = entering(core, chip, start_grad, True, (out_parts,), make_early)
-    early_kept, early_given, early_gain = early_made
-    early_state, half_mark = sum_pieces(
-        chip, early_kept, early_given, "early", True, step, False, (after_prefix,)
-    )
+    grad_after, _ = entering(core, chip, start_grad, True, (out_parts,))
     branch = jnp.sum(deal(out_parts, "head").astype(F32), axis=0)
     block_out = (tokens.astype(F32) + branch).astype(BF16)
 
     value_grads, map_grads = run(
         functools.partial(back_kernel, chunks), "back", count * channels * 2000,
         [
-            (LOOSE, half_mark), (WHOLE, grad_after), (BLOCKED, mixer_grad), (BLOCKED, e_full),
+            (WHOLE, grad_after), (BLOCKED, mixer_grad), (BLOCKED, e_full),
             (BLOCKED, f_full), (WHOLE, factors), (BLOCKED, weighted), (LEADING, high),
             (LEADING, low), (BLOCKED, maps), (BLOCKED, value_slope), (BLOCKED, map_slope),
             (WHOLE, skip_full),
@@ -1115,11 +1097,23 @@
         backward=True,
         scratch=[pltpu.VMEM((NSTATE, channels), F32)],
     )
+    early_kept, early_given, early_gain = run(
+        early_kernel, "early", 4 * count * channels * width,
+        [
+            (LOOSE, value_grads), core, (feature_block, normed), (WHOLE, gate_grad),
+            (((count, BLOCK), lambda i: (0, i // every)), mixed), (WHOLE, full_cotangent),
+            (BLOCK, gate_weight),
+        ],
+        [(WHOLE, (chips, early_rows, channels), BF16)] * 2
+        + [(((1, BLOCK), lambda i: (0, i)), (1, width), F32)],
+        steps=features,
+        scratch=[pltpu.VMEM((BLOCK, width), F32)],
+    )
     after = from_behind(jnp.concatenate([value_grads[:8], map_grads[:8]], axis=1), -1)
     value_raw_grad, state_raw_grad, value_small, state_small, crossed = run(
         functools.partial(conv_back_kernel, chunks), "conv_back", count * channels * 100,
         [
-            (BLOCKED, value_grads), (BLOCKED, map_grads), (WHOLE, after),
+            (LOOSE, early_given), (BLOCKED, value_grads), (BLOCKED, map_grads), (WHOLE, after),
             (WHOLE, value_raw), (WHOLE, state_raw), (WHOLE, value_kernel), (WHOLE, state_kernel),
             (LANES, gate_cross),
         ],
@@ -1134,35 +1128,16 @@
         backward=True,
         scratch=[pltpu.VMEM((8, channels), F32), pltpu.VMEM((8, maps_width), F32)],
     )
-    next_mark = early_state[0]
-    if chips == 4:
-        early_state = square_next("early", early_state, early_rows * channels, crossed)
-        next_mark = early_state[0]
-    normed_parts = run(
-        functools.partial(normed_kernel, chunks), "normed", 4 * count * channels * width,
-        [
-            (LOOSE, next_mark), (WHOLE, gate_grad), (WHOLE, value_raw_grad),
-            (WHOLE, state_raw_grad), (own_width, gate_weight), (own_width, value_weight),
-            (own_width, state_weight), (WHOLE, crossed),
-        ],
-        [(LEADING, (head_size, count + HALO, own_width), BF16)],
-        steps=head_size,
-    )[0]
-    if chips == 4:
-        early_gate, early_out = square_end(
-            "early", early_state,
-            [(WHOLE, (step, channels), BF16), (WHOLE, (early_rows - step, channels), BF16)],
-            early_rows * channels, normed_parts,
-        )
-    else:
-        early_gate, early_out = early_state[0][:step], early_state[0][step:]
+    early_state, half_mark = sum_pieces(
+        chip, early_kept, early_given, "early", True, step, False, (crossed,)
+    )
     lanes = channels // 128
     state_rows = 2 * step // lanes
     late_rows = step + state_rows + HALO
     late_kept, late_given = run(
         late_kernel, "late", 3 * count * channels * width,
         [
-            (LOOSE, early_gate), core, (feature_block, normed), (WHOLE, value_raw_grad),
+            (LOOSE, half_mark), core, (feature_block, normed), (WHOLE, value_raw_grad),
             (WHOLE, state_raw_grad),
             (WHOLE, value_small), (WHOLE, gate_small), (((1, BLOCK), lambda i: (0, i)), early_gain),
             (WHOLE, state_small), (BLOCK, value_weight), (BLOCK, state_weight),
@@ -1176,12 +1151,39 @@
             pltpu.VMEM((8, width), F32),
         ],
     )
+    made = []
+
+    def make_normed(mark):
+        made.extend(
+            run(
+                functools.partial(normed_kernel, chunks), "normed", 4 * count * channels * width,
+                [
+                    (LOOSE, mark), (WHOLE, gate_grad), (WHOLE, value_raw_grad),
+                    (WHOLE, state_raw_grad), (own_width, gate_weight), (own_width, value_weight),
+                    (own_width, state_weight), (WHOLE, crossed),
+                ],
+                [(LEADING, (head_size, count + HALO, own_width), BF16)],
+                steps=head_size,
+            )
+        )
+        return made
+
     (late_piece, shared_piece), late_mark = sum_pieces(
-        chip, late_kept, late_given, "late", False, step, True
-    )
+        chip, late_kept, late_given, "late", False, step, True, meanwhile=make_normed
+    )
+    normed_parts = made[0]
+    shared_piece, heads_mark = heads_sum(shared_piece)
+    if chips == 4:
+        early_state = square_next("early", early_state, early_rows * channels, late_piece)
+    if chips == 4:
+        early_gate, early_out = square_end(
+            "early", early_state,
+            [(WHOLE, (step, channels), BF16), (WHOLE, (early_rows - step, channels), BF16)],
+            early_rows * channels, heads_mark,
+        )
+    else:
+        early_gate, early_out = early_state[0][:step], early_state[0][step:]
     normed_parts = deal(normed_parts, "head")
-    shared_piece = heads_sum(shared_piece)
-
     def unpack(kernel, name, pieces, outs, flops, scratch, extra=(), args=()):
         groups = [collect(*piece) for piece in pieces]
         bits = [[found[2] for found in group] for group in groups]
@@ -1195,7 +1197,7 @@
     gate_weight_gradient, output_weight_gradient = unpack(
         early_out_kernel, "early_out",
         [(early_gate, (2, 1), late_mark), (early_out, (1, 2), late_mark)],
-        [(LOOSE, (width, channels), F32), (LOOSE, (channels, width), F32)], 4 * channels * width,
+        [(FAR, (width, channels), F32), (FAR, (channels, width), F32)], 4 * channels * width,
         [
             pltpu.VMEM((seq_size, step, channels), F32),
             pltpu.VMEM((seq_size, out_rows, width), F32),
@@ -1205,7 +1207,7 @@
     )
     value_weight_gradient = unpack(
         late_out_kernel, "late_out", [(late_piece, None)],
-        [(LOOSE, (width, channels), F32)], 2 * channels * width,
+        [(FAR, (width, channels), F32)], 2 * channels * width,
         [pltpu.VMEM((seq_size, step, channels), F32), sems],
     )[0]
     (
@@ -1214,7 +1216,7 @@
     ) = unpack(
         shared_out_kernel, "shared_out", [(shared_piece, (2, 1))],
         [
-            (LOOSE, (width, maps_width), F32),
+            (FAR, (width, maps_width), F32),
             (WHOLE, (KERNEL, channels), F32),
             (WHOLE, (channels,), F32),
             (WHOLE, (KERNEL, maps_width), F32),
@@ -1231,7 +1233,7 @@
             pltpu.VMEM((HALO, channels), F32),
         ],
         extra=(head_size,),
-        args=[head, (LOOSE, gate_weight_gradient)],
+        args=[head],
     )
     tokens_gradient = run(
         functools.partial(last_kernel, float(width)), "last", count * own_width * 20,

time: 274 us -> 276 us (level)
  starting transfers between devices: 64.9 us -> 77.8 us
  waiting for transfers between devices: 101 us -> 96.6 us
  Pallas kernels: 69.3 us -> 66.5 us
    ppermute x2, waiting for transfers between devices: 17.8 us -> 10 us  [heads_sum(): arrived = lax.ppermute(low, 'head', [(i, i ^ bits) for i in range(size)])]
    ppermute x16, starting transfers between devices: 15.2 us -> 22.5 us  [beside(): return lax.ppermute(value, 'core', [(0, 1), (1, 0)])]
    all_to_all x3, waiting for transfers between devices: 1.8 us -> 8.3 us  [deal(): return lax.all_to_all(parts, axis, 0, 0)]
    ppermute x2, starting transfers between devices: 1.27 us -> 5.14 us  [heads_sum(): arrived = lax.ppermute(low, 'head', [(i, i ^ bits) for i in range(size)])]
    ppermute x22, waiting for transfers between devices: 46.8 us -> 43.3 us  [cross(): lax.ppermute(value, 'chip', [(i, i ^ bits) for i in range(lax.axis_size('...]
    pallas_call x30, Pallas kernels: 69.3 us -> 66.5 us  [run(): pl.pallas_call(kernel, out_shape=shapes, in_specs=[spec(kind, a.shape) fo...]
    unnamed x195 -> x147, local copies, waits for them, and re-layouts: 22.1 us -> 19.4 us
  transfers between devices with their start and end apart: 52 -> 52, of which waited for: 25 -> 24; matrix products, arithmetic and copies ran while one was open for 4% -> 4% of each run, Pallas kernels for 18% -> 15%
where the time goes in v3:
time: 276 us; the launch traced here: 275 us
  waiting for transfers between devices  96.6 us (35%)
  starting transfers between devices  77.8 us (28%)
  Pallas kernels  66.5 us (24%)
  local copies, waits for them, and re-layouts  23 us (8%)
  other arithmetic  5.55 us (2%)
  matrix products  3.44 us (1%)
    pallas_call x30, Pallas kernels, run(): pl.pallas_call(kernel, out_shape=shapes, in_specs=[spec(kind, a.shape) fo...  66.5 us
    ppermute x22, waiting for transfers between devices, cross(): lax.ppermute(value, 'chip', [(i, i ^ bits) for i in range(lax.axis_size('...  43.3 us
    ppermute x16, starting transfers between devices, beside(): return lax.ppermute(value, 'core', [(0, 1), (1, 0)])  22.5 us
    ppermute x22, starting transfers between devices, cross(): lax.ppermute(value, 'chip', [(i, i ^ bits) for i in range(lax.axis_size('...  19.5 us
    unnamed x147, local copies, waits for them, and re-layouts  19.4 us
    ppermute x4, waiting for transfers between devices, turn(): lax.ppermute(value, axis, [(i, (i + by) % size) for i in range(size)])  15.9 us
    all_to_all x3, starting transfers between devices, deal(): return lax.all_to_all(parts, axis, 0, 0)  12.4 us
    ppermute x2, waiting for transfers between devices, heads_sum(): arrived = lax.ppermute(low, 'head', [(i, i ^ bits) for i in range(size)])  10 us
  transfers between devices with their start and end apart: 52, of which 24 were waited for; matrix products, arithmetic and copies ran while one was open for 4% of the time, Pallas kernels for 15%

profile of v3, /device:TPU:1, one launch (start us, length us, event | category | flops | bytes accessed | tf_op | source)
XLA Modules:
  0.0 274.5 jit_solution(10776595400926700817)
XLA Ops:
  1.4 4.5 %collective-permute-start = (bf16[16,384]{1,0:T(8,128)(2,1)S(1)}, bf16[16,384]{1,0:T(8,128)(2,1)S(1)}, u32[]{:S(2)}, u32[]{:S(2)}) collective-permute-start(bf16[16,384]{1,0:T(8,128)(2,1)S(1)} %slice_bitcast_fusion), channel_id=1, source_target_pairs={{0,4},{4,8},{8,12},{12,16},{16,20},{20,24},{24,28},{1,5},{5,9},{9,... | collective-permute-start | bytes 36872 | tf_op jit(solution)/shard_map/ppermute | solution.py:46
  10.8 3.2 %collective-permute-start.3 = (bf16[544,384]{1,0:T(8,128)(2,1)S(1)}, bf16[544,384]{1,0:T(8,128)(2,1)S(1)}, u32[]{:S(2)}, u32[]{:S(2)}) collective-permute-start(bf16[544,384]{1,0:T(8,128)(2,1)S(1)} %pad_maximum_fusion.2.refs_0_.refs_4_), channel_id=1, source_target_pairs={{0,1},{1,2},{2,3},{4,5},{5,6},{6,7},{8,9},{9,10},{10,11},{12,13},{... | collective-permute-start | bytes 1253384 | tf_op jit(solution)/shard_map/ppermute | solution.py:67
  15.3 14.4 %collective-permute-done.1.refs_2_.refs_6_ = bf16[544,384]{1,0:T(8,128)(2,1)S(1)} collective-permute-done((bf16[544,384]{1,0:T(8,128)(2,1)S(1)}, bf16[544,384]{1,0:T(8,128)(2,1)S(1)}, u32[]{:S(2)}, u32[]{:S(2)}) %collective-permute-start.1) | collective-permute-done | bytes 417824 | tf_op jit(solution)/shard_map/ppermute | solution.py:55
  31.0 4.0 %collective-permute-done.4.refs_3_.refs_7_ = bf16[544,384]{1,0:T(8,128)(2,1)S(1)} collective-permute-done((bf16[544,384]{1,0:T(8,128)(2,1)S(1)}, bf16[544,384]{1,0:T(8,128)(2,1)S(1)}, u32[]{:S(2)}, u32[]{:S(2)}) %collective-permute-start.4) | collective-permute-done | bytes 417824 | tf_op jit(solution)/shard_map/ppermute | solution.py:68
  35.8 7.7 %collective-permute-done.2.passed_ref.refs_8_ = bf16[544,384]{1,0:T(8,128)(2,1)S(1)} collective-permute-done((bf16[544,384]{1,0:T(8,128)(2,1)S(1)}, bf16[544,384]{1,0:T(8,128)(2,1)S(1)}, u32[]{:S(2)}, u32[]{:S(2)}) %collective-permute-start.2) | collective-permute-done | bytes 417824 | tf_op jit(solution)/shard_map/ppermute | solution.py:69
  50.0 4.5 %all-to-all-start = ((bf16[4,512,384]{2,1,0:T(8,128)(2,1)}), bf16[4,512,384]{2,1,0:T(8,128)(2,1)}, u32[]{:S(2)}, u32[]{:S(2)}) async-start(bf16[4,512,384]{2,1,0:T(8,128)(2,1)} %copies.1), calls=%async_computation | async-start | bytes 3145728 | tf_op jit(solution)/shard_map/all_to_all | solution.py:74
  58.8 4.1 %conv.1 = (bf16[512,768]{1,0:T(8,128)(2,1)S(1)}, bf16[512,768]{1,0:T(8,128)(2,1)S(1)}, f32[512,768]{1,0:T(8,128)S(1)}, bf16[512,256]{1,0:T(8,128)(2,1)S(1)}, f32...) custom-call(bf16[544,768]{1,0:T(8,128)(2,1)S(1)} %convolution_convert_fusion.value_ref.value_raw_ref, ...), custom_call_target="tpu_custom_call" | custom-call | flops 157286400 | bytes 5523456 | tf_op jit(solution)/shard_map/conv/pallas_call | solution.py:944
  69.6 4.7 %collective-permute-done.6.refs_1_ = f32[72,768]{1,0:T(8,128)} collective-permute-done((f32[72,768]{1,0:T(8,128)}, f32[72,768]{1,0:T(8,128)}, u32[]{:S(2)}, u32[]{:S(2)}) %collective-permute-start.6) | collective-permute-done | bytes 221216 | tf_op jit(solution)/shard_map/ppermute | solution.py:78
  75.1 4.9 %collective-permute-done.8.refs_3_ = f32[72,768]{1,0:T(8,128)} collective-permute-done((f32[72,768]{1,0:T(8,128)}, f32[72,768]{1,0:T(8,128)}, u32[]{:S(2)}, u32[]{:S(2)}) %collective-permute-start.8) | collective-permute-done | bytes 221216 | tf_op jit(solution)/shard_map/ppermute | solution.py:78
  87.6 3.7 %all-to-all-done.parts_ref = bf16[4,512,384]{2,1,0:T(8,128)(2,1)} async-done(((bf16[4,512,384]{2,1,0:T(8,128)(2,1)}), bf16[4,512,384]{2,1,0:T(8,128)(2,1)}, u32[]{:S(2)}, u32[]{:S(2)}) %all-to-all-start) | async-done | bytes 1572896 | tf_op jit(solution)/shard_map/all_to_all | solution.py:74
  103.2 3.7 %gate.1 = (bf16[512,768]{1,0:T(8,128)(2,1)S(1)}, bf16[512,768]{1,0:T(8,128)(2,1)S(1)}, f32[512,768]{1,0:T(8,128)S(1)}, f32[8,768]{1,0:T(8,128)S(1)}, f32[136,768]{1,0:T(8,128)S(1)}, /*index=5*/f32[8,512]{1,0:T(8,128)S(1)}) custom-call(f32[8,512]{1,0:T(8,128)S(1)} %get-tuple-element.87.refs_0_, f32[8,512]{1,0:T(8,128)S(1)} %collective-permute-done.10.refs_1_, ...), custom_call_target="tpu_custom_call" | custom-call | flops 235929600 | bytes 9487872 | tf_op jit(solution)/shard_map/gate/pallas_call | solution.py:944
  115.4 4.4 %collective-permute-done.14.refs_1_ = f32[72,768]{1,0:T(8,128)S(1)} collective-permute-done((f32[72,768]{1,0:T(8,128)S(1)}, f32[72,768]{1,0:T(8,128)S(1)}, u32[]{:S(2)}, u32[]{:S(2)}) %collective-permute-start.14) | collective-permute-done | bytes 221216 | tf_op jit(solution)/shard_map/ppermute | solution.py:78
  119.8 4.8 %collective-permute-done.16.refs_3_ = f32[72,768]{1,0:T(8,128)S(1)} collective-permute-done((f32[72,768]{1,0:T(8,128)S(1)}, f32[72,768]{1,0:T(8,128)S(1)}, u32[]{:S(2)}, u32[]{:S(2)}) %collective-permute-start.16) | collective-permute-done | bytes 221216 | tf_op jit(solution)/shard_map/ppermute | solution.py:78
  127.0 5.6 %back.1 = (f32[512,768]{1,0:T(8,128)S(1)}, f32[512,256]{1,0:T(8,128)S(1)}) custom-call(f32[128,768]{1,0:T(8,128)S(1)} %after_enter.1.state_in_ref, f32[512,768]{1,0:T(8,128)S(1)} %get-tuple-element.91.mixer_grad_ref, f32[512,12]{1,0:T(8,128)S(1)} %get-tuple-element.85.e_ref.refs_9_, f32[512,12]{1,0:T(8,128)S(1)} %copy-done.44, ...), custom_call_target="tpu_custom_call" | custom-call | flops 786432000 | bytes 8858624 | tf_op jit(solution)/shard_map/back/pallas_call | solution.py:944
  132.6 6.6 %early.1 = (bf16[4,384,768]{2,1,0:T(8,128)(2,1)S(1)}, bf16[4,384,768]{2,1,0:T(8,128)(2,1)}, f32[1,1536]{1,0:T(1,128)S(1)}) custom-call(f32[512,768]{1,0:T(8,128)S(1)} %get-tuple-element.96.loose_ref.value_ref, s32[1]{0:T(128)} %bitcast.core_ref, bf16[544,1536]{1,0:T(8,128)(2,1)S(1)} %get-tuple-element.78.loose_ref.normed_ref, ...), custom_call_target="tpu_custom_call" | custom-call | flops 2415919104 | bytes 11900932 | tf_op jit(solution)/shard_map/early/pallas_call | solution.py:944
  141.1 4.4 %all-to-all-start.1 = ((bf16[4,512,384]{2,1,0:T(8,128)(2,1)}), bf16[4,512,384]{2,1,0:T(8,128)(2,1)}, u32[]{:S(2)}, u32[]{:S(2)}) async-start(bf16[4,512,384]{2,1,0:T(8,128)(2,1)} %out.1.refs_0_), calls=%async_computation.1 | async-start | bytes 3145728 | tf_op jit(solution)/shard_map/all_to_all | solution.py:74
  148.5 3.3 %collective-permute-done.19.after_ref = f32[8,1024]{1,0:T(8,128)S(1)} collective-permute-done((f32[8,1024]{1,0:T(8,128)S(1)}, f32[8,1024]{1,0:T(8,128)S(1)}, u32[]{:S(2)}, u32[]{:S(2)}) %collective-permute-start.19) | collective-permute-done | bytes 32800 | tf_op jit(solution)/shard_map/ppermute | solution.py:46
  153.2 3.5 %conv_back.1 = (bf16[512,768]{1,0:T(8,128)(2,1)S(1)}, bf16[512,256]{1,0:T(8,128)(2,1)S(1)}, f32[8,768]{1,0:T(8,128)S(1)}, f32[8,256]{1,0:T(8,128)S(1)}, f32[8,512]{1,0:T(8,128)S(1)}) custom-call(bf16[4,384,768]{2,1,0:T(8,128)(2,1)} %get-tuple-element.100.early_ref, f32[512,768]{1,0:T(8,128)S(1)} %copy-done.32, f32[512,256]{1,0:T(8,128)S(1)} %get-tuple-element.101.map_ref, ...), custom_call_target="tpu_custom_call" | custom-call | flops 39321600 | bytes 4366336 | tf_op jit(solution)/shard_map/conv_back/pallas_call | solution.py:944
  156.8 3.1 %early_half.1 = (f32[2,192,768]{2,1,0:T(8,128)S(1)}, bf16[2,192,768]{2,1,0:T(8,128)(2,1)}, f32[2,192,768]{2,1,0:T(8,128)S(1)}, bf16[2,192,768]{2,1,0:T(8,128)(2,1)}) custom-call(s32[1]{0:T(128)} %bitcast.5.chip_ref, bf16[4,384,768]{2,1,0:T(8,128)(2,1)S(1)} %copy-done.21, bf16[4,384,768]{2,1,0:T(8,128)(2,1)} %collective-permute-done.18.arrived_ref, ...), custom_call_target="tpu_custom_call" | custom-call | flops 1179648 | bytes 8257540 | tf_op jit(solution)/shard_map/early_half/pallas_call | solution.py:944
  159.9 4.0 %late.1 = (bf16[4,272,768]{2,1,0:T(8,128)(2,1)S(1)}, bf16[4,272,768]{2,1,0:T(8,128)(2,1)S(1)}) custom-call(f32[2,192,768]{2,1,0:T(8,128)S(1)} %get-tuple-element.104.early_ref.first_ref, s32[1]{0:T(128)} %bitcast.core_ref, bf16[544,1536]{1,0:T(8,128)(2,1)S(1)} %get-tuple-element.78.loose_ref.normed_ref, ...), custom_call_target="tpu_custom_call" | custom-call | flops 1811939328 | bytes 9320452 | tf_op jit(solution)/shard_map/late/pallas_call | solution.py:944
  172.2 5.4 %normed.1.refs_4_ = bf16[4,528,384]{2,1,0:T(8,128)(2,1)} custom-call(f32[272,768]{1,0:T(8,128)S(1)} %get-tuple-element.114.late_ref.refs_0_.refs_1_, bf16[512,768]{1,0:T(8,128)(2,1)S(1)} %copy-done.46, bf16[512,768]{1,0:T(8,128)(2,1)S(1)} %get-tuple-element.105.value_ref.value_grad_ref, bf16[512,256]{1,0:T(8,128)(2,1)S(1)} %get-tuple-element.106.state_ref.state_grad_ref, ...), custom_call_target="tpu_custom_call" | custom-call | flops 2415919104 | bytes 8978432 | tf_op jit(solution)/shard_map/normed/pallas_call | solution.py:944
  177.5 4.6 %all-to-all-done.1 = bf16[4,512,384]{2,1,0:T(8,128)(2,1)} async-done(((bf16[4,512,384]{2,1,0:T(8,128)(2,1)}), bf16[4,512,384]{2,1,0:T(8,128)(2,1)}, u32[]{:S(2)}, u32[]{:S(2)}) %all-to-all-start.1) | async-done | bytes 1572896 | tf_op jit(solution)/shard_map/all_to_all | solution.py:74
  182.1 3.6 %all-to-all-start.2 = ((bf16[4,528,384]{2,1,0:T(8,128)(2,1)}), bf16[4,528,384]{2,1,0:T(8,128)(2,1)S(1)}, u32[]{:S(2)}, u32[]{:S(2)}) async-start(bf16[4,528,384]{2,1,0:T(8,128)(2,1)} %normed.1.refs_4_), calls=%async_computation.2 | async-start | bytes 3244032 | tf_op jit(solution)/shard_map/all_to_all | solution.py:74
  189.5 9.0 %collective-permute-done.22.refs_2_ = bf16[272,768]{1,0:T(8,128)(2,1)S(1)} collective-permute-done((bf16[272,768]{1,0:T(8,128)(2,1)}, bf16[272,768]{1,0:T(8,128)(2,1)S(1)}, u32[]{:S(2)}, u32[]{:S(2)}) %collective-permute-start.22) | collective-permute-done | bytes 417824 | tf_op jit(solution)/shard_map/ppermute | solution.py:78
  206.3 7.3 %collective-permute-done.24.arrived_ref = bf16[80,768]{1,0:T(8,128)(2,1)S(1)} collective-permute-done((bf16[80,768]{1,0:T(8,128)(2,1)S(1)}, bf16[80,768]{1,0:T(8,128)(2,1)S(1)}, u32[]{:S(2)}, u32[]{:S(2)}) %collective-permute-start.24) | collective-permute-done | bytes 122912 | tf_op jit(solution)/shard_map/ppermute | solution.py:89
  222.5 3.7 %collective-permute-start.25 = (bf16[80,768]{1,0:T(8,128)(2,1)S(1)}, bf16[80,768]{1,0:T(8,128)(2,1)S(1)}, u32[]{:S(2)}, u32[]{:S(2)}) collective-permute-start(bf16[80,768]{1,0:T(8,128)(2,1)S(1)} %get-tuple-element.121.loose_ref), channel_id=1, source_target_pairs={{0,2},{1,3},{2,0},{3,1},{4,6},{5,7},{6,4},{7,5},{8,10},{9,11},{10,... | collective-permute-start | bytes 368648 | tf_op jit(solution)/shard_map/ppermute | solution.py:89
  231.9 6.7 %collective-permute-start.44 = (bf16[1,192,768]{2,1,0:T(8,128)(2,1)}, bf16[1,192,768]{2,1,0:T(8,128)(2,1)S(1)}, u32[]{:S(2)}, u32[]{:S(2)}) collective-permute-start(bf16[1,192,768]{2,1,0:T(8,128)(2,1)} %bitcast.16.refs_2_), channel_id=1, source_target_pairs={{0,4},{4,0},{1,5},{5,1},{2,6},{6,2},{3,7},{7,3},{8,12},{12,8},{9,1... | collective-permute-start | bytes 884744 | tf_op jit(solution)/shard_map/ppermute | solution.py:50
  242.0 5.9 %collective-permute-done.26 = bf16[80,768]{1,0:T(8,128)(2,1)S(1)} collective-permute-done((bf16[80,768]{1,0:T(8,128)(2,1)S(1)}, bf16[80,768]{1,0:T(8,128)(2,1)S(1)}, u32[]{:S(2)}, u32[]{:S(2)}) %collective-permute-start.26) | collective-permute-done | bytes 122912 | tf_op jit(solution)/shard_map/ppermute | solution.py:78
  248.0 4.5 %collective-permute-start.48 = (bf16[1,192,768]{2,1,0:T(8,128)(2,1)}, bf16[1,192,768]{2,1,0:T(8,128)(2,1)S(1)}, u32[]{:S(2)}, u32[]{:S(2)}) collective-permute-start(bf16[1,192,768]{2,1,0:T(8,128)(2,1)} %bitcast.18.refs_6_), channel_id=1, source_target_pairs={{0,4},{4,0},{1,5},{5,1},{2,6},{6,2},{3,7},{7,3},{8,12},{12,8},{9,1... | collective-permute-start | bytes 884744 | tf_op jit(solution)/shard_map/ppermute | solution.py:50
  257.6 4.6 %collective-permute-done.28.refs_2_ = bf16[2,80,768]{2,1,0:T(8,128)(2,1)S(1)} collective-permute-done((bf16[2,80,768]{2,1,0:T(8,128)(2,1)S(1)}, bf16[2,80,768]{2,1,0:T(8,128)(2,1)S(1)}, u32[]{:S(2)}, u32[]{:S(2)}) %collective-permute-start.28) | collective-permute-done | bytes 245792 | tf_op jit(solution)/shard_map/ppermute | solution.py:78
  264.0 3.5 %late_out.1 = f32[1536,768]{1,0:T(8,128)} custom-call(s32[1]{0:T(128)} %bitcast.core_ref, s32[1]{0:T(128)} %bitcast.5.chip_ref, bf16[1,192,768]{2,1,0:T(8,128)(2,1)S(1)} %bitcast.35, bf16[1,192,768]{2,1,0:T(8,128)(2,1)S(1)} %collective-permute-done.42.refs_1_, bf16[1,192,768]{2,1,0:T(8,128)(2,1)} %bitcast.16.refs_2_, ...), custom_call_target="tpu_custom_call" | custom-call | flops 2359296 | bytes 7077896 | tf_op jit(solution)/shard_map/late_out/pallas_call | solution.py:944
  269.4 3.8 %early_out.1 = (f32[1536,768]{1,0:T(8,128)}, f32[768,1536]{1,0:T(8,128)}) custom-call(s32[1]{0:T(128)} %bitcast.core_ref, s32[1]{0:T(128)} %bitcast.5.chip_ref, bf16[2,192,768]{2,1,0:T(8,128)(2,1)S(1)} %copy-done.3, bf16[2,192,768]{2,1,0:T(8,128)(2,1)S(1)} %collective-permute-done.35.refs_1_, bf16[2,192,768]{2,1,0:T(8,128)(2,1)S(1)} %collective-permute-done.36.refs_2_, ...), custom_call_target="tpu_custom_call" | custom-call | flops 4718592 | bytes 14155784 | tf_op jit(solution)/shard_map/early_out/pallas_call | solution.py:944
  (273 shorter events, 111.3 us)
Async XLA Ops:
  8.4 21.3 %collective-permute-start.1 = (bf16[544,384]{1,0:T(8,128)(2,1)S(1)}, bf16[544,384]{1,0:T(8,128)(2,1)S(1)}, u32[]{:S(2)}, u32[]{:S(2)}) collective-permute-start(bf16[544,384]{1,0:T(8,128)(2,1)S(1)} %pad_maximum_fusion.2.refs_0_.refs_4_), channel_id=1, source_target_pairs={{0,2},{1,3},{2,0},{3,1},{4,6},{5,7},{6,4},{7,5},{8,10},{9,11},{10,... | collective-permute-start | bytes 1253384 | tf_op jit(solution)/shard_map/ppermute | solution.py:55
  10.8 20.3 %collective-permute-start.3 = (bf16[544,384]{1,0:T(8,128)(2,1)S(1)}, bf16[544,384]{1,0:T(8,128)(2,1)S(1)}, u32[]{:S(2)}, u32[]{:S(2)}) collective-permute-start(bf16[544,384]{1,0:T(8,128)(2,1)S(1)} %pad_maximum_fusion.2.refs_0_.refs_4_), channel_id=1, source_target_pairs={{0,1},{1,2},{2,3},{4,5},{5,6},{6,7},{8,9},{9,10},{10,11},{12,13},{... | collective-permute-start | bytes 1253384 | tf_op jit(solution)/shard_map/ppermute | solution.py:67
  14.0 21.1 %collective-permute-start.4 = (bf16[544,384]{1,0:T(8,128)(2,1)S(1)}, bf16[544,384]{1,0:T(8,128)(2,1)S(1)}, u32[]{:S(2)}, u32[]{:S(2)}) collective-permute-start(bf16[544,384]{1,0:T(8,128)(2,1)S(1)} %pad_maximum_fusion.2.refs_0_.refs_4_), channel_id=1, source_target_pairs={{1,0},{2,1},{3,2},{5,4},{6,5},{7,6},{9,8},{10,9},{11,10},{13,12},{... | collective-permute-start | bytes 1253384 | tf_op jit(solution)/shard_map/ppermute | solution.py:68
  29.7 13.8 %collective-permute-start.2 = (bf16[544,384]{1,0:T(8,128)(2,1)S(1)}, bf16[544,384]{1,0:T(8,128)(2,1)S(1)}, u32[]{:S(2)}, u32[]{:S(2)}) collective-permute-start(bf16[544,384]{1,0:T(8,128)(2,1)S(1)} %collective-permute-done.1.refs_2_.refs_6_), channel_id=1, source_target_pairs={{2,3},{1,0},{6,7},{5,4},{10,11},{9,8},{14,15},{13,12},{18,19},{17,... | collective-permute-start | bytes 1253384 | tf_op jit(solution)/shard_map/ppermute | solution.py:69
  50.0 41.3 %all-to-all-start = ((bf16[4,512,384]{2,1,0:T(8,128)(2,1)}), bf16[4,512,384]{2,1,0:T(8,128)(2,1)}, u32[]{:S(2)}, u32[]{:S(2)}) async-start(bf16[4,512,384]{2,1,0:T(8,128)(2,1)} %copies.1), calls=%async_computation | async-start | bytes 3145728 | tf_op jit(solution)/shard_map/all_to_all | solution.py:74
  66.3 7.9 %collective-permute-start.6 = (f32[72,768]{1,0:T(8,128)}, f32[72,768]{1,0:T(8,128)}, u32[]{:S(2)}, u32[]{:S(2)}) collective-permute-start(f32[72,768]{1,0:T(8,128)} %before_pair.1.refs_0_), channel_id=1, source_target_pairs={{0,8},{8,0},{16,24},{24,16},{1,9},{9,1},{17,25},{25,17},{2,10},{10... | collective-permute-start | bytes 663560 | tf_op jit(solution)/shard_map/ppermute | solution.py:78
  68.4 11.5 %collective-permute-start.8 = (f32[72,768]{1,0:T(8,128)}, f32[72,768]{1,0:T(8,128)}, u32[]{:S(2)}, u32[]{:S(2)}) collective-permute-start(f32[72,768]{1,0:T(8,128)} %before_pair.1.refs_0_), channel_id=1, source_target_pairs={{0,24},{8,16},{16,8},{24,0},{1,25},{9,17},{17,9},{25,1},{2,26},{10... | collective-permute-start | bytes 663560 | tf_op jit(solution)/shard_map/ppermute | solution.py:78
  113.1 11.5 %collective-permute-start.16 = (f32[72,768]{1,0:T(8,128)S(1)}, f32[72,768]{1,0:T(8,128)S(1)}, u32[]{:S(2)}, u32[]{:S(2)}) collective-permute-start(f32[72,768]{1,0:T(8,128)S(1)} %after_pair.1.refs_0_), channel_id=1, source_target_pairs={{0,24},{8,16},{16,8},{24,0},{1,25},{9,17},{17,9},{25,1},{2,26},{10... | collective-permute-start | bytes 663560 | tf_op jit(solution)/shard_map/ppermute | solution.py:78
  140.7 16.1 %collective-permute-start.18 = (bf16[4,384,768]{2,1,0:T(8,128)(2,1)}, bf16[4,384,768]{2,1,0:T(8,128)(2,1)}, u32[]{:S(2)}, u32[]{:S(2)}) collective-permute-start(bf16[4,384,768]{2,1,0:T(8,128)(2,1)} %get-tuple-element.100.early_ref), channel_id=1, source_target_pairs={{0,4},{4,0},{1,5},{5,1},{2,6},{6,2},{3,7},{7,3},{8,12},{12,8},{9,1... | collective-permute-start | bytes 7077896 | tf_op jit(solution)/shard_map/ppermute | solution.py:50
  141.1 41.1 %all-to-all-start.1 = ((bf16[4,512,384]{2,1,0:T(8,128)(2,1)}), bf16[4,512,384]{2,1,0:T(8,128)(2,1)}, u32[]{:S(2)}, u32[]{:S(2)}) async-start(bf16[4,512,384]{2,1,0:T(8,128)(2,1)} %out.1.refs_0_), calls=%async_computation.1 | async-start | bytes 3145728 | tf_op jit(solution)/shard_map/all_to_all | solution.py:74
  164.1 38.4 %collective-permute-start.30 = (bf16[2,192,768]{2,1,0:T(8,128)(2,1)}, bf16[2,192,768]{2,1,0:T(8,128)(2,1)}, u32[]{:S(2)}, u32[]{:S(2)}) collective-permute-start(bf16[2,192,768]{2,1,0:T(8,128)(2,1)} %get-tuple-element.124), channel_id=1, source_target_pairs={{0,8},{8,0},{16,24},{24,16},{1,9},{9,1},{17,25},{25,17},{2,10},{10... | collective-permute-start | bytes 1769480 | tf_op jit(solution)/shard_map/ppermute | solution.py:78
  166.2 36.3 %collective-permute-start.31 = (bf16[2,192,768]{2,1,0:T(8,128)(2,1)}, bf16[2,192,768]{2,1,0:T(8,128)(2,1)}, u32[]{:S(2)}, u32[]{:S(2)}) collective-permute-start(bf16[2,192,768]{2,1,0:T(8,128)(2,1)} %get-tuple-element.126), channel_id=1, source_target_pairs={{0,16},{8,24},{16,0},{24,8},{1,17},{9,25},{17,1},{25,9},{2,18},{10... | collective-permute-start | bytes 1769480 | tf_op jit(solution)/shard_map/ppermute | solution.py:78
  168.9 19.9 %collective-permute-start.21 = (bf16[272,768]{1,0:T(8,128)(2,1)}, bf16[272,768]{1,0:T(8,128)(2,1)S(1)}, u32[]{:S(2)}, u32[]{:S(2)}) collective-permute-start(bf16[272,768]{1,0:T(8,128)(2,1)} %get-tuple-element.116), channel_id=1, source_target_pairs={{0,8},{8,0},{16,24},{24,16},{1,9},{9,1},{17,25},{25,17},{2,10},{10... | collective-permute-start | bytes 1253384 | tf_op jit(solution)/shard_map/ppermute | solution.py:78
  171.0 27.5 %collective-permute-start.22 = (bf16[272,768]{1,0:T(8,128)(2,1)}, bf16[272,768]{1,0:T(8,128)(2,1)S(1)}, u32[]{:S(2)}, u32[]{:S(2)}) collective-permute-start(bf16[272,768]{1,0:T(8,128)(2,1)} %get-tuple-element.117), channel_id=1, source_target_pairs={{0,16},{8,24},{16,0},{24,8},{1,17},{9,25},{17,1},{25,9},{2,18},{10... | collective-permute-start | bytes 1253384 | tf_op jit(solution)/shard_map/ppermute | solution.py:78
  171.0 28.3 %collective-permute-start.23 = (bf16[272,768]{1,0:T(8,128)(2,1)}, bf16[272,768]{1,0:T(8,128)(2,1)}, u32[]{:S(2)}, u32[]{:S(2)}) collective-permute-start(bf16[272,768]{1,0:T(8,128)(2,1)} %get-tuple-element.118), channel_id=1, source_target_pairs={{0,24},{8,16},{16,8},{24,0},{1,25},{9,17},{17,9},{25,1},{2,26},{10... | collective-permute-start | bytes 1253384 | tf_op jit(solution)/shard_map/ppermute | solution.py:78
  182.1 91.1 %all-to-all-start.2 = ((bf16[4,528,384]{2,1,0:T(8,128)(2,1)}), bf16[4,528,384]{2,1,0:T(8,128)(2,1)S(1)}, u32[]{:S(2)}, u32[]{:S(2)}) async-start(bf16[4,528,384]{2,1,0:T(8,128)(2,1)} %normed.1.refs_4_), calls=%async_computation.2 | async-start | bytes 3244032 | tf_op jit(solution)/shard_map/all_to_all | solution.py:74
  204.0 9.7 %collective-permute-start.32 = (bf16[192,768]{1,0:T(8,128)(2,1)S(1)}, bf16[192,768]{1,0:T(8,128)(2,1)S(1)}, u32[]{:S(2)}, u32[]{:S(2)}) collective-permute-start(bf16[192,768]{1,0:T(8,128)(2,1)S(1)} %get-tuple-element.129), channel_id=1, source_target_pairs={{0,16},{8,24},{16,0},{24,8},{1,17},{9,25},{17,1},{25,9},{2,18},{10... | collective-permute-start | bytes 884744 | tf_op jit(solution)/shard_map/ppermute | solution.py:78
  204.1 9.6 %collective-permute-start.33 = (bf16[192,768]{1,0:T(8,128)(2,1)S(1)}, bf16[192,768]{1,0:T(8,128)(2,1)S(1)}, u32[]{:S(2)}, u32[]{:S(2)}) collective-permute-start(bf16[192,768]{1,0:T(8,128)(2,1)S(1)} %get-tuple-element.131), channel_id=1, source_target_pairs={{0,8},{8,0},{16,24},{24,16},{1,9},{9,1},{17,25},{25,17},{2,10},{10... | collective-permute-start | bytes 884744 | tf_op jit(solution)/shard_map/ppermute | solution.py:78
  204.9 8.7 %collective-permute-start.24 = (bf16[80,768]{1,0:T(8,128)(2,1)S(1)}, bf16[80,768]{1,0:T(8,128)(2,1)S(1)}, u32[]{:S(2)}, u32[]{:S(2)}) collective-permute-start(bf16[80,768]{1,0:T(8,128)(2,1)S(1)} %convert_element_type.29), channel_id=1, source_target_pairs={{0,1},{1,0},{2,3},{3,2},{4,5},{5,4},{6,7},{7,6},{8,9},{9,8},{10,11... | collective-permute-start | bytes 368648 | tf_op jit(solution)/shard_map/ppermute | solution.py:89
  214.8 7.7 %collective-permute-start.38 = (bf16[192,768]{1,0:T(8,128)(2,1)S(1)}, bf16[192,768]{1,0:T(8,128)(2,1)S(1)}, u32[]{:S(2)}, u32[]{:S(2)}) collective-permute-start(bf16[192,768]{1,0:T(8,128)(2,1)S(1)} %get-tuple-element.133), channel_id=1, source_target_pairs={{0,8},{8,0},{16,24},{24,16},{1,9},{9,1},{17,25},{25,17},{2,10},{10... | collective-permute-start | bytes 884744 | tf_op jit(solution)/shard_map/ppermute | solution.py:78
  215.3 16.0 %collective-permute-start.42 = (bf16[1,192,768]{2,1,0:T(8,128)(2,1)S(1)}, bf16[1,192,768]{2,1,0:T(8,128)(2,1)S(1)}, u32[]{:S(2)}, u32[]{:S(2)}) collective-permute-start(bf16[1,192,768]{2,1,0:T(8,128)(2,1)S(1)} %bitcast.34), channel_id=1, source_target_pairs={{0,4},{4,0},{1,5},{5,1},{2,6},{6,2},{3,7},{7,3},{8,12},{12,8},{9,1... | collective-permute-start | bytes 884744 | tf_op jit(solution)/shard_map/ppermute | solution.py:50
  217.8 14.1 %collective-permute-start.43 = (bf16[192,768]{1,0:T(8,128)(2,1)S(1)}, bf16[192,768]{1,0:T(8,128)(2,1)}, u32[]{:S(2)}, u32[]{:S(2)}) collective-permute-start(bf16[192,768]{1,0:T(8,128)(2,1)S(1)} %get-tuple-element.127.loose_ref), channel_id=1, source_target_pairs={{0,8},{8,0},{16,24},{24,16},{1,9},{9,1},{17,25},{25,17},{2,10},{10... | collective-permute-start | bytes 884744 | tf_op jit(solution)/shard_map/ppermute | solution.py:78
  218.7 22.5 %collective-permute-start.45 = (bf16[192,768]{1,0:T(8,128)(2,1)S(1)}, bf16[192,768]{1,0:T(8,128)(2,1)}, u32[]{:S(2)}, u32[]{:S(2)}) collective-permute-start(bf16[192,768]{1,0:T(8,128)(2,1)S(1)} %get-tuple-element.127.loose_ref), channel_id=1, source_target_pairs={{0,16},{8,24},{16,0},{24,8},{1,17},{9,25},{17,1},{25,9},{2,18},{10... | collective-permute-start | bytes 884744 | tf_op jit(solution)/shard_map/ppermute | solution.py:78
  220.4 21.3 %collective-permute-start.47 = (bf16[192,768]{1,0:T(8,128)(2,1)S(1)}, bf16[192,768]{1,0:T(8,128)(2,1)}, u32[]{:S(2)}, u32[]{:S(2)}) collective-permute-start(bf16[192,768]{1,0:T(8,128)(2,1)S(1)} %get-tuple-element.127.loose_ref), channel_id=1, source_target_pairs={{0,24},{8,16},{16,8},{24,0},{1,25},{9,17},{17,9},{25,1},{2,26},{10... | collective-permute-start | bytes 884744 | tf_op jit(solution)/shard_map/ppermute | solution.py:78
  230.5 23.8 %collective-permute-start.36 = (bf16[2,192,768]{2,1,0:T(8,128)(2,1)S(1)}, bf16[2,192,768]{2,1,0:T(8,128)(2,1)S(1)}, u32[]{:S(2)}, u32[]{:S(2)}) collective-permute-start(bf16[2,192,768]{2,1,0:T(8,128)(2,1)S(1)} %copy-done.3), channel_id=1, source_target_pairs={{0,8},{8,0},{16,24},{24,16},{1,9},{9,1},{17,25},{25,17},{2,10},{10... | collective-permute-start | bytes 1769480 | tf_op jit(solution)/shard_map/ppermute | solution.py:78
  231.4 23.0 %collective-permute-start.40 = (bf16[2,192,768]{2,1,0:T(8,128)(2,1)}, bf16[2,192,768]{2,1,0:T(8,128)(2,1)S(1)}, u32[]{:S(2)}, u32[]{:S(2)}) collective-permute-start(bf16[2,192,768]{2,1,0:T(8,128)(2,1)} %tie.3.refs_4_), channel_id=1, source_target_pairs={{0,16},{8,24},{16,0},{24,8},{1,17},{9,25},{17,1},{25,9},{2,18},{10... | collective-permute-start | bytes 1769480 | tf_op jit(solution)/shard_map/ppermute | solution.py:78
  231.9 20.6 %collective-permute-start.44 = (bf16[1,192,768]{2,1,0:T(8,128)(2,1)}, bf16[1,192,768]{2,1,0:T(8,128)(2,1)S(1)}, u32[]{:S(2)}, u32[]{:S(2)}) collective-permute-start(bf16[1,192,768]{2,1,0:T(8,128)(2,1)} %bitcast.16.refs_2_), channel_id=1, source_target_pairs={{0,4},{4,0},{1,5},{5,1},{2,6},{6,2},{3,7},{7,3},{8,12},{12,8},{9,1... | collective-permute-start | bytes 884744 | tf_op jit(solution)/shard_map/ppermute | solution.py:50
  241.8 10.8 %collective-permute-start.46 = (bf16[1,192,768]{2,1,0:T(8,128)(2,1)}, bf16[1,192,768]{2,1,0:T(8,128)(2,1)S(1)}, u32[]{:S(2)}, u32[]{:S(2)}) collective-permute-start(bf16[1,192,768]{2,1,0:T(8,128)(2,1)} %bitcast.17.refs_4_), channel_id=1, source_target_pairs={{0,4},{4,0},{1,5},{5,1},{2,6},{6,2},{3,7},{7,3},{8,12},{12,8},{9,1... | collective-permute-start | bytes 884744 | tf_op jit(solution)/shard_map/ppermute | solution.py:50
  252.6 16.8 %collective-permute-start.35 = (bf16[2,192,768]{2,1,0:T(8,128)(2,1)S(1)}, bf16[2,192,768]{2,1,0:T(8,128)(2,1)S(1)}, u32[]{:S(2)}, u32[]{:S(2)}) collective-permute-start(bf16[2,192,768]{2,1,0:T(8,128)(2,1)S(1)} %copy-done.3), channel_id=1, source_target_pairs={{0,4},{4,0},{1,5},{5,1},{2,6},{6,2},{3,7},{7,3},{8,12},{12,8},{9,1... | collective-permute-start | bytes 1769480 | tf_op jit(solution)/shard_map/ppermute | solution.py:50
  253.9 15.5 %collective-permute-start.39 = (bf16[2,192,768]{2,1,0:T(8,128)(2,1)}, bf16[2,192,768]{2,1,0:T(8,128)(2,1)S(1)}, u32[]{:S(2)}, u32[]{:S(2)}) collective-permute-start(bf16[2,192,768]{2,1,0:T(8,128)(2,1)} %tie.3.refs_4_), channel_id=1, source_target_pairs={{0,4},{4,0},{1,5},{5,1},{2,6},{6,2},{3,7},{7,3},{8,12},{12,8},{9,1... | collective-permute-start | bytes 1769480 | tf_op jit(solution)/shard_map/ppermute | solution.py:50
  254.2 15.2 %collective-permute-start.37 = (bf16[2,192,768]{2,1,0:T(8,128)(2,1)S(1)}, bf16[2,192,768]{2,1,0:T(8,128)(2,1)S(1)}, u32[]{:S(2)}, u32[]{:S(2)}) collective-permute-start(bf16[2,192,768]{2,1,0:T(8,128)(2,1)S(1)} %collective-permute-done.36.refs_2_), channel_id=1, source_target_pairs={{0,4},{4,0},{1,5},{5,1},{2,6},{6,2},{3,7},{7,3},{8,12},{12,8},{9,1... | collective-permute-start | bytes 1769480 | tf_op jit(solution)/shard_map/ppermute | solution.py:50
  254.4 15.0 %collective-permute-start.41 = (bf16[2,192,768]{2,1,0:T(8,128)(2,1)S(1)}, bf16[2,192,768]{2,1,0:T(8,128)(2,1)S(1)}, u32[]{:S(2)}, u32[]{:S(2)}) collective-permute-start(bf16[2,192,768]{2,1,0:T(8,128)(2,1)S(1)} %collective-permute-done.40.refs_6_), channel_id=1, source_target_pairs={{0,4},{4,0},{1,5},{5,1},{2,6},{6,2},{3,7},{7,3},{8,12},{12,8},{9,1... | collective-permute-start | bytes 1769480 | tf_op jit(solution)/shard_map/ppermute | solution.py:50
  (93 other events, 529.1 us)

commit v4 on v1

--- a/solution.py
+++ b/solution.py
@@ -856,7 +856,7 @@
         copy.wait()
 
 
-def shared_out_kernel(chips, groups, size, core_ref, chip_ref, head_ref, loose_ref, *refs):
+def shared_out_kernel(chips, groups, size, core_ref, chip_ref, head_ref, *refs):
     (
         state_ref, value_kernel_ref, value_bias_ref, state_kernel_ref, state_bias_ref, skip_ref,
         gated_ref, gain_ref, buffer, sems, own_ref, shared_ref,
@@ -908,6 +908,7 @@
 BLOCKED = "blocked"
 LANES = "lanes"
 LEADING = "leading"
+FAR = "far"
 LOOSE = "loose"
 
 
@@ -921,6 +922,8 @@
             return pl.BlockSpec(memory_space=pltpu.SMEM)
         if kind == LOOSE:
             return pl.BlockSpec(memory_space=pl.ANY)
+        if kind == FAR:
+            return pl.BlockSpec(memory_space=pltpu.HBM)
         if isinstance(kind, tuple):
             return pl.BlockSpec(*kind)
         if steps is None:
@@ -1195,7 +1198,7 @@
     gate_weight_gradient, output_weight_gradient = unpack(
         early_out_kernel, "early_out",
         [(early_gate, (2, 1), late_mark), (early_out, (1, 2), late_mark)],
-        [(LOOSE, (width, channels), F32), (LOOSE, (channels, width), F32)], 4 * channels * width,
+        [(FAR, (width, channels), F32), (FAR, (channels, width), F32)], 4 * channels * width,
         [
             pltpu.VMEM((seq_size, step, channels), F32),
             pltpu.VMEM((seq_size, out_rows, width), F32),
@@ -1205,7 +1208,7 @@
     )
     value_weight_gradient = unpack(
         late_out_kernel, "late_out", [(late_piece, None)],
-        [(LOOSE, (width, channels), F32)], 2 * channels * width,
+        [(FAR, (width, channels), F32)], 2 * channels * width,
         [pltpu.VMEM((seq_size, step, channels), F32), sems],
     )[0]
     (
@@ -1214,7 +1217,7 @@
     ) = unpack(
         shared_out_kernel, "shared_out", [(shared_piece, (2, 1))],
         [
-            (LOOSE, (width, maps_width), F32),
+            (FAR, (width, maps_width), F32),
             (WHOLE, (KERNEL, channels), F32),
             (WHOLE, (channels,), F32),
             (WHOLE, (KERNEL, maps_width), F32),
@@ -1231,7 +1234,7 @@
             pltpu.VMEM((HALO, channels), F32),
         ],
         extra=(head_size,),
-        args=[head, (LOOSE, gate_weight_gradient)],
+        args=[head],
     )
     tokens_gradient = run(
         functools.partial(last_kernel, float(width)), "last", count * own_width * 20,

time: 274 us -> 271 us (0.989)
    unnamed x195 -> x193, local copies, waits for them, and re-layouts: 22.1 us -> 19.8 us
where the time goes in v4:
time: 271 us; the launch traced here: 270 us
  waiting for transfers between devices  101 us (37%)
  Pallas kernels  69.3 us (26%)
  starting transfers between devices  65 us (24%)
  local copies, waits for them, and re-layouts  21.4 us (8%)
  other arithmetic  6.56 us (2%)
  matrix products  5.02 us (2%)
    pallas_call x30, Pallas kernels, run(): pl.pallas_call(kernel, out_shape=shapes, in_specs=[spec(kind, a.shape) fo...  69.3 us
    ppermute x22, waiting for transfers between devices, cross(): lax.ppermute(value, 'chip', [(i, i ^ bits) for i in range(lax.axis_size('...  46.8 us
    unnamed x193, local copies, waits for them, and re-layouts  19.8 us
    ppermute x2, waiting for transfers between devices, heads_sum(): arrived = lax.ppermute(low, 'head', [(i, i ^ bits) for i in range(size)])  17.8 us
    ppermute x22, starting transfers between devices, cross(): lax.ppermute(value, 'chip', [(i, i ^ bits) for i in range(lax.axis_size('...  16.9 us
    ppermute x4, waiting for transfers between devices, turn(): lax.ppermute(value, axis, [(i, (i + by) % size) for i in range(size)])  15.9 us
    ppermute x16, starting transfers between devices, beside(): return lax.ppermute(value, 'core', [(0, 1), (1, 0)])  15.2 us
    all_to_all x3, starting transfers between devices, deal(): return lax.all_to_all(parts, axis, 0, 0)  13.4 us
  transfers between devices with their start and end apart: 52, of which 25 were waited for; matrix products, arithmetic and copies ran while one was open for 4% of the time, Pallas kernels for 18%

profile of v4, /device:TPU:1, one launch (start us, length us, event | category | flops | bytes accessed | tf_op | source)
XLA Modules:
  0.0 270.4 jit_solution(14084162101057619281)
XLA Ops:
  1.4 4.5 %collective-permute-start = (bf16[16,384]{1,0:T(8,128)(2,1)S(1)}, bf16[16,384]{1,0:T(8,128)(2,1)S(1)}, u32[]{:S(2)}, u32[]{:S(2)}) collective-permute-start(bf16[16,384]{1,0:T(8,128)(2,1)S(1)} %slice_bitcast_fusion), channel_id=1, source_target_pairs={{0,4},{4,8},{8,12},{12,16},{16,20},{20,24},{24,28},{1,5},{5,9},{9,... | collective-permute-start | bytes 36872 | tf_op jit(solution)/shard_map/ppermute | solution.py:46
  10.8 3.2 %collective-permute-start.3 = (bf16[544,384]{1,0:T(8,128)(2,1)S(1)}, bf16[544,384]{1,0:T(8,128)(2,1)S(1)}, u32[]{:S(2)}, u32[]{:S(2)}) collective-permute-start(bf16[544,384]{1,0:T(8,128)(2,1)S(1)} %pad_maximum_fusion.2.refs_0_.refs_4_), channel_id=1, source_target_pairs={{0,1},{1,2},{2,3},{4,5},{5,6},{6,7},{8,9},{9,10},{10,11},{12,13},{... | collective-permute-start | bytes 1253384 | tf_op jit(solution)/shard_map/ppermute | solution.py:67
  15.3 14.4 %collective-permute-done.1.refs_2_.refs_6_ = bf16[544,384]{1,0:T(8,128)(2,1)S(1)} collective-permute-done((bf16[544,384]{1,0:T(8,128)(2,1)S(1)}, bf16[544,384]{1,0:T(8,128)(2,1)S(1)}, u32[]{:S(2)}, u32[]{:S(2)}) %collective-permute-start.1) | collective-permute-done | bytes 417824 | tf_op jit(solution)/shard_map/ppermute | solution.py:55
  31.0 4.0 %collective-permute-done.4.refs_3_.refs_7_ = bf16[544,384]{1,0:T(8,128)(2,1)S(1)} collective-permute-done((bf16[544,384]{1,0:T(8,128)(2,1)S(1)}, bf16[544,384]{1,0:T(8,128)(2,1)S(1)}, u32[]{:S(2)}, u32[]{:S(2)}) %collective-permute-start.4) | collective-permute-done | bytes 417824 | tf_op jit(solution)/shard_map/ppermute | solution.py:68
  35.1 8.5 %collective-permute-done.2.passed_ref.refs_8_ = bf16[544,384]{1,0:T(8,128)(2,1)S(1)} collective-permute-done((bf16[544,384]{1,0:T(8,128)(2,1)S(1)}, bf16[544,384]{1,0:T(8,128)(2,1)S(1)}, u32[]{:S(2)}, u32[]{:S(2)}) %collective-permute-start.2) | collective-permute-done | bytes 417824 | tf_op jit(solution)/shard_map/ppermute | solution.py:69
  48.4 4.5 %all-to-all-start = ((bf16[4,512,384]{2,1,0:T(8,128)(2,1)}), bf16[4,512,384]{2,1,0:T(8,128)(2,1)}, u32[]{:S(2)}, u32[]{:S(2)}) async-start(bf16[4,512,384]{2,1,0:T(8,128)(2,1)} %copies.1), calls=%async_computation | async-start | bytes 3145728 | tf_op jit(solution)/shard_map/all_to_all | solution.py:74
  58.1 4.1 %conv.1 = (bf16[512,768]{1,0:T(8,128)(2,1)S(1)}, bf16[512,768]{1,0:T(8,128)(2,1)S(1)}, f32[512,768]{1,0:T(8,128)S(1)}, bf16[512,256]{1,0:T(8,128)(2,1)S(1)}, f32...) custom-call(bf16[544,768]{1,0:T(8,128)(2,1)S(1)} %convolution_convert_fusion.value_ref.value_raw_ref, ...), custom_call_target="tpu_custom_call" | custom-call | flops 157286400 | bytes 5523456 | tf_op jit(solution)/shard_map/conv/pallas_call | solution.py:942
  69.9 4.7 %collective-permute-done.6.refs_1_ = f32[72,768]{1,0:T(8,128)} collective-permute-done((f32[72,768]{1,0:T(8,128)}, f32[72,768]{1,0:T(8,128)}, u32[]{:S(2)}, u32[]{:S(2)}) %collective-permute-start.6) | collective-permute-done | bytes 221216 | tf_op jit(solution)/shard_map/ppermute | solution.py:78
  75.5 4.8 %collective-permute-done.8.refs_3_ = f32[72,768]{1,0:T(8,128)} collective-permute-done((f32[72,768]{1,0:T(8,128)}, f32[72,768]{1,0:T(8,128)}, u32[]{:S(2)}, u32[]{:S(2)}) %collective-permute-start.8) | collective-permute-done | bytes 221216 | tf_op jit(solution)/shard_map/ppermute | solution.py:78
  91.3 2.9 %mixed_grad.1 = (f32[512,768]{1,0:T(8,128)S(1)}, bf16[512,1536]{1,0:T(8,128)(2,1)S(1)}) custom-call(bf16[4,512,384]{2,1,0:T(8,128)(2,1)} %all-to-all-done.parts_ref, bf16[768,1536]{1,0:T(8,128)(2,1)S(1)} %copy-done.10), custom_call_target="tpu_custom_call" | custom-call | flops 1207959552 | bytes 7077888 | tf_op jit(solution)/shard_map/mixed_grad/pallas_call | solution.py:942
  103.4 3.8 %gate.1 = (bf16[512,768]{1,0:T(8,128)(2,1)S(1)}, bf16[512,768]{1,0:T(8,128)(2,1)S(1)}, f32[512,768]{1,0:T(8,128)S(1)}, f32[8,768]{1,0:T(8,128)S(1)}, f32[136,768]{1,0:T(8,128)S(1)}, /*index=5*/f32[8,512]{1,0:T(8,128)S(1)}) custom-call(f32[8,512]{1,0:T(8,128)S(1)} %get-tuple-element.87.refs_0_, f32[8,512]{1,0:T(8,128)S(1)} %collective-permute-done.10.refs_1_, ...), custom_call_target="tpu_custom_call" | custom-call | flops 235929600 | bytes 9487872 | tf_op jit(solution)/shard_map/gate/pallas_call | solution.py:942
  107.2 2.7 %collective-permute-start.13 = (f32[136,768]{1,0:T(8,128)S(1)}, f32[136,768]{1,0:T(8,128)S(1)}, u32[]{:S(2)}, u32[]{:S(2)}) collective-permute-start(f32[136,768]{1,0:T(8,128)S(1)} %get-tuple-element.89.loose_ref.own_ref), channel_id=1, source_target_pairs={{0,4},{4,0},{1,5},{5,1},{2,6},{6,2},{3,7},{7,3},{8,12},{12,8},{9,1... | collective-permute-start | bytes 1253384 | tf_op jit(solution)/shard_map/ppermute | solution.py:50
  109.9 2.9 %out.1.refs_0_ = bf16[4,512,384]{2,1,0:T(8,128)(2,1)} custom-call(f32[136,768]{1,0:T(8,128)S(1)} %get-tuple-element.89.loose_ref.own_ref, bf16[512,768]{1,0:T(8,128)(2,1)S(1)} %get-tuple-element.90.mixed_ref, bf16[768,1536]{1,0:T(8,128)(2,1)S(1)} %copy-done.11), custom_call_target="tpu_custom_call" | custom-call | flops 1207959552 | bytes 4718592 | tf_op jit(solution)/shard_map/out/pallas_call | solution.py:942
  114.8 6.6 %early.1 = (bf16[4,384,768]{2,1,0:T(8,128)(2,1)S(1)}, bf16[4,384,768]{2,1,0:T(8,128)(2,1)}, f32[1,1536]{1,0:T(1,128)S(1)}) custom-call(f32[72,768]{1,0:T(8,128)S(1)} %after_pair.1.loose_ref.refs_0_, s32[1]{0:T(128)} %bitcast.core_ref, bf16[544,1536]{1,0:T(8,128)(2,1)S(1)} %copy-done.21, bf16[512,768]{1,0:T(8,128)(2,1)S(1)} %get-tuple-element.91.gate_ref.gate_grad_ref, ...), custom_call_target="tpu_custom_call" | custom-call | flops 2415919104 | bytes 11900932 | tf_op jit(solution)/shard_map/early/pallas_call | solution.py:942
  123.4 4.4 %all-to-all-start.1 = ((bf16[4,512,384]{2,1,0:T(8,128)(2,1)}), bf16[4,512,384]{2,1,0:T(8,128)(2,1)}, u32[]{:S(2)}, u32[]{:S(2)}) async-start(bf16[4,512,384]{2,1,0:T(8,128)(2,1)} %out.1.refs_0_), calls=%async_computation.1 | async-start | bytes 3145728 | tf_op jit(solution)/shard_map/all_to_all | solution.py:74
  130.5 4.1 %collective-permute-done.15.refs_1_ = f32[72,768]{1,0:T(8,128)S(1)} collective-permute-done((f32[72,768]{1,0:T(8,128)}, f32[72,768]{1,0:T(8,128)S(1)}, u32[]{:S(2)}, u32[]{:S(2)}) %collective-permute-start.15) | collective-permute-done | bytes 221216 | tf_op jit(solution)/shard_map/ppermute | solution.py:78
  134.6 4.7 %collective-permute-done.17.refs_3_ = f32[72,768]{1,0:T(8,128)S(1)} collective-permute-done((f32[72,768]{1,0:T(8,128)}, f32[72,768]{1,0:T(8,128)S(1)}, u32[]{:S(2)}, u32[]{:S(2)}) %collective-permute-start.17) | collective-permute-done | bytes 221216 | tf_op jit(solution)/shard_map/ppermute | solution.py:78
  147.7 5.6 %back.1 = (f32[512,768]{1,0:T(8,128)S(1)}, f32[512,256]{1,0:T(8,128)S(1)}) custom-call(f32[2,192,768]{2,1,0:T(8,128)S(1)} %get-tuple-element.95.early_ref.first_ref, f32[128,768]{1,0:T(8,128)S(1)} %after_enter.1.state_in_ref, f32[512,768]{1,0:T(8,128)S(1)} %copy-done.31, f32[512,12]{1,0:T(8,128)S(1)} %get-tuple-element.85.e_ref.refs_9_, ...), custom_call_target="tpu_custom_call" | custom-call | flops 786432000 | bytes 8858624 | tf_op jit(solution)/shard_map/back/pallas_call | solution.py:942
  155.6 3.3 %collective-permute-done.21.after_ref = f32[8,1024]{1,0:T(8,128)S(1)} collective-permute-done((f32[8,1024]{1,0:T(8,128)S(1)}, f32[8,1024]{1,0:T(8,128)S(1)}, u32[]{:S(2)}, u32[]{:S(2)}) %collective-permute-start.21) | collective-permute-done | bytes 32800 | tf_op jit(solution)/shard_map/ppermute | solution.py:46
  158.9 3.7 %conv_back.1 = (bf16[512,768]{1,0:T(8,128)(2,1)S(1)}, bf16[512,256]{1,0:T(8,128)(2,1)S(1)}, f32[8,768]{1,0:T(8,128)S(1)}, f32[8,256]{1,0:T(8,128)S(1)}, f32[8,512]{1,0:T(8,128)S(1)}) custom-call(f32[512,768]{1,0:T(8,128)S(1)} %get-tuple-element.104.value_ref, f32[512,256]{1,0:T(8,128)S(1)} %get-tuple-element.105.map_ref, ...), custom_call_target="tpu_custom_call" | custom-call | flops 39321600 | bytes 4366336 | tf_op jit(solution)/shard_map/conv_back/pallas_call | solution.py:942
  164.9 5.4 %normed.1.loose_ref = bf16[4,528,384]{2,1,0:T(8,128)(2,1)} custom-call(f32[192,768]{1,0:T(8,128)S(1)} %get-tuple-element.108.late_ref.first_ref, bf16[512,768]{1,0:T(8,128)(2,1)S(1)} %copy-done.45, bf16[512,768]{1,0:T(8,128)(2,1)S(1)} %get-tuple-element.109.value_grad_ref.value_ref, bf16[512,256]{1,0:T(8,128)(2,1)S(1)} %get-tuple-element.110.state_grad_ref.state_ref, ...), custom_call_target="tpu_custom_call" | custom-call | flops 2415919104 | bytes 8978432 | tf_op jit(solution)/shard_map/normed/pallas_call | solution.py:942
  173.8 5.2 %late.1 = (bf16[4,272,768]{2,1,0:T(8,128)(2,1)S(1)}, bf16[4,272,768]{2,1,0:T(8,128)(2,1)}) custom-call(bf16[192,768]{1,0:T(8,128)(2,1)S(1)} %get-tuple-element.115.early_ref, s32[1]{0:T(128)} %bitcast.core_ref, bf16[544,1536]{1,0:T(8,128)(2,1)S(1)} %copy-done.21, bf16[512,768]{1,0:T(8,128)(2,1)S(1)} %get-tuple-element.109.value_grad_ref.value_ref, ...), custom_call_target="tpu_custom_call" | custom-call | flops 1811939328 | bytes 9320452 | tf_op jit(solution)/shard_map/late/pallas_call | solution.py:942
  180.6 4.5 %all-to-all-start.2 = ((bf16[4,528,384]{2,1,0:T(8,128)(2,1)}), bf16[4,528,384]{2,1,0:T(8,128)(2,1)S(1)}, u32[]{:S(2)}, u32[]{:S(2)}) async-start(bf16[4,528,384]{2,1,0:T(8,128)(2,1)} %normed.1.loose_ref), calls=%async_computation.2 | async-start | bytes 3244032 | tf_op jit(solution)/shard_map/all_to_all | solution.py:74
  185.6 2.7 late_half.1
  198.7 3.8 %collective-permute-done.25.refs_1_ = bf16[272,768]{1,0:T(8,128)(2,1)S(1)} collective-permute-done((bf16[272,768]{1,0:T(8,128)(2,1)}, bf16[272,768]{1,0:T(8,128)(2,1)S(1)}, u32[]{:S(2)}, u32[]{:S(2)}) %collective-permute-start.25) | collective-permute-done | bytes 417824 | tf_op jit(solution)/shard_map/ppermute | solution.py:78
  203.6 8.8 %collective-permute-done.27.refs_3_ = bf16[272,768]{1,0:T(8,128)(2,1)} collective-permute-done((bf16[272,768]{1,0:T(8,128)(2,1)}, bf16[272,768]{1,0:T(8,128)(2,1)}, u32[]{:S(2)}, u32[]{:S(2)}) %collective-permute-start.27) | collective-permute-done | bytes 417824 | tf_op jit(solution)/shard_map/ppermute | solution.py:78
  215.5 10.7 %collective-permute-done.28.arrived_ref = bf16[80,768]{1,0:T(8,128)(2,1)S(1)} collective-permute-done((bf16[80,768]{1,0:T(8,128)(2,1)S(1)}, bf16[80,768]{1,0:T(8,128)(2,1)S(1)}, u32[]{:S(2)}, u32[]{:S(2)}) %collective-permute-start.28) | collective-permute-done | bytes 122912 | tf_op jit(solution)/shard_map/ppermute | solution.py:89
  226.9 7.2 %collective-permute-done.29.arrived_ref = bf16[80,768]{1,0:T(8,128)(2,1)S(1)} collective-permute-done((bf16[80,768]{1,0:T(8,128)(2,1)S(1)}, bf16[80,768]{1,0:T(8,128)(2,1)S(1)}, u32[]{:S(2)}, u32[]{:S(2)}) %collective-permute-start.29) | collective-permute-done | bytes 122912 | tf_op jit(solution)/shard_map/ppermute | solution.py:89
  238.1 5.0 %collective-permute-done.47 = bf16[192,768]{1,0:T(8,128)(2,1)S(1)} collective-permute-done((bf16[192,768]{1,0:T(8,128)(2,1)S(1)}, bf16[192,768]{1,0:T(8,128)(2,1)S(1)}, u32[]{:S(2)}, u32[]{:S(2)}) %collective-permute-start.47) | collective-permute-done | bytes 294944 | tf_op jit(solution)/shard_map/ppermute | solution.py:78
  251.0 3.5 %collective-permute-done.32.refs_2_ = bf16[2,80,768]{2,1,0:T(8,128)(2,1)} collective-permute-done((bf16[2,80,768]{2,1,0:T(8,128)(2,1)S(1)}, bf16[2,80,768]{2,1,0:T(8,128)(2,1)}, u32[]{:S(2)}, u32[]{:S(2)}) %collective-permute-start.32) | collective-permute-done | bytes 245792 | tf_op jit(solution)/shard_map/ppermute | solution.py:78
  261.4 5.7 %early_out.1 = (f32[1536,768]{1,0:T(8,128)}, f32[768,1536]{1,0:T(8,128)}) custom-call(s32[1]{0:T(128)} %bitcast.core_ref, s32[1]{0:T(128)} %bitcast.5.chip_ref, bf16[2,192,768]{2,1,0:T(8,128)(2,1)S(1)} %copy-done.2, bf16[2,192,768]{2,1,0:T(8,128)(2,1)} %collective-permute-done.35.refs_1_, bf16[2,192,768]{2,1,0:T(8,128)(2,1)} %collective-permute-done.36.refs_2_, ...), custom_call_target="tpu_custom_call" | custom-call | flops 4718592 | bytes 14155784 | tf_op jit(solution)/shard_map/early_out/pallas_call | solution.py:942
  267.2 3.0 %shared_out.1 = (f32[1536,256]{1,0:T(8,128)}, f32[4,768]{1,0:T(4,128)}, f32[768]{0:T(1024)}, f32[4,256]{1,0:T(4,128)}, f32[256]{0:T(256)}, /*index=5*/f32[12]{0:T(128)}, f32[768]{0:T(1024)}, f32[384]{0:T(512)}) custom-call(s32[1]{0:T(128)} %bitcast.core_ref, s32[1]{0:T(128)} %bitcast.5.chip_ref, s32[1]{0:T(128)} %bitcast.1.head_ref, ...), custom_call_target="tpu_custom_call" | custom-call | flops 786432 | bytes 2581052 | tf_op jit(solution)/shard_map/shared_out/pallas_call | solution.py:942
  (319 shorter events, 105.6 us)
Async XLA Ops:
  8.4 21.3 %collective-permute-start.1 = (bf16[544,384]{1,0:T(8,128)(2,1)S(1)}, bf16[544,384]{1,0:T(8,128)(2,1)S(1)}, u32[]{:S(2)}, u32[]{:S(2)}) collective-permute-start(bf16[544,384]{1,0:T(8,128)(2,1)S(1)} %pad_maximum_fusion.2.refs_0_.refs_4_), channel_id=1, source_target_pairs={{0,2},{1,3},{2,0},{3,1},{4,6},{5,7},{6,4},{7,5},{8,10},{9,11},{10,... | collective-permute-start | bytes 1253384 | tf_op jit(solution)/shard_map/ppermute | solution.py:55
  10.8 20.3 %collective-permute-start.3 = (bf16[544,384]{1,0:T(8,128)(2,1)S(1)}, bf16[544,384]{1,0:T(8,128)(2,1)S(1)}, u32[]{:S(2)}, u32[]{:S(2)}) collective-permute-start(bf16[544,384]{1,0:T(8,128)(2,1)S(1)} %pad_maximum_fusion.2.refs_0_.refs_4_), channel_id=1, source_target_pairs={{0,1},{1,2},{2,3},{4,5},{5,6},{6,7},{8,9},{9,10},{10,11},{12,13},{... | collective-permute-start | bytes 1253384 | tf_op jit(solution)/shard_map/ppermute | solution.py:67
  14.0 21.1 %collective-permute-start.4 = (bf16[544,384]{1,0:T(8,128)(2,1)S(1)}, bf16[544,384]{1,0:T(8,128)(2,1)S(1)}, u32[]{:S(2)}, u32[]{:S(2)}) collective-permute-start(bf16[544,384]{1,0:T(8,128)(2,1)S(1)} %pad_maximum_fusion.2.refs_0_.refs_4_), channel_id=1, source_target_pairs={{1,0},{2,1},{3,2},{5,4},{6,5},{7,6},{9,8},{10,9},{11,10},{13,12},{... | collective-permute-start | bytes 1253384 | tf_op jit(solution)/shard_map/ppermute | solution.py:68
  29.7 13.8 %collective-permute-start.2 = (bf16[544,384]{1,0:T(8,128)(2,1)S(1)}, bf16[544,384]{1,0:T(8,128)(2,1)S(1)}, u32[]{:S(2)}, u32[]{:S(2)}) collective-permute-start(bf16[544,384]{1,0:T(8,128)(2,1)S(1)} %collective-permute-done.1.refs_2_.refs_6_), channel_id=1, source_target_pairs={{2,3},{1,0},{6,7},{5,4},{10,11},{9,8},{14,15},{13,12},{18,19},{17,... | collective-permute-start | bytes 1253384 | tf_op jit(solution)/shard_map/ppermute | solution.py:69
  48.4 41.3 %all-to-all-start = ((bf16[4,512,384]{2,1,0:T(8,128)(2,1)}), bf16[4,512,384]{2,1,0:T(8,128)(2,1)}, u32[]{:S(2)}, u32[]{:S(2)}) async-start(bf16[4,512,384]{2,1,0:T(8,128)(2,1)} %copies.1), calls=%async_computation | async-start | bytes 3145728 | tf_op jit(solution)/shard_map/all_to_all | solution.py:74
  68.8 11.5 %collective-permute-start.8 = (f32[72,768]{1,0:T(8,128)}, f32[72,768]{1,0:T(8,128)}, u32[]{:S(2)}, u32[]{:S(2)}) collective-permute-start(f32[72,768]{1,0:T(8,128)} %before_pair.1.refs_0_), channel_id=1, source_target_pairs={{0,24},{8,16},{16,8},{24,0},{1,25},{9,17},{17,9},{25,1},{2,26},{10... | collective-permute-start | bytes 663560 | tf_op jit(solution)/shard_map/ppermute | solution.py:78
  123.3 17.0 %collective-permute-start.14 = (bf16[4,384,768]{2,1,0:T(8,128)(2,1)}, bf16[4,384,768]{2,1,0:T(8,128)(2,1)}, u32[]{:S(2)}, u32[]{:S(2)}) collective-permute-start(bf16[4,384,768]{2,1,0:T(8,128)(2,1)} %get-tuple-element.94.refs_4_), channel_id=1, source_target_pairs={{0,4},{4,0},{1,5},{5,1},{2,6},{6,2},{3,7},{7,3},{8,12},{12,8},{9,1... | collective-permute-start | bytes 7077896 | tf_op jit(solution)/shard_map/ppermute | solution.py:50
  123.4 57.2 %all-to-all-start.1 = ((bf16[4,512,384]{2,1,0:T(8,128)(2,1)}), bf16[4,512,384]{2,1,0:T(8,128)(2,1)}, u32[]{:S(2)}, u32[]{:S(2)}) async-start(bf16[4,512,384]{2,1,0:T(8,128)(2,1)} %out.1.refs_0_), calls=%async_computation.1 | async-start | bytes 3145728 | tf_op jit(solution)/shard_map/all_to_all | solution.py:74
  128.6 10.7 %collective-permute-start.17 = (f32[72,768]{1,0:T(8,128)}, f32[72,768]{1,0:T(8,128)S(1)}, u32[]{:S(2)}, u32[]{:S(2)}) collective-permute-start(f32[72,768]{1,0:T(8,128)} %copy-done.40), channel_id=1, source_target_pairs={{0,24},{8,16},{16,8},{24,0},{1,25},{9,17},{17,9},{25,1},{2,26},{10... | collective-permute-start | bytes 663560 | tf_op jit(solution)/shard_map/ppermute | solution.py:78
  142.7 19.9 %collective-permute-start.18 = (bf16[2,192,768]{2,1,0:T(8,128)(2,1)S(1)}, bf16[2,192,768]{2,1,0:T(8,128)(2,1)S(1)}, u32[]{:S(2)}, u32[]{:S(2)}) collective-permute-start(bf16[2,192,768]{2,1,0:T(8,128)(2,1)S(1)} %get-tuple-element.96), channel_id=1, source_target_pairs={{0,8},{8,0},{16,24},{24,16},{1,9},{9,1},{17,25},{25,17},{2,10},{10... | collective-permute-start | bytes 1769480 | tf_op jit(solution)/shard_map/ppermute | solution.py:78
  143.3 19.3 %collective-permute-start.19 = (bf16[2,192,768]{2,1,0:T(8,128)(2,1)S(1)}, bf16[2,192,768]{2,1,0:T(8,128)(2,1)S(1)}, u32[]{:S(2)}, u32[]{:S(2)}) collective-permute-start(bf16[2,192,768]{2,1,0:T(8,128)(2,1)S(1)} %get-tuple-element.98), channel_id=1, source_target_pairs={{0,16},{8,24},{16,0},{24,8},{1,17},{9,25},{17,1},{25,9},{2,18},{10... | collective-permute-start | bytes 1769480 | tf_op jit(solution)/shard_map/ppermute | solution.py:78
  180.6 76.0 %all-to-all-start.2 = ((bf16[4,528,384]{2,1,0:T(8,128)(2,1)}), bf16[4,528,384]{2,1,0:T(8,128)(2,1)S(1)}, u32[]{:S(2)}, u32[]{:S(2)}) async-start(bf16[4,528,384]{2,1,0:T(8,128)(2,1)} %normed.1.loose_ref), calls=%async_computation.2 | async-start | bytes 3244032 | tf_op jit(solution)/shard_map/all_to_all | solution.py:74
  185.1 11.4 %collective-permute-start.38 = (bf16[192,768]{1,0:T(8,128)(2,1)}, bf16[192,768]{1,0:T(8,128)(2,1)}, u32[]{:S(2)}, u32[]{:S(2)}) collective-permute-start(bf16[192,768]{1,0:T(8,128)(2,1)} %copy-done.54), channel_id=1, source_target_pairs={{0,8},{8,0},{16,24},{24,16},{1,9},{9,1},{17,25},{25,17},{2,10},{10... | collective-permute-start | bytes 884744 | tf_op jit(solution)/shard_map/ppermute | solution.py:78
  189.2 13.4 %collective-permute-start.25 = (bf16[272,768]{1,0:T(8,128)(2,1)}, bf16[272,768]{1,0:T(8,128)(2,1)S(1)}, u32[]{:S(2)}, u32[]{:S(2)}) collective-permute-start(bf16[272,768]{1,0:T(8,128)(2,1)} %get-tuple-element.124), channel_id=1, source_target_pairs={{0,8},{8,0},{16,24},{24,16},{1,9},{9,1},{17,25},{25,17},{2,10},{10... | collective-permute-start | bytes 1253384 | tf_op jit(solution)/shard_map/ppermute | solution.py:78
  190.1 13.4 %collective-permute-start.26 = (bf16[272,768]{1,0:T(8,128)(2,1)}, bf16[272,768]{1,0:T(8,128)(2,1)}, u32[]{:S(2)}, u32[]{:S(2)}) collective-permute-start(bf16[272,768]{1,0:T(8,128)(2,1)} %get-tuple-element.125), channel_id=1, source_target_pairs={{0,16},{8,24},{16,0},{24,8},{1,17},{9,25},{17,1},{25,9},{2,18},{10... | collective-permute-start | bytes 1253384 | tf_op jit(solution)/shard_map/ppermute | solution.py:78
  191.6 20.8 %collective-permute-start.27 = (bf16[272,768]{1,0:T(8,128)(2,1)}, bf16[272,768]{1,0:T(8,128)(2,1)}, u32[]{:S(2)}, u32[]{:S(2)}) collective-permute-start(bf16[272,768]{1,0:T(8,128)(2,1)} %get-tuple-element.126), channel_id=1, source_target_pairs={{0,24},{8,16},{16,8},{24,0},{1,25},{9,17},{17,9},{25,1},{2,26},{10... | collective-permute-start | bytes 1253384 | tf_op jit(solution)/shard_map/ppermute | solution.py:78
  194.4 31.8 %collective-permute-start.35 = (bf16[2,192,768]{2,1,0:T(8,128)(2,1)}, bf16[2,192,768]{2,1,0:T(8,128)(2,1)}, u32[]{:S(2)}, u32[]{:S(2)}) collective-permute-start(bf16[2,192,768]{2,1,0:T(8,128)(2,1)} %tie.2.refs_0_), channel_id=1, source_target_pairs={{0,4},{4,0},{1,5},{5,1},{2,6},{6,2},{3,7},{7,3},{8,12},{12,8},{9,1... | collective-permute-start | bytes 1769480 | tf_op jit(solution)/shard_map/ppermute | solution.py:50
  196.5 29.9 %collective-permute-start.36 = (bf16[2,192,768]{2,1,0:T(8,128)(2,1)}, bf16[2,192,768]{2,1,0:T(8,128)(2,1)}, u32[]{:S(2)}, u32[]{:S(2)}) collective-permute-start(bf16[2,192,768]{2,1,0:T(8,128)(2,1)} %tie.2.refs_0_), channel_id=1, source_target_pairs={{0,8},{8,0},{16,24},{24,16},{1,9},{9,1},{17,25},{25,17},{2,10},{10... | collective-permute-start | bytes 1769480 | tf_op jit(solution)/shard_map/ppermute | solution.py:78
  202.5 34.8 %collective-permute-start.40 = (bf16[2,192,768]{2,1,0:T(8,128)(2,1)}, bf16[2,192,768]{2,1,0:T(8,128)(2,1)}, u32[]{:S(2)}, u32[]{:S(2)}) collective-permute-start(bf16[2,192,768]{2,1,0:T(8,128)(2,1)} %tie.3.refs_4_), channel_id=1, source_target_pairs={{0,16},{8,24},{16,0},{24,8},{1,17},{9,25},{17,1},{25,9},{2,18},{10... | collective-permute-start | bytes 1769480 | tf_op jit(solution)/shard_map/ppermute | solution.py:78
  213.8 12.5 %collective-permute-start.28 = (bf16[80,768]{1,0:T(8,128)(2,1)S(1)}, bf16[80,768]{1,0:T(8,128)(2,1)S(1)}, u32[]{:S(2)}, u32[]{:S(2)}) collective-permute-start(bf16[80,768]{1,0:T(8,128)(2,1)S(1)} %convert_element_type.29), channel_id=1, source_target_pairs={{0,1},{1,0},{2,3},{3,2},{4,5},{5,4},{6,7},{7,6},{8,9},{9,8},{10,11... | collective-permute-start | bytes 368648 | tf_op jit(solution)/shard_map/ppermute | solution.py:89
  215.0 20.8 %collective-permute-start.43 = (bf16[192,768]{1,0:T(8,128)(2,1)S(1)}, bf16[192,768]{1,0:T(8,128)(2,1)S(1)}, u32[]{:S(2)}, u32[]{:S(2)}) collective-permute-start(bf16[192,768]{1,0:T(8,128)(2,1)S(1)} %get-tuple-element.134), channel_id=1, source_target_pairs={{0,8},{8,0},{16,24},{24,16},{1,9},{9,1},{17,25},{25,17},{2,10},{10... | collective-permute-start | bytes 884744 | tf_op jit(solution)/shard_map/ppermute | solution.py:78
  226.2 10.3 %collective-permute-start.45 = (bf16[192,768]{1,0:T(8,128)(2,1)S(1)}, bf16[192,768]{1,0:T(8,128)(2,1)S(1)}, u32[]{:S(2)}, u32[]{:S(2)}) collective-permute-start(bf16[192,768]{1,0:T(8,128)(2,1)S(1)} %get-tuple-element.134), channel_id=1, source_target_pairs={{0,16},{8,24},{16,0},{24,8},{1,17},{9,25},{17,1},{25,9},{2,18},{10... | collective-permute-start | bytes 884744 | tf_op jit(solution)/shard_map/ppermute | solution.py:78
  226.4 11.0 %collective-permute-start.42 = (bf16[1,192,768]{2,1,0:T(8,128)(2,1)S(1)}, bf16[1,192,768]{2,1,0:T(8,128)(2,1)S(1)}, u32[]{:S(2)}, u32[]{:S(2)}) collective-permute-start(bf16[1,192,768]{2,1,0:T(8,128)(2,1)S(1)} %bitcast.36), channel_id=1, source_target_pairs={{0,4},{4,0},{1,5},{5,1},{2,6},{6,2},{3,7},{7,3},{8,12},{12,8},{9,1... | collective-permute-start | bytes 884744 | tf_op jit(solution)/shard_map/ppermute | solution.py:50
  234.1 9.0 %collective-permute-start.47 = (bf16[192,768]{1,0:T(8,128)(2,1)S(1)}, bf16[192,768]{1,0:T(8,128)(2,1)S(1)}, u32[]{:S(2)}, u32[]{:S(2)}) collective-permute-start(bf16[192,768]{1,0:T(8,128)(2,1)S(1)} %get-tuple-element.134), channel_id=1, source_target_pairs={{0,24},{8,16},{16,8},{24,0},{1,25},{9,17},{17,9},{25,1},{2,26},{10... | collective-permute-start | bytes 884744 | tf_op jit(solution)/shard_map/ppermute | solution.py:78
  235.8 11.3 %collective-permute-start.44 = (bf16[1,192,768]{2,1,0:T(8,128)(2,1)S(1)}, bf16[1,192,768]{2,1,0:T(8,128)(2,1)S(1)}, u32[]{:S(2)}, u32[]{:S(2)}) collective-permute-start(bf16[1,192,768]{2,1,0:T(8,128)(2,1)S(1)} %bitcast.38), channel_id=1, source_target_pairs={{0,4},{4,0},{1,5},{5,1},{2,6},{6,2},{3,7},{7,3},{8,12},{12,8},{9,1... | collective-permute-start | bytes 884744 | tf_op jit(solution)/shard_map/ppermute | solution.py:50
  236.5 10.6 %collective-permute-start.46 = (bf16[1,192,768]{2,1,0:T(8,128)(2,1)S(1)}, bf16[1,192,768]{2,1,0:T(8,128)(2,1)S(1)}, u32[]{:S(2)}, u32[]{:S(2)}) collective-permute-start(bf16[1,192,768]{2,1,0:T(8,128)(2,1)S(1)} %bitcast.40), channel_id=1, source_target_pairs={{0,4},{4,0},{1,5},{5,1},{2,6},{6,2},{3,7},{7,3},{8,12},{12,8},{9,1... | collective-permute-start | bytes 884744 | tf_op jit(solution)/shard_map/ppermute | solution.py:50
  237.4 9.2 %collective-permute-start.30 = (bf16[80,768]{1,0:T(8,128)(2,1)S(1)}, bf16[80,768]{1,0:T(8,128)(2,1)S(1)}, u32[]{:S(2)}, u32[]{:S(2)}) collective-permute-start(bf16[80,768]{1,0:T(8,128)(2,1)S(1)} %get-tuple-element.130), channel_id=1, source_target_pairs={{0,16},{8,24},{16,0},{24,8},{1,17},{9,25},{17,1},{25,9},{2,18},{10... | collective-permute-start | bytes 368648 | tf_op jit(solution)/shard_map/ppermute | solution.py:78
  237.4 24.0 %collective-permute-start.39 = (bf16[2,192,768]{2,1,0:T(8,128)(2,1)S(1)}, bf16[2,192,768]{2,1,0:T(8,128)(2,1)}, u32[]{:S(2)}, u32[]{:S(2)}) collective-permute-start(bf16[2,192,768]{2,1,0:T(8,128)(2,1)S(1)} %copy-done.3), channel_id=1, source_target_pairs={{0,4},{4,0},{1,5},{5,1},{2,6},{6,2},{3,7},{7,3},{8,12},{12,8},{9,1... | collective-permute-start | bytes 1769480 | tf_op jit(solution)/shard_map/ppermute | solution.py:50
  243.1 18.3 %collective-permute-start.37 = (bf16[2,192,768]{2,1,0:T(8,128)(2,1)}, bf16[2,192,768]{2,1,0:T(8,128)(2,1)}, u32[]{:S(2)}, u32[]{:S(2)}) collective-permute-start(bf16[2,192,768]{2,1,0:T(8,128)(2,1)} %collective-permute-done.36.refs_2_), channel_id=1, source_target_pairs={{0,4},{4,0},{1,5},{5,1},{2,6},{6,2},{3,7},{7,3},{8,12},{12,8},{9,1... | collective-permute-start | bytes 1769480 | tf_op jit(solution)/shard_map/ppermute | solution.py:50
  246.6 14.9 %collective-permute-start.41 = (bf16[2,192,768]{2,1,0:T(8,128)(2,1)}, bf16[2,192,768]{2,1,0:T(8,128)(2,1)}, u32[]{:S(2)}, u32[]{:S(2)}) collective-permute-start(bf16[2,192,768]{2,1,0:T(8,128)(2,1)} %collective-permute-done.40.refs_6_), channel_id=1, source_target_pairs={{0,4},{4,0},{1,5},{5,1},{2,6},{6,2},{3,7},{7,3},{8,12},{12,8},{9,1... | collective-permute-start | bytes 1769480 | tf_op jit(solution)/shard_map/ppermute | solution.py:50
  250.2 16.9 %collective-permute-start.31 = (bf16[2,80,768]{2,1,0:T(8,128)(2,1)S(1)}, bf16[2,80,768]{2,1,0:T(8,128)(2,1)}, u32[]{:S(2)}, u32[]{:S(2)}) collective-permute-start(bf16[2,80,768]{2,1,0:T(8,128)(2,1)S(1)} %pad_maximum_fusion.3.refs_0_), channel_id=1, source_target_pairs={{0,4},{4,0},{1,5},{5,1},{2,6},{6,2},{3,7},{7,3},{8,12},{12,8},{9,1... | collective-permute-start | bytes 737288 | tf_op jit(solution)/shard_map/ppermute | solution.py:50
  254.4 12.8 %collective-permute-start.33 = (bf16[2,80,768]{2,1,0:T(8,128)(2,1)}, bf16[2,80,768]{2,1,0:T(8,128)(2,1)}, u32[]{:S(2)}, u32[]{:S(2)}) collective-permute-start(bf16[2,80,768]{2,1,0:T(8,128)(2,1)} %collective-permute-done.32.refs_2_), channel_id=1, source_target_pairs={{0,4},{4,0},{1,5},{5,1},{2,6},{6,2},{3,7},{7,3},{8,12},{12,8},{9,1... | collective-permute-start | bytes 737288 | tf_op jit(solution)/shard_map/ppermute | solution.py:50
  (116 other events, 766.7 us)
